TPU v7x, 32 devices: a whole 2x2x4 slice. The times are simulated.
32 devices in a mesh: dp: 8 (over z, x), tensor: 4 (over y, core).
Axes of the slice: x: 2, y: 2, z: 4, core: 2. Of those that a mesh axis runs over, the one named last changes fastest.
Arguments:
- inputs: bfloat16 [8, 1024, 1024], P('dp', 'tensor'), may hold values from -6 to 6
- cotangent: bfloat16 [8, 1024, 1024], P('dp', 'tensor'), may hold values from -6 to 6
- segment_ids: int32 [8, 1024], P('dp'), may hold values from 0 to 256, as said below
- norm_gains: bfloat16 [2, 2, 1024], P(None, None, ('dp', 'tensor')), may hold values from 0.5 to 1.5
- w_query: bfloat16 [2, 1024, 512], P(None, 'dp', 'tensor'), may hold values from -0.1875 to 0.1875
- key_value_weight: bfloat16 [2, 1024, 256], P(None, ('dp', 'tensor')), may hold values from -0.1875 to 0.1875
- w_gate_in: bfloat16 [2, 1024, 2, 1536], P(None, 'dp', None, 'tensor'), may hold values from -0.1875 to 0.1875
- w_state_in: bfloat16 [2, 1024, 256], P(None, ('dp', 'tensor')), may hold values from -0.1875 to 0.1875
- w_step: bfloat16 [2, 1024, 24], P(None, 'dp', 'tensor'), may hold values from -0.1875 to 0.1875
- ssm_channel: float32 [2, 6, 1536], P(None, None, 'tensor'), as said below
- conv_state: bfloat16 [2, 1280], P(None, ('dp', 'tensor')), as said below
- head_params: float32 [2, 3, 24], P(None, None, 'tensor'), as said below
- w_attn_out: bfloat16 [2, 512, 1024], P(None, 'tensor', 'dp'), may hold values from -0.75 to 0.75
- w_ssm_out: bfloat16 [2, 1536, 1024], P(None, 'tensor', 'dp'), may hold values from -0.15625 to 0.15625
- w_gate_up: bfloat16 [2, 1024, 2, 2048], P(None, 'dp', None, 'tensor'), may hold values from -0.1875 to 0.1875
- w_down: bfloat16 [2, 2048, 1024], P(None, 'tensor', 'dp'), may hold values from -0.125 to 0.125
Outputs:
- output: bfloat16 [8, 1024, 1024], P('dp', 'tensor')
- input_grad: float32 [8, 1024, 1024], P('dp', 'tensor')
- grad_gains: float32 [2, 2, 1024], P(None, None, ('dp', 'tensor'))
- grad_query: float32 [2, 1024, 512], P(None, 'dp', 'tensor')
- grad_keyval: float32 [2, 1024, 256], P(None, ('dp', 'tensor'))
- grad_gate_in: float32 [2, 1024, 2, 1536], P(None, 'dp', None, 'tensor')
- grad_state_in: float32 [2, 1024, 256], P(None, ('dp', 'tensor'))
- grad_step: float32 [2, 1024, 24], P(None, 'dp', 'tensor')
- grad_channel: float32 [2, 6, 1536], P(None, None, 'tensor')
- grad_conv_state: float32 [2, 1280], P(None, ('dp', 'tensor'))
- grad_head_params: float32 [2, 3, 24], P(None, None, 'tensor')
- grad_attn_out: float32 [2, 512, 1024], P(None, 'tensor', 'dp')
- grad_ssm_out: float32 [2, 1536, 1024], P(None, 'tensor', 'dp')
- grad_gate_up: float32 [2, 1024, 2, 2048], P(None, 'dp', None, 'tensor')
- grad_down: float32 [2, 2048, 1024], P(None, 'tensor', 'dp')
Inputs may be any that keep to these rules, and one draw needn't show every extreme that they name: `segment_ids`: in each row the ids start at 0 and rise by at most one from a position to the next; each row holds one document of exactly 768 positions that starts after position 0 and within the row's first quarter; outside it a new document may start at any position, and in one row it starts at every one. `ssm_channel`: rows 0 to 3 are taps, row 4 a bias, the last row a gain. `conv_state`: entries 0 to 1023 are taps, the rest a bias. `head_params`: row 0 holds log decay rates, row 1 step biases, row 2 skip weights.
All inputs are finite; a program needn't handle non-finite values.
Results may differ from a plain program's by a relative error of at most 0.033.
Values may be sent and summed in bfloat16 or wider, within the bound.
No kernel may reach another device: no remote copies, remote signals or barrier semaphores. Data moves between devices by JAX's collectives and lax.ppermute only.
A program may use at most 256 MiB of HBM per device.

v0:
```python
import jax
import jax.numpy as jnp
from jax import lax
from jax.sharding import PartitionSpec as P

MODEL_DIM = 1024
HQ = 8
HEAD_SIZE = 64
HS = 24
PH = 64
NS = 128
LAYER_COUNT = 2


EPSILON = 1e-05
ROPE_BASE = 100000000000.0
HIGHEST_PRECISION = lax.Precision.HIGHEST


def dot_low(left, right):
    return jnp.dot(left, right, preferred_element_type=jnp.float32)


def dot_trans(left, right):
    return lax.dot_general(
        left, right, (((0,), (0,)), ((), ())), preferred_element_type=jnp.float32
    )


def dot_back(left, right):
    return lax.dot_general(
        left, right, (((1,), (1,)), ((), ())), preferred_element_type=jnp.float32
    )


def norm_rows(values, scale_gain):
    factor = lax.rsqrt(jnp.mean(values * values, axis=-1, keepdims=True) + EPSILON)
    return values * factor * scale_gain


def positions_of(segment_row):
    position_ids = jnp.arange(segment_row.shape[0], dtype=jnp.int32)
    earlier = jnp.concatenate([segment_row[:1] - 1, segment_row[:-1]])
    first_pos = jnp.where(segment_row != earlier, position_ids, 0)
    return position_ids - lax.cummax(first_pos, axis=0)


def rotate_pairs(values, places, sign_value):
    half_width = values.shape[-1] // 2
    frequency = ROPE_BASE ** (-jnp.arange(half_width, dtype=jnp.float32) / half_width)
    angles = sign_value * places.astype(jnp.float32)[:, None] * frequency[None, :]
    cosine = jnp.cos(angles)[:, None, :]
    sine_of = jnp.sin(angles)[:, None, :]
    first_half = values[..., :half_width]
    second_half = values[..., half_width:]
    return jnp.concatenate(
        [first_half * cosine - second_half * sine_of, second_half * cosine + first_half * sine_of],
        axis=-1,
    )


def convolve(values, conv_taps, conv_bias, segment_row):
    sequence_length = values.shape[0]
    tap_count = conv_taps.shape[0]
    summed = jnp.zeros_like(values) + conv_bias[None, :]
    for shift_by in range(tap_count):
        shifted = jnp.pad(values, ((shift_by, 0), (0, 0)))[:sequence_length]
        segment_shift = jnp.pad(segment_row, (shift_by, 0), constant_values=-1)[:sequence_length]
        same_doc = (segment_shift == segment_row)[:, None]
        summed = (
            summed
            + jnp.where(same_doc, shifted, 0.0) * conv_taps[tap_count - 1 - shift_by][None, :]
        )
    return summed


def state_space(inputs, b_matrix, c_matrix, step, rate, segment_row):
    sequence_length, head_count, head_width = inputs.shape
    state_size = b_matrix.shape[1]
    block_len = min(128, sequence_length)
    block_count = sequence_length // block_len
    log_step = step * rate[None, :]
    pieces = (
        inputs.reshape(block_count, block_len, head_count, head_width),
        b_matrix.reshape(block_count, block_len, state_size),
        c_matrix.reshape(block_count, block_len, state_size),
        step.reshape(block_count, block_len, head_count),
        log_step.reshape(block_count, block_len, head_count),
        segment_row.reshape(block_count, block_len),
        jnp.concatenate(
            [jnp.full((1,), -1, jnp.int32), segment_row.reshape(block_count, block_len)[:-1, -1]]
        ),
    )

    def one_block(memory, piece):
        piece_in, piece_b, piece_c, piece_step, piece_log, piece_seg, before = piece
        cumulative = jnp.cumsum(piece_log, axis=0)
        inner_prod = jnp.dot(piece_c, piece_b.T, precision=HIGHEST_PRECISION)
        log_gap = cumulative[:, None, :] - cumulative[None, :, :]
        position_ids = jnp.arange(block_len)
        allowed = (position_ids[None, :] <= position_ids[:, None]) & (
            piece_seg[None, :] == piece_seg[:, None]
        )
        weights = (
            jnp.where(allowed[:, :, None], jnp.exp(jnp.minimum(log_gap, 0.0)), 0.0)
            * inner_prod[:, :, None]
            * piece_step[None, :, :]
        )
        intra_out = jnp.einsum("tsh,shp->thp", weights, piece_in, precision=HIGHEST_PRECISION)
        carried = jnp.where((piece_seg == before)[:, None], jnp.exp(cumulative), 0.0)
        inter_out = (
            jnp.einsum("tn,hnp->thp", piece_c, memory, precision=HIGHEST_PRECISION)
            * carried[:, :, None]
        )
        tail_log = cumulative[-1]
        tail_keep = (
            jnp.where(
                (piece_seg == piece_seg[-1])[:, None],
                jnp.exp(jnp.minimum(tail_log[None, :] - cumulative, 0.0)),
                0.0,
            )
            * piece_step
        )
        fresh_state = jnp.einsum(
            "sn,sh,shp->hnp", piece_b, tail_keep, piece_in, precision=HIGHEST_PRECISION
        )
        kept_state = (
            jnp.where(piece_seg[-1] == before, 1.0, 0.0) * jnp.exp(tail_log)[:, None, None] * memory
        )
        return (kept_state + fresh_state, intra_out + inter_out)

    start_state = jnp.zeros((head_count, state_size, head_width), jnp.float32)
    final_state, outputs = lax.scan(jax.checkpoint(one_block), start_state, pieces)
    return outputs.reshape(sequence_length, head_count, head_width)


def ssm_core(x_in, bc_in, step_raw, gate_z, conv_chan, conv_flat, head_par, segment_row):
    sequence_length = x_in.shape[0]
    head_count = step_raw.shape[-1]
    head_width = x_in.shape[-1] // head_count
    state_size = bc_in.shape[-1] // 2
    taps_state = conv_flat.reshape(-1, 2 * state_size)
    conv_x = jax.nn.silu(convolve(x_in, conv_chan[:-1], conv_chan[-1], segment_row))
    conv_bc = jax.nn.silu(convolve(bc_in, taps_state[:-1], taps_state[-1], segment_row))
    step = jax.nn.softplus(step_raw + head_par[1][None, :])
    rate = -jnp.exp(head_par[0])
    heads_in = conv_x.reshape(sequence_length, head_count, head_width)
    result = state_space(
        heads_in, conv_bc[:, :state_size], conv_bc[:, state_size:], step, rate, segment_row
    )
    result = result + head_par[2][None, :, None] * heads_in
    return result.reshape(sequence_length, head_count * head_width) * jax.nn.silu(gate_z)


def block_probs(query_rows, key_rot, segment_row, block_start, block_len, score_scale):
    sequence_length = key_rot.shape[0]
    raw_scores = (
        jnp.einsum("qhd,kd->hqk", query_rows, key_rot, preferred_element_type=jnp.float32)
        * score_scale
    )
    row_index = block_start + jnp.arange(block_len, dtype=jnp.int32)
    row_segment = lax.dynamic_slice_in_dim(segment_row, block_start, block_len, 0)
    key_index = jnp.arange(sequence_length, dtype=jnp.int32)
    allowed = (key_index[None, :] <= row_index[:, None]) & (
        segment_row[None, :] == row_segment[:, None]
    )
    return jax.nn.softmax(jnp.where(allowed[None], raw_scores, -1e30), axis=-1)


def attend_rows(query_rot, key_rot, value_low, segment_row):
    sequence_length = query_rot.shape[0]
    block_len = min(512, sequence_length)
    score_scale = query_rot.shape[2] ** (-0.5)

    def one_block(block_start):
        query_rows = lax.dynamic_slice_in_dim(query_rot, block_start, block_len, 0)
        probs = block_probs(query_rows, key_rot, segment_row, block_start, block_len, score_scale)
        return jnp.einsum(
            "hqk,kd->qhd", probs.astype(jnp.bfloat16), value_low, preferred_element_type=jnp.float32
        )

    starts = jnp.arange(sequence_length // block_len) * block_len
    return lax.map(one_block, starts).reshape(
        sequence_length, query_rot.shape[1], query_rot.shape[2]
    )


def attend_back(query_rot, key_rot, value_low, segment_row, grad_out):
    sequence_length = query_rot.shape[0]
    block_len = min(512, sequence_length)
    score_scale = query_rot.shape[2] ** (-0.5)

    def one_block(carry, block_start):
        grad_key, grad_value = carry
        query_rows = lax.dynamic_slice_in_dim(query_rot, block_start, block_len, 0)
        grad_rows = lax.dynamic_slice_in_dim(grad_out, block_start, block_len, 0)
        probs = block_probs(query_rows, key_rot, segment_row, block_start, block_len, score_scale)
        grad_value = grad_value + jnp.einsum(
            "hqk,qhd->kd", probs.astype(jnp.bfloat16), grad_rows, preferred_element_type=jnp.float32
        )
        grad_probs = jnp.einsum(
            "qhd,kd->hqk", grad_rows, value_low, preferred_element_type=jnp.float32
        )
        grad_scores = (
            probs * (grad_probs - jnp.sum(probs * grad_probs, axis=-1, keepdims=True))
        ).astype(jnp.bfloat16)
        grad_query_rows = (
            jnp.einsum("hqk,kd->qhd", grad_scores, key_rot, preferred_element_type=jnp.float32)
            * score_scale
        )
        grad_key = (
            grad_key
            + jnp.einsum("hqk,qhd->kd", grad_scores, query_rows, preferred_element_type=jnp.float32)
            * score_scale
        )
        return ((grad_key, grad_value), grad_query_rows)

    starts = jnp.arange(sequence_length // block_len) * block_len
    empty = jnp.zeros(key_rot.shape, jnp.float32)
    (grad_key, grad_value), grad_query = lax.scan(one_block, (empty, empty), starts)
    return (grad_query.reshape(query_rot.shape), grad_key, grad_value)


def body(
    inputs,
    cotangent,
    segment_ids,
    norm_gains,
    w_query,
    key_value_weight,
    w_gate_in,
    w_state_in,
    w_step,
    ssm_channel,
    conv_state,
    head_params,
    w_attn_out,
    w_ssm_out,
    w_gate_up,
    w_down,
):
    rows_dev, quarter, model_width = inputs.shape
    sequence_length = segment_ids.shape[1]
    tokens = rows_dev * sequence_length
    tensor_rank = lax.axis_index("tensor")
    heads_local = w_query.shape[2] // HEAD_SIZE
    kv_heads = key_value_weight.shape[2] // (2 * HEAD_SIZE)
    group_size = HQ // kv_heads
    own_head = tensor_rank * heads_local // group_size
    ssm_heads = w_step.shape[2]
    channels = ssm_heads * PH
    ffn_local = w_gate_up.shape[3]
    places = jax.vmap(positions_of)(segment_ids)

    def gather_rows(values):
        return lax.all_gather(values, "tensor", axis=1, tiled=True)

    def sum_rows(values):
        return lax.psum_scatter(
            values.astype(jnp.bfloat16), "tensor", scatter_dimension=1, tiled=True
        ).astype(jnp.float32)

    def gather_grads(values):
        return lax.all_gather(values, "tensor", axis=1, tiled=True)

    def sum_grads(values):
        return lax.psum_scatter(
            values.astype(jnp.bfloat16), "tensor", scatter_dimension=1, tiled=True
        ).astype(jnp.float32)

    def core_rows(x_in, bc_in, step_raw, gate_z, conv_chan, conv_flat, head_par):
        return jax.vmap(ssm_core, in_axes=(0, 0, 0, 0, None, None, None, 0))(
            x_in, bc_in, step_raw, gate_z, conv_chan, conv_flat, head_par, segment_ids
        )

    def rotate_rows(values, sign_value):
        return jax.vmap(rotate_pairs, in_axes=(0, 0, None))(values, places, sign_value)

    gain_table = [ssm_channel[layer_pos][-1] for layer_pos in range(LAYER_COUNT)]
    residual = inputs.astype(jnp.float32)
    saved_layers = []
    for layer_index in range(LAYER_COUNT):
        shared_now = (
            lax.all_gather(norm_gains[layer_index], ("dp", "tensor"), axis=1, tiled=True),
            lax.all_gather(key_value_weight[layer_index], ("dp", "tensor"), axis=0, tiled=True),
            lax.all_gather(w_state_in[layer_index], ("dp", "tensor"), axis=0, tiled=True),
            lax.all_gather(conv_state[layer_index], ("dp", "tensor"), axis=0, tiled=True),
        )
        head_now = (
            lax.all_gather(w_query[layer_index], "dp", axis=0, tiled=True),
            lax.all_gather(w_gate_in[layer_index], "dp", axis=0, tiled=True),
            lax.all_gather(w_step[layer_index], "dp", axis=0, tiled=True),
            lax.all_gather(w_attn_out[layer_index], "dp", axis=1, tiled=True),
            lax.all_gather(w_ssm_out[layer_index], "dp", axis=1, tiled=True),
            lax.all_gather(w_gate_up[layer_index], "dp", axis=0, tiled=True),
            lax.all_gather(w_down[layer_index], "dp", axis=1, tiled=True),
        )
        forward_gain_pair = shared_now[0].astype(jnp.float32)
        forward_keyval_w = shared_now[1]
        forward_state_w = shared_now[2]
        forward_conv_flat = shared_now[3].astype(jnp.float32)
        (
            forward_query_w,
            forward_gate_in_w,
            forward_step_w,
            forward_attn_out_w,
            forward_ssm_out_w,
            forward_gate_up_w,
            forward_down_w,
        ) = head_now
        channel = ssm_channel[layer_index]
        forward_head_par = head_params[layer_index]
        forward_hidden_low = norm_rows(residual, forward_gain_pair[0]).astype(jnp.bfloat16)
        forward_hidden_rows = gather_rows(forward_hidden_low).reshape(tokens, MODEL_DIM)
        query_lin = dot_low(forward_hidden_rows, forward_query_w).reshape(
            rows_dev, sequence_length, heads_local, HEAD_SIZE
        )
        key_cols = lax.dynamic_slice_in_dim(forward_keyval_w, own_head * HEAD_SIZE, HEAD_SIZE, 1)
        value_cols = lax.dynamic_slice_in_dim(
            forward_keyval_w, (kv_heads + own_head) * HEAD_SIZE, HEAD_SIZE, 1
        )
        keyval_lin = dot_low(
            forward_hidden_rows, jnp.concatenate([key_cols, value_cols], axis=1)
        ).reshape(rows_dev, sequence_length, 2, HEAD_SIZE)
        forward_query_rot = rotate_rows(query_lin, 1.0).astype(jnp.bfloat16)
        forward_key_rot = rotate_rows(keyval_lin[:, :, :1], 1.0)[:, :, 0].astype(jnp.bfloat16)
        forward_value_low = keyval_lin[:, :, 1].astype(jnp.bfloat16)
        attended = jax.vmap(attend_rows)(
            forward_query_rot, forward_key_rot, forward_value_low, segment_ids
        )
        forward_attended_low = attended.reshape(tokens, heads_local * HEAD_SIZE).astype(
            jnp.bfloat16
        )
        gate_in = dot_low(
            forward_hidden_rows, forward_gate_in_w.reshape(MODEL_DIM, 2 * channels)
        ).reshape(rows_dev, sequence_length, 2, channels)
        state_in = dot_low(forward_hidden_rows, forward_state_w).reshape(
            rows_dev, sequence_length, 2 * NS
        )
        forward_step_raw = dot_low(forward_hidden_rows, forward_step_w).reshape(
            rows_dev, sequence_length, ssm_heads
        )
        forward_core_args = (
            gate_in[:, :, 1],
            state_in,
            forward_step_raw,
            gate_in[:, :, 0],
            channel[:-1],
            forward_conv_flat,
            forward_head_par,
        )
        forward_gated_out = core_rows(*forward_core_args)
        squares = lax.psum(jnp.sum(forward_gated_out * forward_gated_out, axis=-1), "tensor")
        forward_factor = lax.rsqrt(squares / (HS * PH) + EPSILON)[..., None]
        forward_normed_low = (
            (forward_gated_out * forward_factor * channel[-1])
            .astype(jnp.bfloat16)
            .reshape(tokens, channels)
        )
        mixed_out = dot_low(forward_attended_low, forward_attn_out_w) + dot_low(
            forward_normed_low, forward_ssm_out_w
        )
        forward_middle = residual + sum_rows(
            mixed_out.reshape(rows_dev, sequence_length, MODEL_DIM)
        )
        second_low = norm_rows(forward_middle, forward_gain_pair[1]).astype(jnp.bfloat16)
        forward_second = gather_rows(second_low).reshape(tokens, MODEL_DIM)
        forward_gate_up = dot_low(
            forward_second, forward_gate_up_w.reshape(MODEL_DIM, 2 * ffn_local)
        ).reshape(tokens, 2, ffn_local)
        forward_active_low = (jax.nn.silu(forward_gate_up[:, 0]) * forward_gate_up[:, 1]).astype(
            jnp.bfloat16
        )
        result = forward_middle + sum_rows(
            dot_low(forward_active_low, forward_down_w).reshape(
                rows_dev, sequence_length, MODEL_DIM
            )
        )
        forward_kept = (
            residual,
            forward_middle,
            forward_hidden_low,
            forward_hidden_rows,
            forward_query_rot,
            forward_key_rot,
            forward_value_low,
            forward_attended_low,
            forward_core_args,
            forward_gated_out,
            forward_factor,
            forward_normed_low,
            forward_second,
            forward_gate_up,
            forward_active_low,
        )
        kept = forward_kept
        residual = result
        saved_layers.append((kept, shared_now, head_now))
    grad_residual = cotangent.astype(jnp.float32)
    collected = [None] * LAYER_COUNT
    current_gain = [gain_table[0]]
    for layer_index in reversed(range(LAYER_COUNT)):
        kept, shared_now, head_now = saved_layers[layer_index]
        current_gain[0] = gain_table[layer_index]
        shared_back = (
            lax.all_gather(norm_gains[layer_index], ("dp", "tensor"), axis=1, tiled=True),
            lax.all_gather(key_value_weight[layer_index], ("dp", "tensor"), axis=0, tiled=True),
            lax.all_gather(w_state_in[layer_index], ("dp", "tensor"), axis=0, tiled=True),
            lax.all_gather(conv_state[layer_index], ("dp", "tensor"), axis=0, tiled=True),
        )
        (
            backward_residual,
            middle,
            hidden_low,
            hidden_rows,
            query_rot,
            key_rot,
            value_low,
            attended_low,
            core_args,
            gated_out,
            factor,
            normed_low,
            second,
            gate_up,
            active_low,
        ) = kept
        gain_pair = shared_back[0].astype(jnp.float32)
        keyval_w = shared_back[1]
        state_w = shared_back[2]
        query_w = lax.all_gather(w_query[layer_index], "dp", axis=0, tiled=True)
        gate_in_w = lax.all_gather(w_gate_in[layer_index], "dp", axis=0, tiled=True)
        step_w = lax.all_gather(w_step[layer_index], "dp", axis=0, tiled=True)
        attn_out_w = lax.all_gather(w_attn_out[layer_index], "dp", axis=1, tiled=True)
        ssm_out_w = lax.all_gather(w_ssm_out[layer_index], "dp", axis=1, tiled=True)
        gate_up_w = lax.all_gather(w_gate_up[layer_index], "dp", axis=0, tiled=True)
        down_w = lax.all_gather(w_down[layer_index], "dp", axis=1, tiled=True)
        channel_gain = core_args[4][0] * 0.0 + current_gain[0]
        grad_full = gather_grads(grad_residual.astype(jnp.bfloat16)).reshape(tokens, MODEL_DIM)
        grad_down = dot_trans(active_low, grad_full)
        grad_active = dot_back(grad_full, down_w)
        gate_part = gate_up[:, 0]
        up_part = gate_up[:, 1]
        sigmoid_gate = jax.nn.sigmoid(gate_part)
        grad_gate = grad_active * up_part * sigmoid_gate * (1.0 + gate_part * (1.0 - sigmoid_gate))
        grad_up = grad_active * gate_part * sigmoid_gate
        grad_gu_low = (
            jnp.stack([grad_gate, grad_up], axis=1)
            .astype(jnp.bfloat16)
            .reshape(tokens, 2 * ffn_local)
        )
        grad_gate_up = dot_trans(second, grad_gu_low).reshape(MODEL_DIM, 2, ffn_local)
        grad_second = sum_grads(
            dot_back(grad_gu_low, gate_up_w.reshape(MODEL_DIM, 2 * ffn_local)).reshape(
                rows_dev, sequence_length, MODEL_DIM
            )
        )
        norm_value, norm_pull = jax.vjp(norm_rows, middle, gain_pair[1])
        grad_mid_norm, grad_gain_two = norm_pull(grad_second)
        grad_middle = grad_residual + grad_mid_norm
        grad_full = gather_grads(grad_middle.astype(jnp.bfloat16)).reshape(tokens, MODEL_DIM)
        grad_attn_out = dot_trans(attended_low, grad_full)
        grad_ssm_out = dot_trans(normed_low, grad_full)
        grad_attended = (
            dot_back(grad_full, attn_out_w)
            .astype(jnp.bfloat16)
            .reshape(rows_dev, sequence_length, heads_local, HEAD_SIZE)
        )
        grad_normed = dot_back(grad_full, ssm_out_w).reshape(rows_dev, sequence_length, channels)
        grad_query_rot, grad_key_rot, grad_value = jax.vmap(attend_back)(
            query_rot, key_rot, value_low, segment_ids, grad_attended
        )
        grad_query = (
            rotate_rows(grad_query_rot, -1.0)
            .astype(jnp.bfloat16)
            .reshape(tokens, heads_local * HEAD_SIZE)
        )
        grad_key = rotate_rows(grad_key_rot[:, :, None], -1.0)[:, :, 0]
        grad_kv_part = jnp.zeros((rows_dev, sequence_length, 2, kv_heads, HEAD_SIZE), jnp.float32)
        grad_kv_part = lax.dynamic_update_slice(
            grad_kv_part,
            jnp.stack([grad_key, grad_value], axis=2)[:, :, :, None, :],
            (0, 0, 0, own_head, 0),
        )
        weighted = grad_normed * channel_gain
        cross_sum = lax.psum(jnp.sum(weighted * gated_out, axis=-1), "tensor")
        grad_gated = weighted * factor - gated_out * factor**3 * (cross_sum[..., None] / (HS * PH))
        grad_channel_gain = jnp.sum(grad_normed * gated_out * factor, axis=(0, 1))
        core_value, core_pull = jax.vjp(core_rows, *core_args)
        (
            grad_xin,
            grad_state_part,
            grad_step_raw,
            grad_gate_z,
            grad_conv_chan,
            grad_conv_flat,
            grad_head_par,
        ) = core_pull(grad_gated)
        grad_gate_in_low = (
            jnp.stack([grad_gate_z, grad_xin], axis=2)
            .astype(jnp.bfloat16)
            .reshape(tokens, 2 * channels)
        )
        grad_step_low = grad_step_raw.astype(jnp.bfloat16).reshape(tokens, ssm_heads)
        grad_query_w = dot_trans(hidden_rows, grad_query)
        grad_gate_in_w = dot_trans(hidden_rows, grad_gate_in_low).reshape(MODEL_DIM, 2, channels)
        grad_step_w = dot_trans(hidden_rows, grad_step_low)
        head_part = (
            dot_back(grad_query, query_w)
            + dot_back(grad_gate_in_low, gate_in_w.reshape(MODEL_DIM, 2 * channels))
            + dot_back(grad_step_low, step_w)
        )
        grad_hidden = sum_grads(head_part.reshape(rows_dev, sequence_length, MODEL_DIM))
        kv_total = lax.psum_scatter(
            grad_kv_part.reshape(rows_dev, sequence_length, 2 * kv_heads * HEAD_SIZE).astype(
                jnp.bfloat16
            ),
            "tensor",
            scatter_dimension=1,
            tiled=True,
        )
        state_total = lax.psum_scatter(
            grad_state_part.astype(jnp.bfloat16), "tensor", scatter_dimension=1, tiled=True
        )
        kv_low = kv_total.reshape(rows_dev * quarter, 2 * kv_heads * HEAD_SIZE)
        state_low = state_total.reshape(rows_dev * quarter, 2 * NS)
        hidden_quarter = hidden_low.reshape(rows_dev * quarter, MODEL_DIM)
        grad_keyval_w = dot_trans(hidden_quarter, kv_low)
        grad_state_w = dot_trans(hidden_quarter, state_low)
        grad_hidden = grad_hidden + (
            dot_back(kv_low, keyval_w) + dot_back(state_low, state_w)
        ).reshape(rows_dev, quarter, MODEL_DIM)
        first_value, first_pull = jax.vjp(norm_rows, backward_residual, gain_pair[0])
        grad_res_norm, grad_gain_one = first_pull(grad_hidden)
        grad_next = grad_middle + grad_res_norm
        small_grads = lax.psum(
            (jnp.concatenate([grad_conv_chan, grad_channel_gain[None, :]], axis=0), grad_head_par),
            "dp",
        )
        layer_grads = (
            lax.psum_scatter(
                jnp.stack([grad_gain_one, grad_gain_two]),
                ("dp", "tensor"),
                scatter_dimension=1,
                tiled=True,
            ),
            lax.psum_scatter(
                grad_query_w.astype(jnp.bfloat16), "dp", scatter_dimension=0, tiled=True
            ).astype(jnp.float32),
            lax.psum_scatter(grad_keyval_w, ("dp", "tensor"), scatter_dimension=0, tiled=True),
            lax.psum_scatter(
                grad_gate_in_w.astype(jnp.bfloat16), "dp", scatter_dimension=0, tiled=True
            ).astype(jnp.float32),
            lax.psum_scatter(grad_state_w, ("dp", "tensor"), scatter_dimension=0, tiled=True),
            lax.psum_scatter(
                grad_step_w.astype(jnp.bfloat16), "dp", scatter_dimension=0, tiled=True
            ).astype(jnp.float32),
            small_grads[0],
            lax.psum_scatter(grad_conv_flat, ("dp", "tensor"), scatter_dimension=0, tiled=True),
            small_grads[1],
            lax.psum_scatter(
                grad_attn_out.astype(jnp.bfloat16), "dp", scatter_dimension=1, tiled=True
            ).astype(jnp.float32),
            lax.psum_scatter(
                grad_ssm_out.astype(jnp.bfloat16), "dp", scatter_dimension=1, tiled=True
            ).astype(jnp.float32),
            lax.psum_scatter(
                grad_gate_up.astype(jnp.bfloat16), "dp", scatter_dimension=0, tiled=True
            ).astype(jnp.float32),
            lax.psum_scatter(
                grad_down.astype(jnp.bfloat16), "dp", scatter_dimension=1, tiled=True
            ).astype(jnp.float32),
        )
        collected[layer_index], grad_residual = (layer_grads, grad_next)
    stacked = [
        jnp.stack([collected[layer_pos][member] for layer_pos in range(LAYER_COUNT)])
        for member in range(13)
    ]
    return (
        residual.astype(jnp.bfloat16),
        grad_residual,
        stacked[0],
        stacked[1],
        stacked[2],
        stacked[3],
        stacked[4],
        stacked[5],
        stacked[6],
        stacked[7],
        stacked[8],
        stacked[9],
        stacked[10],
        stacked[11],
        stacked[12],
    )


def solution(mesh):
    in_specs = (
        P("dp", "tensor", None),
        P("dp", "tensor", None),
        P("dp", None),
        P(None, None, ("dp", "tensor")),
        P(None, "dp", "tensor"),
        P(None, ("dp", "tensor"), None),
        P(None, "dp", None, "tensor"),
        P(None, ("dp", "tensor"), None),
        P(None, "dp", "tensor"),
        P(None, None, "tensor"),
        P(None, ("dp", "tensor")),
        P(None, None, "tensor"),
        P(None, "tensor", "dp"),
        P(None, "tensor", "dp"),
        P(None, "dp", None, "tensor"),
        P(None, "tensor", "dp"),
    )
    out_specs = (
        P("dp", "tensor", None),
        P("dp", "tensor", None),
        P(None, None, ("dp", "tensor")),
        P(None, "dp", "tensor"),
        P(None, ("dp", "tensor"), None),
        P(None, "dp", None, "tensor"),
        P(None, ("dp", "tensor"), None),
        P(None, "dp", "tensor"),
        P(None, None, "tensor"),
        P(None, ("dp", "tensor")),
        P(None, None, "tensor"),
        P(None, "tensor", "dp"),
        P(None, "tensor", "dp"),
        P(None, "dp", None, "tensor"),
        P(None, "tensor", "dp"),
    )
    return jax.shard_map(body, mesh=mesh, in_specs=in_specs, out_specs=out_specs, check_vma=False)
```

profile of v0, /device:TPU:0, one launch (start us, length us, event | category | flops | bytes accessed | tf_op | source)
XLA Modules:
  0.0 4207.0 jit_solution(10669960198195179787)
XLA Ops:
  10.7 45.5 %all-gather = bf16[1,2,1024]{1,0,2:T(2,128)(2,1)S(1)} all-gather(bf16[1,2,32]{1,0,2:T(2,128)(2,1)S(1)} %copy.818), channel_id=2, replica_groups=mesh['dp'=8,'tensor'=4] {'dp','tensor'}, dimensions={2}, use_global_device_ids=true | all-gather | bytes 4224 | tf_op jit(solution)/shard_map/all_gather | solution.py:284
  64.4 38.4 all-gather.13
  102.8 39.3 all-gather.2
  144.4 30.7 all-gather.1
  179.0 37.0 all-reduce.73
  277.5 40.2 all-gather.7
  317.6 30.1 all-gather.8
  402.8 104.0 %while.174 = (s32[]{:T(128)}, f32[1,6,128,64]{2,3,1,0:T(8,128)S(1)}, f32[8,1,128,6,64]{2,4,3,1,0:T(8,128)}, s32[8,1,128]{2,1,0:T(1,128)S(1)}, s32[8,1]{1,0:T(8,1...) while((s32[]{:T(128)}, f32[1,6,128,64]{2,3,1,0:T(8,128)S(1)}, ...), condition=%wide.region_9.10_spmd.clone, body=%wide.region_7.9_spmd.clone.sunk | while | flops 252595456 | bytes 2472789 | solution.py:133
  562.5 47.9 %all-gather.55.cloned.1.call-done = bf16[1,1024,2,512]{3,1,2,0:T(8,128)(2,1)} async-done(((bf16[1,128,2,512]{3,1,2,0:T(8,128)(2,1)}), bf16[1,1024,2,512]{3,1,2,0:T(8,128)(2,1)}) %all-gather.55.cloned.1.call-update) | async-done | bytes 2097168 | tf_op jit(solution)/shard_map/all_gather | solution.py:295
  639.6 36.3 all-gather.57.cloned.1.call-done
  681.9 41.2 all-gather.11
  735.1 31.2 all-gather.12
  821.6 37.8 all-gather.18
  859.4 30.1 all-gather.19
  920.5 120.6 %while.175 = (s32[]{:T(128)}, f32[1,6,128,64]{2,3,1,0:T(8,128)}, f32[8,1,128,6,64]{2,4,3,1,0:T(8,128)}, s32[8,1,128]{2,1,0:T(1,128)S(1)}, s32[8,1]{1,0:T(8,128)}...) while((s32[]{:T(128)}, f32[1,6,128,64]{2,3,1,0:T(8,128)}, ...), condition=%wide.region_22.23_spmd.clone, body=%wide.region_20.22_spmd.clone.sunk | while | flops 252595456 | bytes 2472789 | solution.py:133
  1088.0 28.6 reduce-scatter.57.cloned.1.call-done
  1120.8 48.1 %all-gather.61.cloned.1.call-done = bf16[1,1024,2,512]{3,1,2,0:T(8,128)(2,1)} async-done(((bf16[1,128,2,512]{3,1,2,0:T(8,128)(2,1)}), bf16[1,1024,2,512]{3,1,2,0:T(8,128)(2,1)}) %all-gather.61.cloned.1.call-update) | async-done | bytes 2097168 | tf_op jit(solution)/shard_map/all_gather | solution.py:295
  1198.7 35.8 all-gather.63.cloned.1.call-done
  1270.4 28.8 reduce-scatter.61.cloned.1.call-done
  1305.5 177.4 %while.177 = (s32[]{:T(128)}, f32[1,6,128,64]{2,3,1,0:T(8,128)}, f32[8,1,128,6,64]{2,0,4,3,1:T(8,128)}, f32[8,1,6,128,64]{3,4,2,1,0:T(8,128)}, s32[8,1,128]{2,1,...) while((s32[]{:T(128)}, f32[1,6,128,64]{2,3,1,0:T(8,128)}, ...), condition=%wide.region_37.39_spmd.clone, body=%wide.region_35.38_spmd.clone.sunk | while | flops 252595456 | bytes 3061113 | solution.py:133
  1517.5 196.4 %while.178 = (s32[]{:T(128)}, f32[1,6,128,64]{2,3,1,0:T(8,128)S(1)}, f32[8,1,128,6,64]{2,0,4,3,1:T(8,128)}, f32[8,1,128,128]{3,2,0,1:T(8,128)}, f32[8,1,128,128]...) while((s32[]{:T(128)}, f32[1,6,128,64]{2,3,1,0:T(8,128)S(1)}, ...), condition=%wide.region_50.52_spmd.clone, body=%wide.region_40.51_spmd.clone.sunk | while | flops 607312640 | bytes 8163889 | solution.py:133
  1738.6 50.1 %while.176 = (s32[]{:T(128)}, f32[1,1024,64]{1,2,0:T(8,128)S(1)}, f32[1,1024,64]{1,2,0:T(8,128)}, f32[2,1,512,2,64]{2,0,4,3,1:T(2,128)}, s32[2]{0:T(128)}, /*ind...) while((s32[]{:T(128)}, f32[1,1024,64]{1,2,0:T(8,128)S(1)}, ...), condition=%wide.region_34.35_spmd.clone, body=%wide.region_30.34_spmd.clone.sunk | while | flops 699266560 | bytes 58910972 | solution.py:220
  1841.8 34.0 reduce-scatter.63.cloned.1.call-done
  1879.1 30.7 reduce-scatter.59.cloned.1.call-done
  1950.3 28.7 reduce-scatter.69.cloned.1.call-done
  1985.6 153.0 %while.180 = (s32[]{:T(128)}, f32[1,6,128,64]{2,3,1,0:T(8,128)S(1)}, f32[8,1,128,6,64]{2,0,4,3,1:T(8,128)}, f32[8,1,6,128,64]{3,4,2,1,0:T(8,128)}, s32[8,1,128]{...) while((s32[]{:T(128)}, f32[1,6,128,64]{2,3,1,0:T(8,128)S(1)}, ...), condition=%wide.region_64.66_spmd.clone, body=%wide.region_62.65_spmd.clone.sunk | while | flops 252595456 | bytes 3061113 | solution.py:133
  2163.4 192.1 %while.181 = (s32[]{:T(128)}, f32[1,6,128,64]{2,3,1,0:T(8,128)S(1)}, f32[8,1,128,6,64]{2,0,4,3,1:T(8,128)}, f32[8,1,128,128]{3,2,0,1:T(8,128)S(1)}, f32[8,1,128,...) while((s32[]{:T(128)}, f32[1,6,128,64]{2,3,1,0:T(8,128)S(1)}, ...), condition=%wide.region_77.79_spmd.clone, body=%wide.region_67.78_spmd.clone.sunk | while | flops 607312640 | bytes 8163889 | solution.py:133
  2365.2 50.1 %while.179 = (s32[]{:T(128)}, f32[1,1024,64]{1,2,0:T(8,128)S(1)}, f32[1,1024,64]{1,2,0:T(8,128)}, f32[2,1,512,2,64]{2,0,4,3,1:T(2,128)}, s32[2]{0:T(128)}, /*ind...) while((s32[]{:T(128)}, f32[1,1024,64]{1,2,0:T(8,128)S(1)}, ...), condition=%wide.region_61.63_spmd.clone, body=%wide.region_57.62_spmd.clone.sunk | while | flops 699266560 | bytes 58910972 | solution.py:220
  2515.9 55.8 %reduce-scatter.103.cloned.1.call-done = bf16[128,6]{1,0:T(8,128)(2,1)} async-done(((bf16[1024,6]{1,0:T(8,128)(2,1)}), bf16[128,6]{1,0:T(8,128)(2,1)}) %reduce-scatter.103.cloned.1.call-update) | async-done | bytes 1552
  2572.5 62.7 %reduce-scatter.107.cloned.1.call-done = bf16[128,128]{1,0:T(8,128)(2,1)} async-done(((bf16[1024,128]{1,0:T(8,128)(2,1)}), bf16[128,128]{1,0:T(8,128)(2,1)}) %reduce-scatter.107.cloned.1.call-update) | async-done | bytes 32784
  2636.2 64.5 %reduce-scatter.111.cloned.1.call-done = bf16[128,384]{1,0:T(8,128)(2,1)} async-done(((bf16[1024,384]{1,0:T(8,128)(2,1)}), bf16[128,384]{1,0:T(8,128)(2,1)}) %reduce-scatter.111.cloned.1.call-update) | async-done | bytes 98320
  2701.7 133.9 %reduce-scatter.99.cloned.1.call-done = f32[32,2]{1,0:T(8,128)} async-done(((f32[1024,2]{1,0:T(8,128)}), f32[32,2]{1,0:T(8,128)}) %reduce-scatter.99.cloned.1.call-update) | async-done | bytes 272
  2836.4 62.0 %reduce-scatter.113.cloned.1.call-done = bf16[128,512]{1,0:T(8,128)(2,1)} async-done(((bf16[1024,512]{1,0:T(8,128)(2,1)}), bf16[128,512]{1,0:T(8,128)(2,1)}) %reduce-scatter.113.cloned.1.call-update) | async-done | bytes 131088
  2900.3 69.0 %reduce-scatter.95.cloned.1.call-done = bf16[128,2,512]{2,0,1:T(8,128)(2,1)} async-done(((bf16[1024,2,512]{2,0,1:T(8,128)(2,1)}), bf16[128,2,512]{2,0,1:T(8,128)(2,1)}) %reduce-scatter.95.cloned.1.call-update) | async-done | bytes 262160 | tf_op jit(solution)/shard_map/reduce_scatter | solution.py:567
  2969.3 70.6 %reduce-scatter.93.cloned.1.call-done = bf16[128,2,512]{2,0,1:T(8,128)(2,1)} async-done(((bf16[1024,2,512]{2,0,1:T(8,128)(2,1)}), bf16[128,2,512]{2,0,1:T(8,128)(2,1)}) %reduce-scatter.93.cloned.1.call-update) | async-done | bytes 262160 | tf_op jit(solution)/shard_map/reduce_scatter | solution.py:567
  3044.0 34.9 all-reduce.72
  3080.2 37.1 all-reduce.71
  3119.5 48.2 %reduce-scatter.105.cloned.1.call-done = bf16[128,128]{1,0:T(8,128)(2,1)} async-done(((bf16[1024,128]{1,0:T(8,128)(2,1)}), bf16[128,128]{1,0:T(8,128)(2,1)}) %reduce-scatter.105.cloned.1.call-update) | async-done | bytes 32784
  3169.3 62.8 %reduce-scatter.79.cloned.1.call-done = bf16[128,128]{1,0:T(8,128)(2,1)} async-done(((bf16[1024,128]{1,0:T(8,128)(2,1)}), bf16[128,128]{1,0:T(8,128)(2,1)}) %reduce-scatter.79.cloned.1.call-update) | async-done | bytes 32784 | tf_op jit(solution)/shard_map/reduce_scatter | solution.py:547
  3232.1 64.3 %reduce-scatter.77.cloned.1.call-done = bf16[128,128]{1,0:T(8,128)(2,1)} async-done(((bf16[1024,128]{1,0:T(8,128)(2,1)}), bf16[128,128]{1,0:T(8,128)(2,1)}) %reduce-scatter.77.cloned.1.call-update) | async-done | bytes 32784 | tf_op jit(solution)/shard_map/reduce_scatter | solution.py:547
  3299.2 62.4 %reduce-scatter.109.cloned.1.call-done = bf16[128,384]{1,0:T(8,128)(2,1)} async-done(((bf16[1024,384]{1,0:T(8,128)(2,1)}), bf16[128,384]{1,0:T(8,128)(2,1)}) %reduce-scatter.109.cloned.1.call-update) | async-done | bytes 98320
  3363.4 65.3 %reduce-scatter.87.cloned.1.call-done = bf16[128,2,384]{2,0,1:T(8,128)(2,1)} async-done(((bf16[1024,2,384]{2,0,1:T(8,128)(2,1)}), bf16[128,2,384]{2,0,1:T(8,128)(2,1)}) %reduce-scatter.87.cloned.1.call-update) | async-done | bytes 196624 | tf_op jit(solution)/shard_map/reduce_scatter | solution.py:551
  3428.6 67.6 %reduce-scatter.85.cloned.1.call-done = bf16[128,2,384]{2,0,1:T(8,128)(2,1)} async-done(((bf16[1024,2,384]{2,0,1:T(8,128)(2,1)}), bf16[128,2,384]{2,0,1:T(8,128)(2,1)}) %reduce-scatter.85.cloned.1.call-update) | async-done | bytes 196624 | tf_op jit(solution)/shard_map/reduce_scatter | solution.py:551
  3498.8 133.4 %reduce-scatter.91.cloned.1.call-done = f32[32,256]{1,0:T(8,128)} async-done(((f32[1024,256]{1,0:T(8,128)}), f32[32,256]{1,0:T(8,128)}) %reduce-scatter.91.cloned.1.call-update) | async-done | bytes 32784 | tf_op jit(solution)/shard_map/reduce_scatter | solution.py:554
  3632.2 133.0 %reduce-scatter.89.cloned.1.call-done = f32[32,256]{1,0:T(8,128)} async-done(((f32[1024,256]{1,0:T(8,128)}), f32[32,256]{1,0:T(8,128)}) %reduce-scatter.89.cloned.1.call-update) | async-done | bytes 32784 | tf_op jit(solution)/shard_map/reduce_scatter | solution.py:554
  3766.6 131.4 %reduce-scatter.83.cloned.1.call-done = f32[32,256]{1,0:T(8,128)} async-done(((f32[1024,256]{1,0:T(8,128)}), f32[32,256]{1,0:T(8,128)}) %reduce-scatter.83.cloned.1.call-update) | async-done | bytes 32784 | tf_op jit(solution)/shard_map/reduce_scatter | solution.py:550
  3898.0 133.0 %reduce-scatter.81.cloned.1.call-done = f32[32,256]{1,0:T(8,128)} async-done(((f32[1024,256]{1,0:T(8,128)}), f32[32,256]{1,0:T(8,128)}) %reduce-scatter.81.cloned.1.call-update) | async-done | bytes 32784 | tf_op jit(solution)/shard_map/reduce_scatter | solution.py:550
  4067.7 131.2 %reduce-scatter.97.cloned.1.call-done = f32[32,2]{1,0:T(8,128)} async-done(((f32[1024,2]{1,0:T(8,128)}), f32[32,2]{1,0:T(8,128)}) %reduce-scatter.97.cloned.1.call-update) | async-done | bytes 272
  (2548 shorter events, 1820.3 us)
Async XLA Ops:
  7.2 340.5 %all-gather.53.cloned.1.call-start = ((), (), s32[]{:S(2)}) async-start(), calls=%async_computation.62 | async-start | bytes 1769472 | tf_op jit(solution)/shard_map/all_gather | solution.py:291
  9.3 341.8 %all-gather.37.cloned.1.call-start = ((), (), s32[]{:S(2)}) async-start(), calls=%async_computation.32 | async-start | bytes 2621440 | tf_op jit(solution)/shard_map/all_gather | solution.py:256
  64.3 494.0 %reduce-scatter.53.cloned.1.call-start = ((), (), s32[]{:S(2)}) async-start(), calls=%async_computation.33 | async-start | bytes 2621440 | tf_op jit(solution)/shard_map/reduce_scatter | solution.py:259
  529.5 81.0 %all-gather.55.cloned.1.call-start = ((), (), s32[]{:S(2)}) async-start(), calls=%async_computation.63 | async-start | bytes 2359296 | tf_op jit(solution)/shard_map/all_gather | solution.py:295
  532.3 101.3 %all-gather.39.cloned.1.call-start = ((), (), s32[]{:S(2)}) async-start(), calls=%async_computation.34 | async-start | bytes 2621440 | tf_op jit(solution)/shard_map/all_gather | solution.py:256
  561.6 114.2 %all-gather.57.cloned.1.call-start = ((), (), s32[]{:S(2)}) async-start(), calls=%async_computation.64 | async-start | bytes 1179648 | tf_op jit(solution)/shard_map/all_gather | solution.py:296
  562.5 168.5 %reduce-scatter.55.cloned.1.call-start = ((), (), s32[]{:S(2)}) async-start(), calls=%async_computation.35 | async-start | bytes 2621440 | tf_op jit(solution)/shard_map/reduce_scatter | solution.py:259
  681.0 208.4 %all-gather.59.cloned.1.call-start = ((), (), s32[]{:S(2)}) async-start(), calls=%async_computation.65 | async-start | bytes 1769472 | tf_op jit(solution)/shard_map/all_gather | solution.py:291
  681.8 211.2 %all-gather.41.cloned.1.call-start = ((), (), s32[]{:S(2)}) async-start(), calls=%async_computation.36 | async-start | bytes 2621440 | tf_op jit(solution)/shard_map/all_gather | solution.py:256
  734.0 382.6 %reduce-scatter.57.cloned.1.call-start = ((), (), s32[]{:S(2)}) async-start(), calls=%async_computation.37 | async-start | bytes 2621440 | tf_op jit(solution)/shard_map/reduce_scatter | solution.py:259
  1086.2 82.6 %all-gather.61.cloned.1.call-start = ((), (), s32[]{:S(2)}) async-start(), calls=%async_computation.66 | async-start | bytes 2359296 | tf_op jit(solution)/shard_map/all_gather | solution.py:295
  1087.9 104.1 %all-gather.43.cloned.1.call-start = ((), (), s32[]{:S(2)}) async-start(), calls=%async_computation.38 | async-start | bytes 2621440 | tf_op jit(solution)/shard_map/all_gather | solution.py:256
  1118.9 115.5 %all-gather.63.cloned.1.call-start = ((), (), s32[]{:S(2)}) async-start(), calls=%async_computation.67 | async-start | bytes 1179648 | tf_op jit(solution)/shard_map/all_gather | solution.py:296
  1119.7 137.8 %all-gather.45.cloned.1.call-start = ((), (), s32[]{:S(2)}) async-start(), calls=%async_computation.40 | async-start | bytes 2621440 | tf_op jit(solution)/shard_map/all_gather | solution.py:264
  1120.3 178.9 %reduce-scatter.61.cloned.1.call-start = ((), (), s32[]{:S(2)}) async-start(), calls=%async_computation.41 | async-start | bytes 2621440 | tf_op jit(solution)/shard_map/reduce_scatter | solution.py:267
  1267.6 225.4 %all-gather.47.cloned.1.call-start = ((), (), s32[]{:S(2)}) async-start(), calls=%async_computation.42 | async-start | bytes 2621440 | tf_op jit(solution)/shard_map/all_gather | solution.py:264
  1302.6 514.4 %reduce-scatter.65.cloned.1.call-start = ((), (), s32[]{:S(2)}) async-start(), calls=%async_computation.44 | async-start | bytes 655360 | tf_op jit(solution)/shard_map/reduce_scatter | solution.py:514
  1794.2 47.6 %reduce-scatter.67.cloned.1.call-start = ((), (), s32[]{:S(2)}) async-start(), calls=%async_computation.45 | async-start | bytes 655360 | tf_op jit(solution)/shard_map/reduce_scatter | solution.py:522
  1802.5 73.3 %reduce-scatter.63.cloned.1.call-start = ((), (), s32[]{:S(2)}) async-start(), calls=%async_computation.43 | async-start | bytes 2621440 | tf_op jit(solution)/shard_map/reduce_scatter | solution.py:267
  1809.2 100.6 %reduce-scatter.59.cloned.1.call-start = ((), (), s32[]{:S(2)}) async-start(), calls=%async_computation.39 | async-start | bytes 2621440 | tf_op jit(solution)/shard_map/reduce_scatter | solution.py:259
  1815.4 120.4 %all-gather.49.cloned.1.call-start = ((), (), s32[]{:S(2)}) async-start(), calls=%async_computation.46 | async-start | bytes 2621440 | tf_op jit(solution)/shard_map/all_gather | solution.py:264
  1913.0 66.0 %reduce-scatter.69.cloned.1.call-start = ((), (), s32[]{:S(2)}) async-start(), calls=%async_computation.47 | async-start | bytes 2621440 | tf_op jit(solution)/shard_map/reduce_scatter | solution.py:267
  1947.4 194.1 %all-gather.51.cloned.1.call-start = ((), (), s32[]{:S(2)}) async-start(), calls=%async_computation.48 | async-start | bytes 2621440 | tf_op jit(solution)/shard_map/all_gather | solution.py:264
  1982.4 519.9 %reduce-scatter.75.cloned.1.call-start = ((), (), s32[]{:S(2)}) async-start(), calls=%async_computation.51 | async-start | bytes 655360 | tf_op jit(solution)/shard_map/reduce_scatter | solution.py:522
  2361.3 144.8 %reduce-scatter.73.cloned.1.call-start = ((), (), s32[]{:S(2)}) async-start(), calls=%async_computation.50 | async-start | bytes 655360 | tf_op jit(solution)/shard_map/reduce_scatter | solution.py:514
  2417.8 96.7 %reduce-scatter.115.cloned.1.call-start = ((), (), s32[]{:S(2)}) async-start(), calls=%async_computation.77 | async-start | bytes 1179648
  2423.4 148.4 %reduce-scatter.103.cloned.1.call-start = ((), (), s32[]{:S(2)}) async-start(), calls=%async_computation.71 | async-start | bytes 294912
  2425.3 210.0 %reduce-scatter.107.cloned.1.call-start = ((), (), s32[]{:S(2)}) async-start(), calls=%async_computation.73 | async-start | bytes 294912
  2428.5 272.2 %reduce-scatter.111.cloned.1.call-start = ((), (), s32[]{:S(2)}) async-start(), calls=%async_computation.75 | async-start | bytes 884736
  2432.5 403.1 %reduce-scatter.99.cloned.1.call-start = ((), (), s32[]{:S(2)}) async-start(), calls=%async_computation.69 | async-start | bytes 540672
  2433.6 464.8 %reduce-scatter.113.cloned.1.call-start = ((), (), s32[]{:S(2)}) async-start(), calls=%async_computation.76 | async-start | bytes 1179648
  2439.3 530.0 %reduce-scatter.95.cloned.1.call-start = ((), (), s32[]{:S(2)}) async-start(), calls=%async_computation.61 | async-start | bytes 2359296 | tf_op jit(solution)/shard_map/reduce_scatter | solution.py:567
  2445.2 594.7 %reduce-scatter.93.cloned.1.call-start = ((), (), s32[]{:S(2)}) async-start(), calls=%async_computation.60 | async-start | bytes 2359296 | tf_op jit(solution)/shard_map/reduce_scatter | solution.py:567
  2452.2 665.9 %reduce-scatter.101.cloned.1.call-start = ((), (), s32[]{:S(2)}) async-start(), calls=%async_computation.70 | async-start | bytes 294912
  2455.1 712.6 %reduce-scatter.105.cloned.1.call-start = ((), (), s32[]{:S(2)}) async-start(), calls=%async_computation.72 | async-start | bytes 294912
  2458.1 774.0 %reduce-scatter.79.cloned.1.call-start = ((), (), s32[]{:S(2)}) async-start(), calls=%async_computation.53 | async-start | bytes 294912 | tf_op jit(solution)/shard_map/reduce_scatter | solution.py:547
  2461.3 835.1 %reduce-scatter.77.cloned.1.call-start = ((), (), s32[]{:S(2)}) async-start(), calls=%async_computation.52 | async-start | bytes 294912 | tf_op jit(solution)/shard_map/reduce_scatter | solution.py:547
  2463.5 898.1 %reduce-scatter.109.cloned.1.call-start = ((), (), s32[]{:S(2)}) async-start(), calls=%async_computation.74 | async-start | bytes 884736
  2468.4 960.2 %reduce-scatter.87.cloned.1.call-start = ((), (), s32[]{:S(2)}) async-start(), calls=%async_computation.57 | async-start | bytes 1769472 | tf_op jit(solution)/shard_map/reduce_scatter | solution.py:551
  2473.5 1022.7 %reduce-scatter.85.cloned.1.call-start = ((), (), s32[]{:S(2)}) async-start(), calls=%async_computation.56 | async-start | bytes 1769472 | tf_op jit(solution)/shard_map/reduce_scatter | solution.py:551
  2499.9 1132.4 %reduce-scatter.91.cloned.1.call-start = ((), (), s32[]{:S(2)}) async-start(), calls=%async_computation.59 | async-start | bytes 1081344 | tf_op jit(solution)/shard_map/reduce_scatter | solution.py:554
  2502.2 1263.0 %reduce-scatter.89.cloned.1.call-start = ((), (), s32[]{:S(2)}) async-start(), calls=%async_computation.58 | async-start | bytes 1081344 | tf_op jit(solution)/shard_map/reduce_scatter | solution.py:554
  2504.6 1393.4 %reduce-scatter.83.cloned.1.call-start = ((), (), s32[]{:S(2)}) async-start(), calls=%async_computation.55 | async-start | bytes 1081344 | tf_op jit(solution)/shard_map/reduce_scatter | solution.py:550
  2506.0 1525.0 %reduce-scatter.81.cloned.1.call-start = ((), (), s32[]{:S(2)}) async-start(), calls=%async_computation.54 | async-start | bytes 1081344 | tf_op jit(solution)/shard_map/reduce_scatter | solution.py:550
  2508.4 1552.4 %reduce-scatter.71.cloned.1.call-start = ((), (), s32[]{:S(2)}) async-start(), calls=%async_computation.49 | async-start | bytes 2621440 | tf_op jit(solution)/shard_map/reduce_scatter | solution.py:267
  2514.4 1684.5 %reduce-scatter.97.cloned.1.call-start = ((), (), s32[]{:S(2)}) async-start(), calls=%async_computation.68 | async-start | bytes 540672
  3363.4 697.4 %copy-start.167 = (f32[1024]{0:T(1024)S(1)}, f32[1024]{0:T(1024)}, u32[]{:S(2)}) copy-start(f32[1024]{0:T(1024)} %copy-done.166) | copy-start | bytes 12292
  3363.4 697.4 %copy-start.213 = (f32[256]{0:T(256)S(1)}, f32[256]{0:T(256)}, u32[]{:S(2)}) copy-start(f32[256]{0:T(256)} %copy-done.212) | copy-start | bytes 3076
  (298 other events, 11866.4 us)
Sparse Core Ops, SparseCore 0:
  10.8 47.2 all-gather.52
  64.4 21.0 all-gather.36
  529.6 28.6 reduce-scatter.52
  561.1 49.2 all-gather.54
  612.5 21.0 all-gather.38
  636.3 39.5 all-gather.56
  681.1 32.2 reduce-scatter.54
  715.6 46.5 all-gather.58
  763.8 21.6 all-gather.40
  1086.4 30.1 reduce-scatter.56
  1119.6 49.2 all-gather.60
  1170.9 21.0 all-gather.42
  1194.9 39.5 all-gather.62
  1235.9 21.4 all-gather.44
  1267.7 31.4 reduce-scatter.60
  1302.8 22.6 all-gather.46
  1794.3 22.6 reduce-scatter.64
  1820.1 21.6 reduce-scatter.66
  1844.3 31.4 reduce-scatter.62
  1878.3 31.4 reduce-scatter.58
  1913.1 22.5 all-gather.48
  1947.5 31.4 reduce-scatter.68
  1982.5 22.5 all-gather.50
  2361.4 22.7 reduce-scatter.74
  2417.9 22.7 reduce-scatter.72
  2444.9 63.3 reduce-scatter.114
  2511.5 60.1 reduce-scatter.102
  2575.0 60.2 reduce-scatter.106
  2639.2 61.4 reduce-scatter.110
  2702.8 132.7 reduce-scatter.98
  2839.0 59.3 reduce-scatter.112
  2902.4 66.9 reduce-scatter.94
  2973.1 66.7 reduce-scatter.92
  3043.6 60.1 reduce-scatter.100
  3107.5 60.2 reduce-scatter.104
  3171.8 60.2 reduce-scatter.78
  3236.2 60.1 reduce-scatter.76
  3300.1 61.4 reduce-scatter.108
  3364.8 63.7 reduce-scatter.86
  3432.5 63.7 reduce-scatter.84
  3498.5 133.6 reduce-scatter.90
  3634.6 130.6 reduce-scatter.88
  3767.3 130.6 reduce-scatter.82
  3900.4 130.6 reduce-scatter.80
  4033.4 27.3 reduce-scatter.70
  4064.9 133.9 reduce-scatter.96
where the time goes:
time: 4240 us; the launch traced here: 4210 us
  waiting for transfers between devices  2040 us (48%)
  local copies, waits for them, and re-layouts  611 us (14%)
  blocking collectives  604 us (14%)
  matrix products  513 us (12%)
  other arithmetic  357 us (8%)
  loops' own time  62.2 us (1%)
    unnamed x56, waiting for transfers between devices  623 us
    reduce_scatter x2, waiting for transfers between devices, body(): lax.psum_scatter(grad_state_w, ('dp', 'tensor'), scatter_dimension=0, til...  266 us
    reduce_scatter x2, waiting for transfers between devices, body(): lax.psum_scatter(grad_keyval_w, ('dp', 'tensor'), scatter_dimension=0, ti...  264 us
    dynamic_update_slice x96, local copies, waits for them, and re-layouts, state_space(): lax.scan(jax.checkpoint(one_block), start_state, pieces)  203 us
    reduce_scatter x2, waiting for transfers between devices, body(): lax.psum_scatter(grad_gate_up.astype(jnp.bfloat16), 'dp', scatter_dimensi...  140 us
    reduce_scatter x2, waiting for transfers between devices, body(): lax.psum_scatter(grad_gate_in_w.astype(jnp.bfloat16), 'dp', scatter_dimen...  133 us
    reduce_scatter x2, waiting for transfers between devices, body(): lax.psum_scatter(grad_query_w.astype(jnp.bfloat16), 'dp', scatter_dimensi...  127 us
    reduce_scatter x4, waiting for transfers between devices, sum_grads(): lax.psum_scatter(values.astype(jnp.bfloat16), 'tensor', scatter_dimension...  120 us
  transfers between devices with their start and end apart: 46, of which 35 were waited for; matrix products, arithmetic and copies ran while one was open for 14% of the time, Pallas kernels for 0%

commit v1 on v0

v1 whole, which is shorter than its diff:
```python
import functools

import jax
import jax.numpy as jnp
from jax import lax
from jax.experimental import pallas as pl
from jax.experimental.pallas import tpu as pltpu
from jax.sharding import PartitionSpec as P

HQ = 8
HD = 64
HS = 24
PH = 64
NS = 128
LAYERS = 2
EPS = 1e-05
ROPE_BASE = 100000000000.0
CHUNK = 128
QBLOCK = 256
F32 = jnp.float32
BF16 = jnp.bfloat16
EXACT = lax.Precision.HIGHEST
NEG = -1e30
VMEM_BYTES = 48 * 1024 * 1024


def dot_nn(left, right, **kw):
    return lax.dot_general(
        left, right, (((1,), (0,)), ((), ())), preferred_element_type=F32, **kw
    )


def dot_nt(left, right, **kw):
    return lax.dot_general(
        left, right, (((1,), (1,)), ((), ())), preferred_element_type=F32, **kw
    )


def dot_tn(left, right, **kw):
    return lax.dot_general(
        left, right, (((0,), (0,)), ((), ())), preferred_element_type=F32, **kw
    )


def iota(shape, dim):
    return lax.broadcasted_iota(jnp.int32, shape, dim)


def softplus(v):
    return jnp.maximum(v, 0.0) + jnp.log1p(jnp.exp(-jnp.abs(v)))


def partner(v, lane):
    return jnp.where(lane % HD < HD // 2, pltpu.roll(v, 96, 1), pltpu.roll(v, 32, 1))


def chunk_terms(act, raw_step, tok, seg_row, par):
    shape = (CHUNK, CHUNK)
    row, lane = iota(shape, 0), iota(shape, 1)
    b, c = act[:, 384:512], act[:, 512:640]
    bb, cb = b.astype(BF16), c.astype(BF16)
    dt = softplus(raw_step + par[1:2])
    tri = (row >= lane).astype(F32)
    cum = dot_nn(tri, dt * par[0:1], precision=EXACT)
    last = cum[CHUNK - 1 : CHUNK]
    okay = (row >= lane) & (tok[:, 5:6] == seg_row)
    inner = jnp.where(okay, dot_nt(cb, bb), 0.0)
    enter = jnp.exp(cum) * tok[:, 3:4]
    tail = jnp.exp(jnp.minimum(last - cum, 0.0)) * tok[:, 4:5]
    return b, c, bb, cb, dt, cum, cum.T, dt.T, okay, inner, enter, tail


def ssm_fwd_kernel(
    pa, ps, tok_r, seg_r, cos_r, sin_r, taps, par, skip,
    y_o, pre_o, st_o, sq_o, q_o, kv_o, state, hist,
):
    @pl.when(pl.program_id(0) == 0)
    def _():
        state[...] = jnp.zeros_like(state)
        hist[...] = jnp.zeros_like(hist)

    lane = iota((CHUNK, CHUNK), 1)
    half = lane < PH
    tok = tok_r[...]
    xin = jnp.concatenate([pa[:, 512:896], ps[:, 128:384]], axis=1)
    ext = jnp.concatenate([hist[...], xin], axis=0)
    hist[...] = xin[CHUNK - 8 :]
    pre = taps[4:5] + xin * taps[3:4]
    for k in (1, 2, 3):
        pre = pre + ext[8 - k : 8 - k + CHUNK] * tok[:, k - 1 : k] * taps[3 - k : 4 - k]
    pre_o[...] = pre
    act = pre * jax.nn.sigmoid(pre)
    b, c, bb, cb, dt, cum, cum_t, dt_t, okay, inner, enter, tail = chunk_terms(
        act, pa[:, 896:1024], tok, seg_r[0:1], par
    )
    tail = tail * dt
    keep = enter[CHUNK - 1 : CHUNK]
    b_t = b.T.astype(BF16)
    squares = jnp.zeros((CHUNK, CHUNK), F32)
    for p in range(3):
        h0, h1 = 2 * p, 2 * p + 1
        cols = slice(128 * p, 128 * p + 128)
        xp = act[:, cols]
        xb = xp.astype(BF16)
        own = st_o.at[0]
        sp = state[:, cols]
        own[:, cols] = sp

        def weights(h):
            gap = jnp.minimum(cum[:, h : h + 1] - cum_t[h : h + 1], 0.0)
            return (inner * jnp.exp(gap) * dt_t[h : h + 1]).astype(BF16)

        y = jnp.where(half, dot_nn(weights(h0), xb), dot_nn(weights(h1), xb))
        y = y + dot_nn(cb, sp.astype(BF16)) * jnp.where(
            half, enter[:, h0 : h0 + 1], enter[:, h1 : h1 + 1]
        )
        y = y + skip[0:1, cols] * xp
        y_o[:, cols] = y
        tp = jnp.where(half, tail[:, h0 : h0 + 1], tail[:, h1 : h1 + 1])
        kp = jnp.where(half[0:1], keep[:, h0 : h0 + 1], keep[:, h1 : h1 + 1])
        state[:, cols] = kp * sp + dot_nn(b_t, (tp * xp).astype(BF16))
        z = pa[:, 128 + 128 * p : 256 + 128 * p]
        u = y * z * jax.nn.sigmoid(z)
        squares = squares + u * u
    sq_o[...] = dot_nt(jnp.ones((8, CHUNK), F32), squares, precision=EXACT)
    cos, sin = cos_r[...], sin_r[...]
    q = pa[:, 0:128]
    q_o[...] = (q * cos + partner(q, lane) * sin).astype(BF16)
    kv = ps[:, 0:128]
    kv_o[...] = jnp.where(half, kv * cos + partner(kv, lane) * sin, kv).astype(BF16)


def ssm_bwd_kernel(
    pa, ps, pre_r, y_r, st_r, dyn_r, red_r, dq_r, dkv_r, tok_r, seg_r, taps, par, skip, gain,
    da_o, ds_o, gt_o, gc_o, gh_o, dstate, nxt,
):
    @pl.when(pl.program_id(0) == 0)
    def _():
        dstate[...] = jnp.zeros_like(dstate)
        nxt[...] = jnp.zeros_like(nxt)
        gt_o[...] = jnp.zeros_like(gt_o)
        gc_o[...] = jnp.zeros_like(gc_o)
        gh_o[...] = jnp.zeros_like(gh_o)

    shape = (CHUNK, CHUNK)
    row, lane = iota(shape, 0), iota(shape, 1)
    half = lane < PH
    sub = iota((8, CHUNK), 0)
    tok = tok_r[...]
    pre = pre_r[...]
    sg = jax.nn.sigmoid(pre)
    act = pre * sg
    b, c, bb, cb, dt, cum, cum_t, dt_t, okay, inner, enter, tail = chunk_terms(
        act, pa[:, 896:1024], tok, seg_r[0:1], par
    )
    tail_dt = tail * dt
    keep = enter[CHUNK - 1 : CHUNK]
    c_t = c.T.astype(BF16)
    r2 = jnp.broadcast_to(red_r[0:1], shape).T
    coef = jnp.broadcast_to(red_r[1:2], shape).T
    db = jnp.zeros(shape, F32)
    dc = jnp.zeros(shape, F32)
    dinner = jnp.zeros(shape, F32)
    dcum = jnp.zeros(shape, F32)
    extra = jnp.zeros(shape, F32)
    col_sum = jnp.zeros((8, CHUNK), F32)
    last_row = jnp.zeros((1, CHUNK), F32)
    dx_parts = []
    for p in range(3):
        cols = slice(128 * p, 128 * p + 128)
        z = pa[:, 128 + 128 * p : 256 + 128 * p]
        y, dyn = y_r[:, cols], dyn_r[:, cols]
        zs = jax.nn.sigmoid(z)
        sz = z * zs
        u = y * sz
        dn = dyn * r2
        gc_o[0:1, cols] += jnp.sum(dn * u, axis=0, keepdims=True)
        du = gain[0:1, cols] * dn - u * coef
        da_o[:, 128 + 128 * p : 256 + 128 * p] = (
            du * y * zs * (1.0 + z * (1.0 - zs))
        ).astype(BF16)
        dy = du * sz
        dyb = dy.astype(BF16)
        xp = act[:, cols]
        xb = xp.astype(BF16)
        gc_o[1:2, cols] += jnp.sum(dy * xp, axis=0, keepdims=True)
        own = st_r.at[0]
        sp = own[:, cols]
        sb = sp.astype(BF16)
        dsp = dstate[:, cols]
        dsb = dsp.astype(BF16)
        h0, h1 = 2 * p, 2 * p + 1
        ep = jnp.where(half, enter[:, h0 : h0 + 1], enter[:, h1 : h1 + 1])
        tp = jnp.where(half, tail_dt[:, h0 : h0 + 1], tail_dt[:, h1 : h1 + 1])
        kp = jnp.where(half[0:1], keep[:, h0 : h0 + 1], keep[:, h1 : h1 + 1])
        cdb = (ep * dy).astype(BF16)
        through = dy * ep * dot_nn(cb, sb)
        bds = dot_nn(bb, dsb)
        qx = xp * bds
        kept = jnp.sum(dsp * sp, axis=0, keepdims=True) * kp
        dxi = []
        for h in (h0, h1):
            mine = half if h == h0 else ~half
            gap = jnp.minimum(cum[:, h : h + 1] - cum_t[h : h + 1], 0.0)
            decay = jnp.where(okay, jnp.exp(gap), 0.0)
            dt_row = dt_t[h : h + 1]
            dg = dot_nt(jnp.where(mine, dy, 0.0).astype(BF16), xb)
            t1 = dg * decay
            dinner = dinner + t1 * dt_row
            w0 = t1 * inner
            col_sum = col_sum + jnp.where(sub == h, jnp.sum(w0, axis=0, keepdims=True), 0.0)
            w1 = w0 * dt_row + jnp.where(mine, through, 0.0)
            dcum = dcum + jnp.where(lane == h, jnp.sum(w1, axis=1, keepdims=True), 0.0)
            e = jnp.sum(jnp.where(mine, qx, 0.0), axis=1, keepdims=True)
            extra = extra + jnp.where(lane == h, e, 0.0)
            k = jnp.sum(jnp.where(mine[0:1], kept, 0.0), axis=1, keepdims=True)
            last_row = last_row + jnp.where(lane[0:1] == h, k, 0.0)
            dxi.append(dot_tn((decay * inner * dt_row).astype(BF16), dyb))
        dx_parts.append(jnp.where(half, dxi[0], dxi[1]) + tp * bds + skip[0:1, cols] * dy)
        dc = dc + dot_nt(cdb, sb)
        db = db + dot_nt((tp * xp).astype(BF16), dsb)
        dstate[:, cols] = kp * dsp + dot_nn(c_t, cdb)
    col_sum = jnp.concatenate([col_sum, jnp.zeros((CHUNK - 8, CHUNK), F32)], axis=0).T
    moved = tail_dt * extra
    last_row = last_row + jnp.sum(moved, axis=0, keepdims=True)
    dcum = dcum - col_sum * dt - moved + jnp.where(row == CHUNK - 1, last_row, 0.0)
    dlog = dot_nn((row <= lane).astype(F32), dcum, precision=EXACT)
    ddt = col_sum + tail * extra + par[0:1] * dlog
    gh_o[0:1] += jnp.sum(dt * dlog, axis=0, keepdims=True)
    ddr = ddt * jax.nn.sigmoid(pa[:, 896:1024] + par[1:2])
    gh_o[1:2] += jnp.sum(ddr, axis=0, keepdims=True)
    da_o[:, 896:1024] = ddr.astype(BF16)
    dib = dinner.astype(BF16)
    dc = dc + dot_nn(dib, bb)
    db = db + dot_tn(dib, cb)
    dact = jnp.concatenate([*dx_parts, db, dc], axis=1)
    dpre = dact * sg * (1.0 + pre * (1.0 - sg))
    xin = jnp.concatenate([pa[:, 512:896], ps[:, 128:384]], axis=1)
    dxin = dpre * taps[3:4]
    gt_o[3:4] += jnp.sum(dpre * xin, axis=0, keepdims=True)
    gt_o[4:5] += jnp.sum(dpre, axis=0, keepdims=True)
    for k in (1, 2, 3):
        zk = dpre * tok[:, k - 1 : k]
        later = nxt.at[k - 1]
        moved_up = jnp.concatenate([zk, later[...]], axis=0)[k : k + CHUNK]
        later[...] = zk[0:8]
        dxin = dxin + moved_up * taps[3 - k : 4 - k]
        gt_o[3 - k : 4 - k] += jnp.sum(moved_up * xin, axis=0, keepdims=True)
    da_o[:, 512:896] = dxin[:, 0:384].astype(BF16)
    ds_o[:, 128:384] = dxin[:, 384:640].astype(BF16)
    da_o[:, 0:128] = dq_r[...]
    ds_o[:, 0:128] = dkv_r[...]


def ssm_forward(pa, ps, tok, seg_rows, cos, sin, taps, par, skip):
    n = pa.shape[0]
    steps = n // CHUNK

    def rows(width):
        return pl.BlockSpec((CHUNK, width), lambda i: (i, 0))

    def fixed(shape):
        return pl.BlockSpec(shape, lambda i: (0,) * len(shape))

    return pl.pallas_call(
        ssm_fwd_kernel,
        grid=(steps,),
        in_specs=[
            rows(1024), rows(384), rows(8), pl.BlockSpec((8, CHUNK), lambda i: (0, i)),
            rows(128), rows(128), fixed((8, 640)), fixed((8, 128)), fixed((8, 384)),
        ],
        out_specs=[
            rows(384), rows(640), pl.BlockSpec((1, NS, 384), lambda i: (i, 0, 0)),
            pl.BlockSpec((8, CHUNK), lambda i: (0, i)), rows(128), rows(128),
        ],
        out_shape=[
            jax.ShapeDtypeStruct((n, 384), F32),
            jax.ShapeDtypeStruct((n, 640), F32),
            jax.ShapeDtypeStruct((steps, NS, 384), F32),
            jax.ShapeDtypeStruct((8, n), F32),
            jax.ShapeDtypeStruct((n, 128), BF16),
            jax.ShapeDtypeStruct((n, 128), BF16),
        ],
        scratch_shapes=[pltpu.VMEM((NS, 384), F32), pltpu.VMEM((8, 640), F32)],
        compiler_params=pltpu.CompilerParams(
            dimension_semantics=("arbitrary",), vmem_limit_bytes=VMEM_BYTES
        ),
        cost_estimate=pl.CostEstimate(
            flops=2 * 10**9, bytes_accessed=14 * 2**20, transcendentals=3 * 10**6
        ),
        name="ssm_forward",
    )(pa, ps, tok, seg_rows, cos, sin, taps, par, skip)


def ssm_backward(pa, ps, pre, y, states, dyn, red, dq, dkv, tok, seg_rows, taps, par, skip, gain):
    n = pa.shape[0]
    steps = n // CHUNK

    def rows(width):
        return pl.BlockSpec((CHUNK, width), lambda i: (steps - 1 - i, 0))

    def lanes():
        return pl.BlockSpec((8, CHUNK), lambda i: (0, steps - 1 - i))

    def fixed(shape):
        return pl.BlockSpec(shape, lambda i: (0,) * len(shape))

    return pl.pallas_call(
        ssm_bwd_kernel,
        grid=(steps,),
        in_specs=[
            rows(1024), rows(384), rows(640), rows(384),
            pl.BlockSpec((1, NS, 384), lambda i: (steps - 1 - i, 0, 0)),
            rows(384), lanes(), rows(128), rows(128), rows(8), lanes(),
            fixed((8, 640)), fixed((8, 128)), fixed((8, 384)), fixed((8, 384)),
        ],
        out_specs=[
            rows(1024), rows(384), fixed((8, 640)), fixed((8, 384)), fixed((8, 128)),
        ],
        out_shape=[
            jax.ShapeDtypeStruct((n, 1024), BF16),
            jax.ShapeDtypeStruct((n, 384), BF16),
            jax.ShapeDtypeStruct((8, 640), F32),
            jax.ShapeDtypeStruct((8, 384), F32),
            jax.ShapeDtypeStruct((8, 128), F32),
        ],
        scratch_shapes=[pltpu.VMEM((NS, 384), F32), pltpu.VMEM((3, 8, 640), F32)],
        compiler_params=pltpu.CompilerParams(
            dimension_semantics=("arbitrary",), vmem_limit_bytes=VMEM_BYTES
        ),
        cost_estimate=pl.CostEstimate(
            flops=5 * 10**9, bytes_accessed=20 * 2**20, transcendentals=4 * 10**6
        ),
        name="ssm_backward",
    )(pa, ps, pre, y, states, dyn, red, dq, dkv, tok, seg_rows, taps, par, skip, gain)


def head_views(kv, lane):
    zero = jnp.zeros_like(kv)
    left = lane < HD
    k0 = jnp.where(left, kv, zero)
    v1 = jnp.where(left, zero, kv)
    k1 = pltpu.roll(k0.astype(F32), HD, 1).astype(BF16)
    v0 = pltpu.roll(v1.astype(F32), HD, 1).astype(BF16)
    return (k0, k1), (v0, v1)


def allowed_keys(tok_r, seg_r, start, rows, keys):
    return (
        (iota((rows, keys), 1) <= start + iota((rows, keys), 0))
        & (tok_r[start : start + rows, 5:6] == seg_r[0:1, 0:keys])
    )


def attend_fwd_kernel(q_r, kv_r, tok_r, seg_r, o_o, lse_o):
    n = q_r.shape[0]
    ks, vs = head_views(kv_r[...], iota((n, 2 * HD), 1))
    lane = iota((QBLOCK, 128), 1)
    for start in range(0, n, QBLOCK):
        keys = start + QBLOCK
        q = q_r[start:keys]
        okay = allowed_keys(tok_r, seg_r, start, QBLOCK, keys)
        out = jnp.zeros((QBLOCK, 2 * HD), F32)
        stats = []
        for h in range(2):
            s = jnp.where(okay, dot_nt(q, ks[h][0:keys]) * HD**-0.5, NEG)
            top = jnp.max(s, axis=1, keepdims=True)
            e = jnp.exp(s - top)
            total = jnp.sum(e, axis=1, keepdims=True)
            out = out + dot_nn((e * (1.0 / total)).astype(BF16), vs[h][0:keys])
            stats.append(top + jnp.log(total))
        o_o[start:keys] = out.astype(BF16)
        lse_o[start:keys] = jnp.where(lane == 0, stats[0], stats[1])


def attend_bwd_kernel(
    q_r, kv_r, do_r, lse_r, tok_r, seg_r, cos_r, sin_r, dq_o, dkv_o, dk_acc, dv_acc
):
    n = q_r.shape[0]
    ks, vs = head_views(kv_r[...], iota((n, 2 * HD), 1))
    lane = iota((QBLOCK, 128), 1)
    left = lane < HD
    dk_acc[...] = jnp.zeros_like(dk_acc)
    dv_acc[...] = jnp.zeros_like(dv_acc)
    for start in range(0, n, QBLOCK):
        keys = start + QBLOCK
        q = q_r[start:keys]
        do = do_r[start:keys]
        okay = allowed_keys(tok_r, seg_r, start, QBLOCK, keys)
        lse = lse_r[start:keys]
        zero = jnp.zeros_like(q)
        dq = jnp.zeros((QBLOCK, 2 * HD), F32)
        for h in range(2):
            mine = left if h == 0 else ~left
            s = dot_nt(q, ks[h][0:keys]) * HD**-0.5
            p = jnp.where(okay, jnp.exp(s - lse[:, h : h + 1]), 0.0)
            dp = dot_nt(do, vs[h][0:keys])
            dot_sum = jnp.sum(p * dp, axis=1, keepdims=True)
            ds = (p * (dp - dot_sum)).astype(BF16)
            dq = dq + dot_nn(ds, ks[h][0:keys])
            dk_acc[0:keys] += dot_tn(ds, jnp.where(mine, q, zero))
            dv_acc[0:keys] += dot_tn(p.astype(BF16), jnp.where(mine, do, zero))
        dq = dq * HD**-0.5
        dq_o[start:keys] = (
            dq * cos_r[start:keys] - partner(dq, lane) * sin_r[start:keys]
        ).astype(BF16)
    for start in range(0, n, QBLOCK):
        rows = slice(start, start + QBLOCK)
        dk, dv = dk_acc[rows], dv_acc[rows]
        dk = (dk + pltpu.roll(dk, HD, 1)) * HD**-0.5
        dv = dv + pltpu.roll(dv, HD, 1)
        dk = dk * cos_r[rows] - partner(dk, lane) * sin_r[rows]
        dkv_o[rows] = jnp.where(left, dk, dv).astype(BF16)


def attend_forward(q, kv, tok, seg_rows):
    n = q.shape[0]
    return pl.pallas_call(
        attend_fwd_kernel,
        out_shape=[
            jax.ShapeDtypeStruct((n, 128), BF16),
            jax.ShapeDtypeStruct((n, 128), F32),
        ],
        compiler_params=pltpu.CompilerParams(vmem_limit_bytes=VMEM_BYTES),
        cost_estimate=pl.CostEstimate(
            flops=10**9, bytes_accessed=3 * 2**20, transcendentals=2 * 10**6
        ),
        name="attend_forward",
    )(q, kv, tok, seg_rows)


def attend_backward(q, kv, do, lse, tok, seg_rows, cos, sin):
    n = q.shape[0]
    return pl.pallas_call(
        attend_bwd_kernel,
        out_shape=[
            jax.ShapeDtypeStruct((n, 128), BF16),
            jax.ShapeDtypeStruct((n, 128), BF16),
        ],
        scratch_shapes=[pltpu.VMEM((n, 128), F32), pltpu.VMEM((n, 128), F32)],
        compiler_params=pltpu.CompilerParams(vmem_limit_bytes=VMEM_BYTES),
        cost_estimate=pl.CostEstimate(
            flops=2 * 10**9, bytes_accessed=5 * 2**20, transcendentals=2 * 10**6
        ),
        name="attend_backward",
    )(q, kv, do, lse, tok, seg_rows, cos, sin)


def swap(values, axis, distance):
    size = lax.axis_size(axis)
    return lax.ppermute(values, axis, [(i, i ^ distance) for i in range(size)])


def bits_of(axis):
    size = lax.axis_size(axis)
    return [1 << b for b in range(size.bit_length() - 1)]


def sum_over(values, axes):
    for axis in axes:
        for bit in bits_of(axis):
            values = values + swap(values, axis, bit)
    return values


def rows_gather(own, rank):
    far = swap(own, "tensor", 2)
    near = swap(own, "tensor", 1)
    both = swap(far, "tensor", 1)
    q = own.shape[0]
    full = jnp.zeros((4 * q, own.shape[1]), own.dtype)
    for distance, piece in ((0, own), (1, near), (2, far), (3, both)):
        full = lax.dynamic_update_slice(full, piece, ((rank ^ distance) * q, 0))
    return full


def rows_scatter(full, rank):
    q = full.shape[0] // 4

    def part(distance):
        return lax.dynamic_slice_in_dim(full, (rank ^ distance) * q, q, 0)

    other = swap(part(3), "tensor", 1)
    near = swap(part(1), "tensor", 1)
    sent = (part(2).astype(F32) + other.astype(F32)).astype(BF16)
    far = swap(sent, "tensor", 2)
    return part(0).astype(F32) + near.astype(F32) + far.astype(F32)


def gather_everywhere(row):
    index = lax.axis_index("dp") * lax.axis_size("tensor") + lax.axis_index("tensor")
    held, order = row, [0]
    for axis, scale in (("tensor", 1), ("dp", lax.axis_size("tensor"))):
        for bit in bits_of(axis):
            held = jnp.concatenate([held, swap(held, axis, bit)], axis=0)
            order = order + [o + bit * scale for o in order]
    want = index ^ jnp.arange(len(order))
    pick = (jnp.asarray(order)[None, :] == want[:, None]).astype(F32)
    return jnp.dot(pick, held.astype(F32), precision=EXACT)


def rms_factor(v):
    return lax.rsqrt(jnp.mean(v * v, axis=-1, keepdims=True) + EPS)


def rms_back(v, factor, gain, grad):
    weighted = grad * gain
    inner = jnp.mean(weighted * v, axis=-1, keepdims=True)
    grad_gain = jnp.sum(grad * v * factor, axis=0)
    return factor * weighted - v * factor**3 * inner, grad_gain


def pad_rows(v, rows=8):
    return jnp.pad(v, ((0, rows - v.shape[0]), (0, 0)))


def body(
    inputs, cotangent, segment_ids, norm_gains, w_query, key_value_weight, w_gate_in, w_state_in,
    w_step, ssm_channel, conv_state, head_params, w_attn_out, w_ssm_out, w_gate_up, w_down,
):
    quarter, width = inputs.shape[1:]
    n = segment_ids.shape[1]
    dp_size, tp_size = lax.axis_size("dp"), lax.axis_size("tensor")
    rank = lax.axis_index("tensor")
    slot = lax.axis_index("dp") * tp_size + rank
    kv_heads = key_value_weight.shape[2] // (2 * HD)
    own_head = rank * (w_query.shape[2] // HD) // (HQ // kv_heads)
    ssm_heads = w_step.shape[2]
    channels = ssm_heads * PH
    hidden = w_gate_up.shape[3]
    depth = w_query.shape[1]

    seg = segment_ids[0]
    segf = seg.astype(F32)
    index = jnp.arange(n, dtype=jnp.int32)
    places = index - jnp.sum((seg[None, :] < seg[:, None]).astype(jnp.int32), axis=1)
    freq = ROPE_BASE ** (-jnp.arange(HD // 2, dtype=F32) / (HD // 2))
    angle = places.astype(F32)[:, None] * freq[None, :]
    cos_one, sin_one = jnp.cos(angle), jnp.sin(angle)
    cos = jnp.concatenate([cos_one] * 4, axis=1)
    sin = jnp.concatenate([-sin_one, sin_one] * 2, axis=1)
    shifted = [
        (jnp.pad(seg, (k, 0), constant_values=-1)[:n] == seg).astype(F32) for k in (1, 2, 3)
    ]
    ends = seg.reshape(-1, CHUNK)[:, -1]
    before = jnp.concatenate([jnp.full((1,), -1, jnp.int32), ends[:-1]])
    enters = (seg.reshape(-1, CHUNK) == before[:, None]).astype(F32).reshape(-1)
    leaves = (seg.reshape(-1, CHUNK) == ends[:, None]).astype(F32).reshape(-1)
    tok = jnp.stack([*shifted, enters, leaves, segf, segf, segf], axis=1)
    seg_rows = jnp.broadcast_to(segf[None, :], (8, n))

    x_full = rows_gather(inputs[0], rank)

    small = jnp.concatenate([norm_gains.reshape(-1), conv_state.reshape(-1)])[None, :]
    small_all = gather_everywhere(small)
    gain_count = norm_gains.size
    gains = (
        small_all[:, :gain_count]
        .reshape(-1, LAYERS, 2, norm_gains.shape[2])
        .transpose(1, 2, 0, 3)
        .reshape(LAYERS, 2, width)
    )
    conv_flat = (
        small_all[:, gain_count:]
        .reshape(-1, LAYERS, conv_state.shape[1])
        .transpose(1, 0, 2)
        .reshape(LAYERS, 5, 2 * NS)
    )
    shared = jnp.concatenate([key_value_weight, w_state_in], axis=2)
    near = swap(shared, "tensor", 1)
    far = swap(shared, "tensor", 2)
    both = swap(shared, "tensor", 3)
    sq = shared.shape[1]
    block = jnp.zeros((LAYERS, tp_size * sq, shared.shape[2]), BF16)
    for distance, piece in ((0, shared), (1, near), (2, far), (3, both)):
        block = lax.dynamic_update_slice(block, piece, (0, (rank ^ distance) * sq, 0))

    def gather_dp(v):
        return lax.all_gather(v, "dp", axis=0, tiled=True)

    weights = []
    for layer in range(LAYERS):
        first = jnp.concatenate(
            [
                w_query[layer],
                w_gate_in[layer].reshape(depth, 2 * channels),
                jnp.pad(w_step[layer], ((0, 0), (0, 128 - ssm_heads))),
                block[layer],
            ],
            axis=1,
        )
        second = jnp.concatenate(
            [
                w_attn_out[layer].T,
                w_ssm_out[layer].T,
                w_gate_up[layer].reshape(depth, 2 * hidden),
                w_down[layer].T,
            ],
            axis=1,
        )
        first, second = gather_dp(first), gather_dp(second)
        w_in = first[:, :1024]
        keys = lax.dynamic_slice_in_dim(first, 1024 + own_head * HD, HD, 1)
        values = lax.dynamic_slice_in_dim(first, 1024 + (kv_heads + own_head) * HD, HD, 1)
        w_sh = jnp.concatenate([keys, values, first[:, 1024 + 2 * kv_heads * HD :]], axis=1)
        weights.append(
            (w_in, w_sh, second[:, :512], second[:, 512 : 512 + 2 * hidden], second[:, 512 + 2 * hidden :])
        )

    residual = inputs[0].astype(F32)
    saved = []
    for layer in range(LAYERS):
        w_in, w_sh, w_mix, w_gu, w_dn = weights[layer]
        channel = ssm_channel[layer]
        head = head_params[layer]
        taps = jnp.concatenate([channel[:5], conv_flat[layer]], axis=1)
        taps = pad_rows(taps)
        rate = -jnp.exp(head[0])
        par = pad_rows(
            jnp.pad(jnp.stack([rate, head[1]]), ((0, 0), (0, 128 - ssm_heads)))
        )
        skip = pad_rows(jnp.repeat(head[2], PH)[None, :])
        gain_row = pad_rows(channel[5:6])
        if layer == 0:
            xf = x_full.astype(F32)
            h = (xf * rms_factor(xf) * gains[0, 0]).astype(BF16)
        else:
            h = rows_gather((residual * rms_factor(residual) * gains[layer, 0]).astype(BF16), rank)
        pa = dot_nn(h, w_in)
        ps = dot_nn(h, w_sh)
        y, pre, states, sq, q_rot, kv_rot = ssm_forward(
            pa, ps, tok, seg_rows, cos, sin, taps, par, skip
        )
        sq_own = sq[0:1]
        sq_all = (
            sq_own + swap(sq_own, "tensor", 1) + swap(sq_own, "tensor", 2) + swap(sq_own, "tensor", 3)
        )
        o, lse = attend_forward(q_rot, kv_rot, tok, seg_rows)
        factor = lax.rsqrt(sq_all[0] / (HS * PH) + EPS)
        u = y * jax.nn.silu(pa[:, 128 : 128 + channels])
        yn = (u * factor[:, None] * channel[5]).astype(BF16)
        mixed_in = jnp.concatenate([o, yn], axis=1)
        middle = residual + rows_scatter(dot_nt(mixed_in, w_mix).astype(BF16), rank)
        h2 = rows_gather((middle * rms_factor(middle) * gains[layer, 1]).astype(BF16), rank)
        gu = dot_nn(h2, w_gu)
        act = (jax.nn.silu(gu[:, :hidden]) * gu[:, hidden:]).astype(BF16)
        result = middle + rows_scatter(dot_nt(act, w_dn).astype(BF16), rank)
        saved.append(
            (residual, middle, h, pa, ps, y, pre, states, q_rot, kv_rot, lse, factor, mixed_in, h2, gu, act,
             taps, par, skip, gain_row, rate)
        )
        residual = result

    grad = cotangent[0].astype(F32)
    big, small_grads = [None] * LAYERS, [None] * LAYERS
    for layer in reversed(range(LAYERS)):
        w_in, w_sh, w_mix, w_gu, w_dn = weights[layer]
        (first_in, middle, h, pa, ps, y, pre, states, q_rot, kv_rot, lse, factor, mixed_in, h2, gu, act,
         taps, par, skip, gain_row, rate) = saved[layer]
        df = rows_gather(grad.astype(BF16), rank)
        dact = dot_nn(df, w_dn)
        g0, g1 = gu[:, :hidden], gu[:, hidden:]
        sg = jax.nn.sigmoid(g0)
        dgu = jnp.concatenate(
            [dact * g1 * sg * (1.0 + g0 * (1.0 - sg)), dact * g0 * sg], axis=1
        ).astype(BF16)
        dh2 = rows_scatter(dot_nt(dgu, w_gu).astype(BF16), rank)
        ffn_grads = jnp.concatenate([dot_tn(h2, dgu), dot_tn(df, act)], axis=1).astype(BF16)
        ffn_grads = lax.psum_scatter(ffn_grads, "dp", scatter_dimension=0, tiled=True)
        through, dgain2 = rms_back(middle, rms_factor(middle), gains[layer, 1], dh2)
        dx1 = grad + through
        dm = rows_gather(dx1.astype(BF16), rank)
        dmix = dot_nn(dm, w_mix)
        do = dmix[:, :128].astype(BF16)
        dyn = dmix[:, 128:]
        u = y * jax.nn.silu(pa[:, 128 : 128 + channels])
        cross = jnp.sum(dyn * u * gain_row[0:1], axis=1)[None, :]
        cross = cross + swap(cross, "tensor", 1) + swap(cross, "tensor", 2) + swap(cross, "tensor", 3)
        dq, dkv = attend_backward(q_rot, kv_rot, do, lse, tok, seg_rows, cos, sin)
        red = pad_rows(jnp.stack([factor, factor**3 * cross[0] / (HS * PH)]))
        da, dsh, g_taps, g_chan, g_head = ssm_backward(
            pa, ps, pre, y, states, dyn, red, dq, dkv, tok, seg_rows, taps, par, skip, gain_row
        )
        dh = rows_scatter((dot_nt(da, w_in) + dot_nt(dsh, w_sh)).astype(BF16), rank)
        g_sh = dot_tn(h, dsh)
        wide = jnp.zeros((width, 2 * kv_heads * HD), F32)
        wide = lax.dynamic_update_slice(wide, g_sh[:, :HD], (0, own_head * HD))
        wide = lax.dynamic_update_slice(wide, g_sh[:, HD : 2 * HD], (0, (kv_heads + own_head) * HD))
        mix_grads = jnp.concatenate(
            [dot_tn(h, da), dot_tn(dm, mixed_in), wide, g_sh[:, 2 * HD :]], axis=1
        ).astype(BF16)
        mix_grads = lax.psum_scatter(mix_grads, "dp", scatter_dimension=0, tiled=True)
        back, dgain1 = rms_back(first_in, rms_factor(first_in), gains[layer, 0], dh)
        grad = dx1 + back
        chan_grad = jnp.concatenate([g_taps[:5, :channels], g_chan[0:1]], axis=0)
        head_grad = jnp.stack(
            [
                g_head[0, :ssm_heads] * rate,
                g_head[1, :ssm_heads],
                jnp.sum(g_chan[1].reshape(ssm_heads, PH), axis=1),
            ]
        )
        big[layer] = (ffn_grads, mix_grads)
        small_grads[layer] = (
            jnp.concatenate([dgain1, dgain2, g_taps[:5, channels:].reshape(-1)]),
            jnp.concatenate([chan_grad.reshape(-1), head_grad.reshape(-1)]),
        )

    wide_small = jnp.concatenate([small_grads[l][0] for l in range(LAYERS)])
    local_small = jnp.concatenate([small_grads[l][1] for l in range(LAYERS)])
    total = sum_over(jnp.concatenate([wide_small, local_small])[None, :], ("dp",))[0]
    wide_small = sum_over(total[None, : wide_small.shape[0]], ("tensor",))[0]
    wide_small = wide_small.reshape(LAYERS, -1)
    local_small = total[wide_small.size :].reshape(LAYERS, -1)
    gain_share = norm_gains.shape[2]
    conv_share = conv_state.shape[1]
    grad_gains = lax.dynamic_slice_in_dim(
        wide_small[:, : 2 * width].reshape(LAYERS, 2, width), slot * gain_share, gain_share, 2
    )
    grad_conv = lax.dynamic_slice_in_dim(wide_small[:, 2 * width :], slot * conv_share, conv_share, 1)
    grad_channel = local_small[:, : 6 * channels].reshape(LAYERS, 6, channels)
    grad_head = local_small[:, 6 * channels :].reshape(LAYERS, 3, ssm_heads)

    outs = {k: [] for k in ("q", "gate", "step", "attn", "ssm", "gu", "down", "kv", "state")}
    for layer in range(LAYERS):
        ffn_grads, mix_grads = (v.astype(F32) for v in big[layer])
        outs["gu"].append(ffn_grads[:, : 2 * hidden].reshape(depth, 2, hidden))
        outs["down"].append(ffn_grads[:, 2 * hidden :].T)
        outs["q"].append(mix_grads[:, :128])
        outs["gate"].append(mix_grads[:, 128 : 128 + 2 * channels].reshape(depth, 2, channels))
        outs["step"].append(mix_grads[:, 896 : 896 + ssm_heads])
        outs["attn"].append(mix_grads[:, 1024:1152].T)
        outs["ssm"].append(mix_grads[:, 1152:1536].T)
        sh = big[layer][1][:, 1536:]
        rows = sh.shape[0] // tp_size

        def part(distance):
            return lax.dynamic_slice_in_dim(sh, (rank ^ distance) * rows, rows, 0).astype(F32)

        sh = part(0) + sum(swap(part(d), "tensor", d) for d in (1, 2, 3))
        outs["kv"].append(sh[:, : 2 * kv_heads * HD])
        outs["state"].append(sh[:, 2 * kv_heads * HD :])
    st = {k: jnp.stack(v) for k, v in outs.items()}
    return (
        residual.astype(BF16)[None], grad[None], grad_gains, st["q"], st["kv"], st["gate"], st["state"],
        st["step"], grad_channel, grad_conv, grad_head, st["attn"], st["ssm"], st["gu"], st["down"],
    )


def solution(mesh):
    split = (
        P("dp", "tensor", None),
        P("dp", "tensor", None),
        P("dp", None),
        P(None, None, ("dp", "tensor")),
        P(None, "dp", "tensor"),
        P(None, ("dp", "tensor"), None),
        P(None, "dp", None, "tensor"),
        P(None, ("dp", "tensor"), None),
        P(None, "dp", "tensor"),
        P(None, None, "tensor"),
        P(None, ("dp", "tensor")),
        P(None, None, "tensor"),
        P(None, "tensor", "dp"),
        P(None, "tensor", "dp"),
        P(None, "dp", None, "tensor"),
        P(None, "tensor", "dp"),
    )
    out_split = split[:2] + split[3:]
    return jax.shard_map(body, mesh=mesh, in_specs=split, out_specs=out_split, check_vma=False)
```

time: 4240 us -> 751 us (0.18)
  waiting for transfers between devices: 2040 us -> 336 us
  blocking collectives: 604 us -> 0 us
  local copies, waits for them, and re-layouts: 611 us -> 98.9 us
  matrix products: 513 us -> 76.6 us
  other arithmetic: 357 us -> 72.1 us
  Pallas kernels: 0 us -> 83 us
  loops' own time: 62.2 us -> 0 us
  starting transfers between devices: 4.09 us -> 56.2 us
    reduce_scatter x22 -> x0, waiting for transfers between devices: 1160 us -> none  [the longest x2 266 us: body(): lax.psum_scatter(grad_state_w, ('dp', 'tensor'), scatter_dimension=0, til...]
    unnamed x56 -> x12, waiting for transfers between devices: 623 us -> 60.9 us
    all_gather x14 -> x0, blocking collectives: 472 us -> none  [the longest x2 86.8 us: body(): lax.all_gather(norm_gains[layer_index], ('dp', 'tensor'), axis=1, tiled=T...]
    dot_general x322 -> x31, matrix products: 459 us -> 76.6 us  [the longest x10 31.4 us: dot_nn(): lax.dot_general(left, right, (((1,), (0,)), ((), ())), preferred_element_...]
    dynamic_update_slice x104 -> x34, local copies, waits for them, and re-layouts: 227 us -> 15.3 us  [the longest x26 15.2 us: rows_gather(): full = lax.dynamic_update_slice(full, piece, ((rank ^ distance) * q, 0))]
    ppermute x0 -> x79, waiting for transfers between devices: none -> 190 us  [swap(): return lax.ppermute(values, axis, [(i, i ^ distance) for i in range(size)])]
    all_gather x14 -> x4, waiting for transfers between devices: 253 us -> 84.7 us  [gather_dp(): return lax.all_gather(v, 'dp', axis=0, tiled=True)]
    eq x113 -> x0, other arithmetic: 123 us -> none  [the longest x32 60.8 us: one_block(): piece_seg[-1] == before]
  transfers between devices with their start and end apart: 46 -> 87, of which waited for: 35 -> 38; matrix products, arithmetic and copies ran while one was open for 14% -> 29% of each run, Pallas kernels for 0% -> 11%
where the time goes in v1:
time: 751 us; the launch traced here: 740 us
  waiting for transfers between devices  336 us (45%)
  local copies, waits for them, and re-layouts  98.9 us (13%)
  Pallas kernels  83 us (11%)
  matrix products  76.6 us (10%)
  other arithmetic  72.1 us (10%)
  starting transfers between devices  56.2 us (7%)
  between operations  17.3 us (2%)
    ppermute x79, waiting for transfers between devices, swap(): return lax.ppermute(values, axis, [(i, i ^ distance) for i in range(size)])  190 us
    all_gather x4, waiting for transfers between devices, gather_dp(): return lax.all_gather(v, 'dp', axis=0, tiled=True)  84.7 us
    unnamed x12, waiting for transfers between devices  60.9 us
    ppermute x79, starting transfers between devices, swap(): return lax.ppermute(values, axis, [(i, i ^ distance) for i in range(size)])  55 us
    unnamed x284, local copies, waits for them, and re-layouts  51.1 us
    pallas_call x2, Pallas kernels, ssm_backward(): pl.pallas_call(ssm_bwd_kernel, grid=(steps,), in_specs=[rows(1024), rows(...  39.8 us
    dot_general x10, matrix products, dot_nn(): lax.dot_general(left, right, (((1,), (0,)), ((), ())), preferred_element_...  31.4 us
    dot_general x10, matrix products, dot_nt(): lax.dot_general(left, right, (((1,), (1,)), ((), ())), preferred_element_...  26.2 us
  transfers between devices with their start and end apart: 87, of which 38 were waited for; matrix products, arithmetic and copies ran while one was open for 29% of the time, Pallas kernels for 11%

profile of v1, /device:TPU:0, one launch (start us, length us, event | category | flops | bytes accessed | tf_op | source)
XLA Modules:
  0.0 740.0 jit_solution(709413433637137828)
XLA Ops:
  30.4 4.9 collective-permute-done.4
  56.8 22.5 %all-gather.5.cloned.1.call-done = bf16[1024,1536]{1,0:T(8,128)(2,1)} async-done(((bf16[128,1536]{1,0:T(8,128)(2,1)}), bf16[1024,1536]{1,0:T(8,128)(2,1)}) %all-gather.5.cloned.1.call-update) | async-done | bytes 3145744 | tf_op jit(solution)/shard_map/all_gather | solution.py:579
  84.7 4.6 fusion.15.pa
  89.4 11.5 %ssm_forward.2 = (f32[1024,384]{1,0:T(8,128)S(1)}, f32[1024,640]{1,0:T(8,128)}, f32[8,128,384]{2,1,0:T(8,128)S(1)}, f32[8,1024]{1,0:T(8,128)S(1)}, bf16[1024,128...) custom-call(f32[1024,1024]{1,0:T(8,128)} %fusion.15.pa, f32[1024,384]{1,0:T(8,128)} %fusion.46.ps, ...), custom_call_target="tpu_custom_call" | custom-call | flops 2000000000 | bytes 14680064 | tf_op jit(solution)/shard_map/ssm_forward/pallas_call | solution.py:265
  104.0 4.0 attend_forward.2
  111.0 43.1 %all-gather.7.cloned.1.call-done = bf16[1024,2048]{1,0:T(8,128)(2,1)} async-done(((bf16[128,2048]{1,0:T(8,128)(2,1)}), bf16[1024,2048]{1,0:T(8,128)(2,1)}) %all-gather.7.cloned.1.call-update) | async-done | bytes 4194320 | tf_op jit(solution)/shard_map/all_gather | solution.py:579
  160.5 12.5 %collective-permute-done.16 = bf16[256,1024]{0,1:T(8,128)(2,1)S(1)} collective-permute-done((bf16[256,1024]{0,1:T(8,128)(2,1)S(1)}, bf16[256,1024]{0,1:T(8,128)(2,1)S(1)}, u32[]{:S(2)}, u32[]{:S(2)}) %collective-permute-start.16) | collective-permute-done | bytes 524320 | tf_op jit(solution)/shard_map/ppermute | solution.py:451
  182.8 8.1 %collective-permute-done.18 = bf16[256,1024]{0,1:T(8,128)(2,1)} collective-permute-done((bf16[256,1024]{0,1:T(8,128)(2,1)}, bf16[256,1024]{0,1:T(8,128)(2,1)}, u32[]{:S(2)}, u32[]{:S(2)}) %collective-permute-start.18) | collective-permute-done | bytes 524320 | tf_op jit(solution)/shard_map/ppermute | solution.py:451
  194.5 4.7 fusion.11
  201.2 2.9 convolution_convert_fusion.3
  208.1 12.7 %collective-permute-done.22 = bf16[256,1024]{0,1:T(8,128)(2,1)S(1)} collective-permute-done((bf16[256,1024]{0,1:T(8,128)(2,1)S(1)}, bf16[256,1024]{0,1:T(8,128)(2,1)S(1)}, u32[]{:S(2)}, u32[]{:S(2)}) %collective-permute-start.22) | collective-permute-done | bytes 524320 | tf_op jit(solution)/shard_map/ppermute | solution.py:451
  226.0 12.1 %collective-permute-done.24 = bf16[256,1024]{0,1:T(8,128)(2,1)S(1)} collective-permute-done((bf16[256,1024]{0,1:T(8,128)(2,1)}, bf16[256,1024]{0,1:T(8,128)(2,1)S(1)}, u32[]{:S(2)}, u32[]{:S(2)}) %collective-permute-start.24) | collective-permute-done | bytes 524320 | tf_op jit(solution)/shard_map/ppermute | solution.py:451
  244.7 4.4 fusion.8.pa
  249.1 11.4 %ssm_forward.3 = (f32[1024,384]{1,0:T(8,128)S(1)}, f32[1024,640]{1,0:T(8,128)}, f32[8,128,384]{2,1,0:T(8,128)S(1)}, f32[8,1024]{1,0:T(8,128)S(1)}, bf16[1024,128...) custom-call(f32[1024,1024]{1,0:T(8,128)} %fusion.8.pa, f32[1024,384]{1,0:T(8,128)} %fusion.45.ps, ...), custom_call_target="tpu_custom_call" | custom-call | flops 2000000000 | bytes 14680064 | tf_op jit(solution)/shard_map/ssm_forward/pallas_call | solution.py:265
  262.6 4.0 attend_forward.3
  268.1 2.9 multiply_convert_fusion.6
  271.0 19.2 %all-gather.11.cloned.1.call-done = bf16[1024,2048]{1,0:T(8,128)(2,1)} async-done(((bf16[128,2048]{1,0:T(8,128)(2,1)}), bf16[1024,2048]{1,0:T(8,128)(2,1)}) %all-gather.11.cloned.1.call-update) | async-done | bytes 4194320 | tf_op jit(solution)/shard_map/all_gather | solution.py:579
  301.8 11.0 %collective-permute-done.31 = bf16[256,1024]{0,1:T(8,128)(2,1)} collective-permute-done((bf16[256,1024]{0,1:T(8,128)(2,1)}, bf16[256,1024]{0,1:T(8,128)(2,1)}, u32[]{:S(2)}, u32[]{:S(2)}) %collective-permute-start.31) | collective-permute-done | bytes 524320 | tf_op jit(solution)/shard_map/ppermute | solution.py:451
  317.2 6.7 collective-permute-done.39
  324.7 9.6 %collective-permute-done.33 = bf16[256,1024]{0,1:T(8,128)(2,1)S(1)} collective-permute-done((bf16[256,1024]{0,1:T(8,128)(2,1)S(1)}, bf16[256,1024]{0,1:T(8,128)(2,1)S(1)}, u32[]{:S(2)}, u32[]{:S(2)}) %collective-permute-start.33) | collective-permute-done | bytes 524320 | tf_op jit(solution)/shard_map/ppermute | solution.py:451
  357.9 4.7 copy.315
  363.2 4.8 collective-permute-done.37
  368.0 10.8 %collective-permute-done.43 = bf16[256,1024]{0,1:T(8,128)(2,1)} collective-permute-done((bf16[256,1024]{0,1:T(8,128)(2,1)}, bf16[256,1024]{0,1:T(8,128)(2,1)}, u32[]{:S(2)}, u32[]{:S(2)}) %collective-permute-start.43) | collective-permute-done | bytes 524320 | tf_op jit(solution)/shard_map/ppermute | solution.py:451
  378.8 3.6 multiply_reduce_fusion.2
  383.8 3.0 constant_dynamic-update-slice_fusion.11
  389.7 12.3 %collective-permute-done.45 = bf16[256,1024]{0,1:T(8,128)(2,1)} collective-permute-done((bf16[256,1024]{0,1:T(8,128)(2,1)}, bf16[256,1024]{0,1:T(8,128)(2,1)}, u32[]{:S(2)}, u32[]{:S(2)}) %collective-permute-start.45) | collective-permute-done | bytes 524320 | tf_op jit(solution)/shard_map/ppermute | solution.py:451
  407.8 3.1 fusion.28
  411.0 3.3 multiply_reduce_fusion.1
  417.8 6.2 attend_backward.2
  424.1 19.7 %ssm_backward.2 = (bf16[1024,1024]{1,0:T(8,128)(2,1)}, bf16[1024,384]{1,0:T(8,128)(2,1)S(1)}, f32[8,640]{1,0:T(8,128)S(1)}, f32[8,384]{1,0:T(8,128)S(1)}, f32[8,128]{1,0:T(8,128)S(1)}) custom-call(f32[1024,1024]{1,0:T(8,128)} %fusion.8.pa, f32[1024,384]{1,0:T(8,128)S(1)} %copy-done.15, f32[1024,640]{1,0:T(8,128)} %get-tuple-element.55.pre_r, ...), custom_call_target="tpu_custom_call" | custom-call | flops 5000000000 | bytes 20971520 | tf_op jit(solution)/shard_map/ssm_backward/pallas_call | solution.py:308
  451.1 6.5 copy.311
  457.7 4.7 fusion.6
  468.0 12.6 %collective-permute-done.52 = bf16[256,1024]{0,1:T(8,128)(2,1)S(1)} collective-permute-done((bf16[256,1024]{0,1:T(8,128)(2,1)S(1)}, bf16[256,1024]{0,1:T(8,128)(2,1)S(1)}, u32[]{:S(2)}, u32[]{:S(2)}) %collective-permute-start.52) | collective-permute-done | bytes 524320 | tf_op jit(solution)/shard_map/ppermute | solution.py:451
  484.5 11.9 %collective-permute-done.54 = bf16[256,1024]{0,1:T(8,128)(2,1)S(1)} collective-permute-done((bf16[256,1024]{0,1:T(8,128)(2,1)S(1)}, bf16[256,1024]{0,1:T(8,128)(2,1)S(1)}, u32[]{:S(2)}, u32[]{:S(2)}) %collective-permute-start.54) | collective-permute-done | bytes 524320 | tf_op jit(solution)/shard_map/ppermute | solution.py:451
  504.4 4.0 convolution_convert_fusion.5
  514.5 4.7 copy.313
  519.3 4.5 collective-permute-done.58
  530.2 11.6 %collective-permute-done.60 = bf16[256,1024]{0,1:T(8,128)(2,1)S(1)} collective-permute-done((bf16[256,1024]{0,1:T(8,128)(2,1)S(1)}, bf16[256,1024]{0,1:T(8,128)(2,1)S(1)}, u32[]{:S(2)}, u32[]{:S(2)}) %collective-permute-start.60) | collective-permute-done | bytes 524320 | tf_op jit(solution)/shard_map/ppermute | solution.py:451
  546.4 3.2 multiply_reduce_fusion
  553.0 6.2 attend_backward.3
  559.3 20.1 %ssm_backward.3 = (bf16[1024,1024]{1,0:T(8,128)(2,1)}, bf16[1024,384]{1,0:T(8,128)(2,1)S(1)}, f32[8,640]{1,0:T(8,128)S(1)}, f32[8,384]{1,0:T(8,128)S(1)}, f32[8,128]{1,0:T(8,128)S(1)}) custom-call(f32[1024,1024]{1,0:T(8,128)} %fusion.15.pa, f32[1024,384]{1,0:T(8,128)S(1)} %copy-done.14, f32[1024,640]{1,0:T(8,128)} %get-tuple-element.62.pre_r, ...), custom_call_target="tpu_custom_call" | custom-call | flops 5000000000 | bytes 20971520 | tf_op jit(solution)/shard_map/ssm_backward/pallas_call | solution.py:308
  587.1 6.6 copy.309
  593.8 4.7 fusion.13
  607.5 11.4 %collective-permute-done.67 = bf16[256,1024]{0,1:T(8,128)(2,1)S(1)} collective-permute-done((bf16[256,1024]{0,1:T(8,128)(2,1)S(1)}, bf16[256,1024]{0,1:T(8,128)(2,1)S(1)}, u32[]{:S(2)}, u32[]{:S(2)}) %collective-permute-start.67) | collective-permute-done | bytes 524320 | tf_op jit(solution)/shard_map/ppermute | solution.py:451
  630.7 4.0 collective-permute-done.70
  653.1 60.7 %reduce-scatter.13.cloned.1.call-done = bf16[128,2048]{1,0:T(8,128)(2,1)} async-done(((bf16[1024,2048]{1,0:T(8,128)(2,1)}), bf16[128,2048]{1,0:T(8,128)(2,1)}) %reduce-scatter.13.cloned.1.call-update) | async-done | bytes 524304
  721.8 3.6 collective-permute-done.74
  725.4 4.7 collective-permute-done.75
  (722 shorter events, 252.8 us)
Async XLA Ops:
  7.2 72.1 %all-gather.5.cloned.1.call-start = ((), (), s32[]{:S(2)}) async-start(), calls=%async_computation.4 | async-start | bytes 3538944 | tf_op jit(solution)/shard_map/all_gather | solution.py:579
  17.3 136.7 %all-gather.7.cloned.1.call-start = ((), (), s32[]{:S(2)}) async-start(), calls=%async_computation.5 | async-start | bytes 4718592 | tf_op jit(solution)/shard_map/all_gather | solution.py:579
  20.5 218.0 %all-gather.9.cloned.1.call-start = ((), (), s32[]{:S(2)}) async-start(), calls=%async_computation.6 | async-start | bytes 3538944 | tf_op jit(solution)/shard_map/all_gather | solution.py:579
  20.8 29.1 %collective-permute-start = (bf16[256,1024]{0,1:T(8,128)(2,1)S(1)}, bf16[256,1024]{0,1:T(8,128)(2,1)}, u32[]{:S(2)}, u32[]{:S(2)}) collective-permute-start(bf16[256,1024]{0,1:T(8,128)(2,1)S(1)} %bitcast.200), channel_id=1, source_target_pairs={{0,1},{1,0},{2,3},{3,2},{4,5},{5,4},{6,7},{7,6},{8,9},{9,8},{10,11... | collective-permute-start | bytes 1572872 | tf_op jit(solution)/shard_map/ppermute | solution.py:451
  21.0 27.1 %collective-permute-start.1 = (bf16[256,1024]{0,1:T(8,128)(2,1)S(1)}, bf16[256,1024]{0,1:T(8,128)(2,1)}, u32[]{:S(2)}, u32[]{:S(2)}) collective-permute-start(bf16[256,1024]{0,1:T(8,128)(2,1)S(1)} %bitcast.201), channel_id=1, source_target_pairs={{0,2},{1,3},{2,0},{3,1},{4,6},{5,7},{6,4},{7,5},{8,10},{9,11},{10,... | collective-permute-start | bytes 1572872 | tf_op jit(solution)/shard_map/ppermute | solution.py:451
  49.9 240.3 %all-gather.11.cloned.1.call-start = ((), (), s32[]{:S(2)}) async-start(), calls=%async_computation.7 | async-start | bytes 4718592 | tf_op jit(solution)/shard_map/all_gather | solution.py:579
  158.9 14.0 %collective-permute-start.16 = (bf16[256,1024]{0,1:T(8,128)(2,1)S(1)}, bf16[256,1024]{0,1:T(8,128)(2,1)S(1)}, u32[]{:S(2)}, u32[]{:S(2)}) collective-permute-start(bf16[256,1024]{0,1:T(8,128)(2,1)S(1)} %add_convert_fusion.10), channel_id=1, source_target_pairs={{0,2},{1,3},{2,0},{3,1},{4,6},{5,7},{6,4},{7,5},{8,10},{9,11},{10,... | collective-permute-start | bytes 1572872 | tf_op jit(solution)/shard_map/ppermute | solution.py:451
  177.3 13.6 %collective-permute-start.18 = (bf16[256,1024]{0,1:T(8,128)(2,1)}, bf16[256,1024]{0,1:T(8,128)(2,1)}, u32[]{:S(2)}, u32[]{:S(2)}) collective-permute-start(bf16[256,1024]{0,1:T(8,128)(2,1)} %get-tuple-element.178), channel_id=1, source_target_pairs={{0,2},{1,3},{2,0},{3,1},{4,6},{5,7},{6,4},{7,5},{8,10},{9,11},{10,... | collective-permute-start | bytes 1572872 | tf_op jit(solution)/shard_map/ppermute | solution.py:451
  180.5 10.4 %collective-permute-start.17 = (bf16[256,1024]{0,1:T(8,128)(2,1)}, bf16[256,1024]{0,1:T(8,128)(2,1)S(1)}, u32[]{:S(2)}, u32[]{:S(2)}) collective-permute-start(bf16[256,1024]{0,1:T(8,128)(2,1)} %get-tuple-element.178), channel_id=1, source_target_pairs={{0,1},{1,0},{2,3},{3,2},{4,5},{5,4},{6,7},{7,6},{8,9},{9,8},{10,11... | collective-permute-start | bytes 1572872 | tf_op jit(solution)/shard_map/ppermute | solution.py:451
  182.4 440.0 %reduce-scatter.19.cloned.1.call-start = ((), (), s32[]{:S(2)}) async-start(), calls=%async_computation.11 | async-start | bytes 3538944
  206.6 14.3 %collective-permute-start.22 = (bf16[256,1024]{0,1:T(8,128)(2,1)S(1)}, bf16[256,1024]{0,1:T(8,128)(2,1)S(1)}, u32[]{:S(2)}, u32[]{:S(2)}) collective-permute-start(bf16[256,1024]{0,1:T(8,128)(2,1)S(1)} %add_convert_fusion.9), channel_id=1, source_target_pairs={{0,2},{1,3},{2,0},{3,1},{4,6},{5,7},{6,4},{7,5},{8,10},{9,11},{10,... | collective-permute-start | bytes 1572872 | tf_op jit(solution)/shard_map/ppermute | solution.py:451
  224.6 13.6 %collective-permute-start.24 = (bf16[256,1024]{0,1:T(8,128)(2,1)}, bf16[256,1024]{0,1:T(8,128)(2,1)S(1)}, u32[]{:S(2)}, u32[]{:S(2)}) collective-permute-start(bf16[256,1024]{0,1:T(8,128)(2,1)} %get-tuple-element.174), channel_id=1, source_target_pairs={{0,2},{1,3},{2,0},{3,1},{4,6},{5,7},{6,4},{7,5},{8,10},{9,11},{10,... | collective-permute-start | bytes 1572872 | tf_op jit(solution)/shard_map/ppermute | solution.py:451
  226.0 15.2 %collective-permute-start.23 = (bf16[256,1024]{0,1:T(8,128)(2,1)}, bf16[256,1024]{0,1:T(8,128)(2,1)S(1)}, u32[]{:S(2)}, u32[]{:S(2)}) collective-permute-start(bf16[256,1024]{0,1:T(8,128)(2,1)} %get-tuple-element.174), channel_id=1, source_target_pairs={{0,1},{1,0},{2,3},{3,2},{4,5},{5,4},{6,7},{7,6},{8,9},{9,8},{10,11... | collective-permute-start | bytes 1572872 | tf_op jit(solution)/shard_map/ppermute | solution.py:451
  294.1 7.7 %collective-permute-start.29 = (bf16[256,1024]{0,1:T(8,128)(2,1)}, bf16[256,1024]{0,1:T(8,128)(2,1)}, u32[]{:S(2)}, u32[]{:S(2)}) collective-permute-start(bf16[256,1024]{0,1:T(8,128)(2,1)} %get-tuple-element.204), channel_id=1, source_target_pairs={{0,1},{1,0},{2,3},{3,2},{4,5},{5,4},{6,7},{7,6},{8,9},{9,8},{10,11... | collective-permute-start | bytes 1572872 | tf_op jit(solution)/shard_map/ppermute | solution.py:451
  297.7 15.1 %collective-permute-start.31 = (bf16[256,1024]{0,1:T(8,128)(2,1)}, bf16[256,1024]{0,1:T(8,128)(2,1)}, u32[]{:S(2)}, u32[]{:S(2)}) collective-permute-start(bf16[256,1024]{0,1:T(8,128)(2,1)} %add_convert_fusion.8), channel_id=1, source_target_pairs={{0,2},{1,3},{2,0},{3,1},{4,6},{5,7},{6,4},{7,5},{8,10},{9,11},{10,... | collective-permute-start | bytes 1572872 | tf_op jit(solution)/shard_map/ppermute | solution.py:451
  301.2 22.6 %collective-permute-start.39 = (bf16[256,1024]{0,1:T(8,128)(2,1)}, bf16[256,1024]{0,1:T(8,128)(2,1)S(1)}, u32[]{:S(2)}, u32[]{:S(2)}) collective-permute-start(bf16[256,1024]{0,1:T(8,128)(2,1)} %bitcast.202), channel_id=1, source_target_pairs={{0,2},{1,3},{2,0},{3,1},{4,6},{5,7},{6,4},{7,5},{8,10},{9,11},{10,... | collective-permute-start | bytes 1572872 | tf_op jit(solution)/shard_map/ppermute | solution.py:451
  315.7 18.6 %collective-permute-start.33 = (bf16[256,1024]{0,1:T(8,128)(2,1)S(1)}, bf16[256,1024]{0,1:T(8,128)(2,1)S(1)}, u32[]{:S(2)}, u32[]{:S(2)}) collective-permute-start(bf16[256,1024]{0,1:T(8,128)(2,1)S(1)} %get-tuple-element.170), channel_id=1, source_target_pairs={{0,2},{1,3},{2,0},{3,1},{4,6},{5,7},{6,4},{7,5},{8,10},{9,11},{10,... | collective-permute-start | bytes 1572872 | tf_op jit(solution)/shard_map/ppermute | solution.py:451
  317.2 17.1 %collective-permute-start.38 = (bf16[256,1024]{0,1:T(8,128)(2,1)S(1)}, bf16[256,1024]{0,1:T(8,128)(2,1)S(1)}, u32[]{:S(2)}, u32[]{:S(2)}) collective-permute-start(bf16[256,1024]{0,1:T(8,128)(2,1)S(1)} %bitcast.203), channel_id=1, source_target_pairs={{0,1},{1,0},{2,3},{3,2},{4,5},{5,4},{6,7},{7,6},{8,9},{9,8},{10,11... | collective-permute-start | bytes 1572872 | tf_op jit(solution)/shard_map/ppermute | solution.py:451
  323.9 10.6 %collective-permute-start.40 = (bf16[256,1024]{0,1:T(8,128)(2,1)S(1)}, bf16[256,1024]{0,1:T(8,128)(2,1)S(1)}, u32[]{:S(2)}, u32[]{:S(2)}) collective-permute-start(bf16[256,1024]{0,1:T(8,128)(2,1)S(1)} %collective-permute-done.39), channel_id=1, source_target_pairs={{0,1},{1,0},{2,3},{3,2},{4,5},{5,4},{6,7},{7,6},{8,9},{9,8},{10,11... | collective-permute-start | bytes 1572872 | tf_op jit(solution)/shard_map/ppermute | solution.py:451
  323.9 10.7 %collective-permute-start.32 = (bf16[256,1024]{0,1:T(8,128)(2,1)S(1)}, bf16[256,1024]{0,1:T(8,128)(2,1)S(1)}, u32[]{:S(2)}, u32[]{:S(2)}) collective-permute-start(bf16[256,1024]{0,1:T(8,128)(2,1)S(1)} %get-tuple-element.170), channel_id=1, source_target_pairs={{0,1},{1,0},{2,3},{3,2},{4,5},{5,4},{6,7},{7,6},{8,9},{9,8},{10,11... | collective-permute-start | bytes 1572872 | tf_op jit(solution)/shard_map/ppermute | solution.py:451
  343.8 8.2 %collective-permute-start.36 = (bf16[256,1024]{0,1:T(8,128)(2,1)S(1)}, bf16[256,1024]{0,1:T(8,128)(2,1)S(1)}, u32[]{:S(2)}, u32[]{:S(2)}) collective-permute-start(bf16[256,1024]{0,1:T(8,128)(2,1)S(1)} %get-tuple-element.203), channel_id=1, source_target_pairs={{0,1},{1,0},{2,3},{3,2},{4,5},{5,4},{6,7},{7,6},{8,9},{9,8},{10,11... | collective-permute-start | bytes 1572872 | tf_op jit(solution)/shard_map/ppermute | solution.py:451
  344.3 18.8 %collective-permute-start.35 = (bf16[256,1024]{0,1:T(8,128)(2,1)}, bf16[256,1024]{0,1:T(8,128)(2,1)}, u32[]{:S(2)}, u32[]{:S(2)}) collective-permute-start(bf16[256,1024]{0,1:T(8,128)(2,1)} %get-tuple-element.202), channel_id=1, source_target_pairs={{0,1},{1,0},{2,3},{3,2},{4,5},{5,4},{6,7},{7,6},{8,9},{9,8},{10,11... | collective-permute-start | bytes 1572872 | tf_op jit(solution)/shard_map/ppermute | solution.py:451
  350.7 12.5 %collective-permute-start.41 = (bf16[256,1024]{0,1:T(8,128)(2,1)}, bf16[256,1024]{0,1:T(8,128)(2,1)}, u32[]{:S(2)}, u32[]{:S(2)}) collective-permute-start(bf16[256,1024]{0,1:T(8,128)(2,1)} %get-tuple-element.200), channel_id=1, source_target_pairs={{0,1},{1,0},{2,3},{3,2},{4,5},{5,4},{6,7},{7,6},{8,9},{9,8},{10,11... | collective-permute-start | bytes 1572872 | tf_op jit(solution)/shard_map/ppermute | solution.py:451
  353.0 15.0 %collective-permute-start.37 = (bf16[256,1024]{0,1:T(8,128)(2,1)}, bf16[256,1024]{0,1:T(8,128)(2,1)}, u32[]{:S(2)}, u32[]{:S(2)}) collective-permute-start(bf16[256,1024]{0,1:T(8,128)(2,1)} %add_convert_fusion.7), channel_id=1, source_target_pairs={{0,2},{1,3},{2,0},{3,1},{4,6},{5,7},{6,4},{7,5},{8,10},{9,11},{10,... | collective-permute-start | bytes 1572872 | tf_op jit(solution)/shard_map/ppermute | solution.py:451
  355.5 23.4 %collective-permute-start.43 = (bf16[256,1024]{0,1:T(8,128)(2,1)}, bf16[256,1024]{0,1:T(8,128)(2,1)}, u32[]{:S(2)}, u32[]{:S(2)}) collective-permute-start(bf16[256,1024]{0,1:T(8,128)(2,1)} %add_convert_fusion.5), channel_id=1, source_target_pairs={{0,2},{1,3},{2,0},{3,1},{4,6},{5,7},{6,4},{7,5},{8,10},{9,11},{10,... | collective-permute-start | bytes 1572872 | tf_op jit(solution)/shard_map/ppermute | solution.py:451
  362.6 280.6 %reduce-scatter.15.cloned.1.call-start = ((), (), s32[]{:S(2)}) async-start(), calls=%async_computation.9 | async-start | bytes 4718592
  388.1 13.9 %collective-permute-start.45 = (bf16[256,1024]{0,1:T(8,128)(2,1)}, bf16[256,1024]{0,1:T(8,128)(2,1)}, u32[]{:S(2)}, u32[]{:S(2)}) collective-permute-start(bf16[256,1024]{0,1:T(8,128)(2,1)} %get-tuple-element.167), channel_id=1, source_target_pairs={{0,2},{1,3},{2,0},{3,1},{4,6},{5,7},{6,4},{7,5},{8,10},{9,11},{10,... | collective-permute-start | bytes 1572872 | tf_op jit(solution)/shard_map/ppermute | solution.py:451
  389.7 12.4 %collective-permute-start.44 = (bf16[256,1024]{0,1:T(8,128)(2,1)}, bf16[256,1024]{0,1:T(8,128)(2,1)}, u32[]{:S(2)}, u32[]{:S(2)}) collective-permute-start(bf16[256,1024]{0,1:T(8,128)(2,1)} %get-tuple-element.167), channel_id=1, source_target_pairs={{0,1},{1,0},{2,3},{3,2},{4,5},{5,4},{6,7},{7,6},{8,9},{9,8},{10,11... | collective-permute-start | bytes 1572872 | tf_op jit(solution)/shard_map/ppermute | solution.py:451
  414.3 9.7 %collective-permute-start.47 = (f32[1,1024]{1,0:T(1,128)S(1)}, f32[1,1024]{1,0:T(1,128)S(1)}, u32[]{:S(2)}, u32[]{:S(2)}) collective-permute-start(f32[1,1024]{1,0:T(1,128)S(1)} %bitcast.248), channel_id=1, source_target_pairs={{0,1},{1,0},{2,3},{3,2},{4,5},{5,4},{6,7},{7,6},{8,9},{9,8},{10,11... | collective-permute-start | bytes 12296 | tf_op jit(solution)/shard_map/ppermute | solution.py:451
  414.9 9.1 %collective-permute-start.48 = (f32[1,1024]{1,0:T(1,128)S(1)}, f32[1,1024]{1,0:T(1,128)S(1)}, u32[]{:S(2)}, u32[]{:S(2)}) collective-permute-start(f32[1,1024]{1,0:T(1,128)S(1)} %bitcast.249), channel_id=1, source_target_pairs={{0,2},{1,3},{2,0},{3,1},{4,6},{5,7},{6,4},{7,5},{8,10},{9,11},{10,... | collective-permute-start | bytes 12296 | tf_op jit(solution)/shard_map/ppermute | solution.py:451
  457.7 191.5 %reduce-scatter.17.cloned.1.call-start = ((), (), s32[]{:S(2)}) async-start(), calls=%async_computation.10 | async-start | bytes 3538944
  466.4 14.2 %collective-permute-start.52 = (bf16[256,1024]{0,1:T(8,128)(2,1)S(1)}, bf16[256,1024]{0,1:T(8,128)(2,1)S(1)}, u32[]{:S(2)}, u32[]{:S(2)}) collective-permute-start(bf16[256,1024]{0,1:T(8,128)(2,1)S(1)} %add_convert_fusion.4), channel_id=1, source_target_pairs={{0,2},{1,3},{2,0},{3,1},{4,6},{5,7},{6,4},{7,5},{8,10},{9,11},{10,... | collective-permute-start | bytes 1572872 | tf_op jit(solution)/shard_map/ppermute | solution.py:451
  482.9 13.4 %collective-permute-start.54 = (bf16[256,1024]{0,1:T(8,128)(2,1)S(1)}, bf16[256,1024]{0,1:T(8,128)(2,1)S(1)}, u32[]{:S(2)}, u32[]{:S(2)}) collective-permute-start(bf16[256,1024]{0,1:T(8,128)(2,1)S(1)} %get-tuple-element.164), channel_id=1, source_target_pairs={{0,2},{1,3},{2,0},{3,1},{4,6},{5,7},{6,4},{7,5},{8,10},{9,11},{10,... | collective-permute-start | bytes 1572872 | tf_op jit(solution)/shard_map/ppermute | solution.py:451
  484.5 11.9 %collective-permute-start.53 = (bf16[256,1024]{0,1:T(8,128)(2,1)S(1)}, bf16[256,1024]{0,1:T(8,128)(2,1)S(1)}, u32[]{:S(2)}, u32[]{:S(2)}) collective-permute-start(bf16[256,1024]{0,1:T(8,128)(2,1)S(1)} %get-tuple-element.164), channel_id=1, source_target_pairs={{0,1},{1,0},{2,3},{3,2},{4,5},{5,4},{6,7},{7,6},{8,9},{9,8},{10,11... | collective-permute-start | bytes 1572872 | tf_op jit(solution)/shard_map/ppermute | solution.py:451
  504.0 15.3 %collective-permute-start.56 = (bf16[256,1024]{0,1:T(8,128)(2,1)}, bf16[256,1024]{0,1:T(8,128)(2,1)S(1)}, u32[]{:S(2)}, u32[]{:S(2)}) collective-permute-start(bf16[256,1024]{0,1:T(8,128)(2,1)} %get-tuple-element.194), channel_id=1, source_target_pairs={{0,1},{1,0},{2,3},{3,2},{4,5},{5,4},{6,7},{7,6},{8,9},{9,8},{10,11... | collective-permute-start | bytes 1572872 | tf_op jit(solution)/shard_map/ppermute | solution.py:451
  509.4 14.4 %collective-permute-start.58 = (bf16[256,1024]{0,1:T(8,128)(2,1)}, bf16[256,1024]{0,1:T(8,128)(2,1)}, u32[]{:S(2)}, u32[]{:S(2)}) collective-permute-start(bf16[256,1024]{0,1:T(8,128)(2,1)} %add_convert_fusion.3), channel_id=1, source_target_pairs={{0,2},{1,3},{2,0},{3,1},{4,6},{5,7},{6,4},{7,5},{8,10},{9,11},{10,... | collective-permute-start | bytes 1572872 | tf_op jit(solution)/shard_map/ppermute | solution.py:451
  519.2 194.6 %reduce-scatter.13.cloned.1.call-start = ((), (), s32[]{:S(2)}) async-start(), calls=%async_computation.8 | async-start | bytes 4718592
  528.5 13.2 %collective-permute-start.60 = (bf16[256,1024]{0,1:T(8,128)(2,1)S(1)}, bf16[256,1024]{0,1:T(8,128)(2,1)S(1)}, u32[]{:S(2)}, u32[]{:S(2)}) collective-permute-start(bf16[256,1024]{0,1:T(8,128)(2,1)S(1)} %get-tuple-element.161), channel_id=1, source_target_pairs={{0,2},{1,3},{2,0},{3,1},{4,6},{5,7},{6,4},{7,5},{8,10},{9,11},{10,... | collective-permute-start | bytes 1572872 | tf_op jit(solution)/shard_map/ppermute | solution.py:451
  530.2 11.6 %collective-permute-start.59 = (bf16[256,1024]{0,1:T(8,128)(2,1)S(1)}, bf16[256,1024]{0,1:T(8,128)(2,1)S(1)}, u32[]{:S(2)}, u32[]{:S(2)}) collective-permute-start(bf16[256,1024]{0,1:T(8,128)(2,1)S(1)} %get-tuple-element.161), channel_id=1, source_target_pairs={{0,1},{1,0},{2,3},{3,2},{4,5},{5,4},{6,7},{7,6},{8,9},{9,8},{10,11... | collective-permute-start | bytes 1572872 | tf_op jit(solution)/shard_map/ppermute | solution.py:451
  549.6 9.6 %collective-permute-start.62 = (f32[1,1024]{1,0:T(1,128)S(1)}, f32[1,1024]{1,0:T(1,128)S(1)}, u32[]{:S(2)}, u32[]{:S(2)}) collective-permute-start(f32[1,1024]{1,0:T(1,128)S(1)} %bitcast.244), channel_id=1, source_target_pairs={{0,1},{1,0},{2,3},{3,2},{4,5},{5,4},{6,7},{7,6},{8,9},{9,8},{10,11... | collective-permute-start | bytes 12296 | tf_op jit(solution)/shard_map/ppermute | solution.py:451
  549.8 9.4 %collective-permute-start.63 = (f32[1,1024]{1,0:T(1,128)S(1)}, f32[1,1024]{1,0:T(1,128)S(1)}, u32[]{:S(2)}, u32[]{:S(2)}) collective-permute-start(f32[1,1024]{1,0:T(1,128)S(1)} %bitcast.245), channel_id=1, source_target_pairs={{0,2},{1,3},{2,0},{3,1},{4,6},{5,7},{6,4},{7,5},{8,10},{9,11},{10,... | collective-permute-start | bytes 12296 | tf_op jit(solution)/shard_map/ppermute | solution.py:451
  551.4 7.8 %collective-permute-start.64 = (f32[1,1024]{1,0:T(1,128)S(1)}, f32[1,1024]{1,0:T(1,128)S(1)}, u32[]{:S(2)}, u32[]{:S(2)}) collective-permute-start(f32[1,1024]{1,0:T(1,128)S(1)} %bitcast.246), channel_id=1, source_target_pairs={{0,3},{1,2},{2,1},{3,0},{4,7},{5,6},{6,5},{7,4},{8,11},{9,10},{10,... | collective-permute-start | bytes 12296 | tf_op jit(solution)/shard_map/ppermute | solution.py:451
  604.7 14.3 %collective-permute-start.67 = (bf16[256,1024]{0,1:T(8,128)(2,1)S(1)}, bf16[256,1024]{0,1:T(8,128)(2,1)S(1)}, u32[]{:S(2)}, u32[]{:S(2)}) collective-permute-start(bf16[256,1024]{0,1:T(8,128)(2,1)S(1)} %add_convert_fusion.2), channel_id=1, source_target_pairs={{0,2},{1,3},{2,0},{3,1},{4,6},{5,7},{6,4},{7,5},{8,10},{9,11},{10,... | collective-permute-start | bytes 1572872 | tf_op jit(solution)/shard_map/ppermute | solution.py:451
  645.7 75.0 %collective-permute-start.76 = (f32[32,512]{0,1:T(8,128)}, f32[32,512]{0,1:T(8,128)}, u32[]{:S(2)}, u32[]{:S(2)}) collective-permute-start(f32[32,512]{0,1:T(8,128)} %get-tuple-element.235), channel_id=1, source_target_pairs={{0,1},{1,0},{2,3},{3,2},{4,5},{5,4},{6,7},{7,6},{8,9},{9,8},{10,11... | collective-permute-start | bytes 196616 | tf_op jit(solution)/shard_map/ppermute | solution.py:451
  645.7 76.0 %collective-permute-start.77 = (f32[32,512]{0,1:T(8,128)}, f32[32,512]{0,1:T(8,128)}, u32[]{:S(2)}, u32[]{:S(2)}) collective-permute-start(f32[32,512]{0,1:T(8,128)} %get-tuple-element.233), channel_id=1, source_target_pairs={{0,2},{1,3},{2,0},{3,1},{4,6},{5,7},{6,4},{7,5},{8,10},{9,11},{10,... | collective-permute-start | bytes 196616 | tf_op jit(solution)/shard_map/ppermute | solution.py:451
  647.3 74.5 %collective-permute-start.78 = (f32[32,512]{0,1:T(8,128)}, f32[32,512]{0,1:T(8,128)}, u32[]{:S(2)}, u32[]{:S(2)}) collective-permute-start(f32[32,512]{0,1:T(8,128)} %get-tuple-element.234), channel_id=1, source_target_pairs={{0,3},{1,2},{2,1},{3,0},{4,7},{5,6},{6,5},{7,4},{8,11},{9,10},{10,... | collective-permute-start | bytes 196616 | tf_op jit(solution)/shard_map/ppermute | solution.py:451
  716.2 9.2 %collective-permute-start.74 = (f32[32,512]{0,1:T(8,128)S(1)}, f32[32,512]{0,1:T(8,128)S(1)}, u32[]{:S(2)}, u32[]{:S(2)}) collective-permute-start(f32[32,512]{0,1:T(8,128)S(1)} %get-tuple-element.230), channel_id=1, source_target_pairs={{0,2},{1,3},{2,0},{3,1},{4,6},{5,7},{6,4},{7,5},{8,10},{9,11},{10,... | collective-permute-start | bytes 196616 | tf_op jit(solution)/shard_map/ppermute | solution.py:451
  720.7 9.3 %collective-permute-start.75 = (f32[32,512]{0,1:T(8,128)S(1)}, f32[32,512]{0,1:T(8,128)S(1)}, u32[]{:S(2)}, u32[]{:S(2)}) collective-permute-start(f32[32,512]{0,1:T(8,128)S(1)} %get-tuple-element.231), channel_id=1, source_target_pairs={{0,3},{1,2},{2,1},{3,0},{4,7},{5,6},{6,5},{7,4},{8,11},{9,10},{10,... | collective-permute-start | bytes 196616 | tf_op jit(solution)/shard_map/ppermute | solution.py:451
  (169 other events, 1422.6 us)
Sparse Core Ops, SparseCore 0:
  17.5 61.7 all-gather.4
  82.0 72.0 all-gather.6
  156.8 58.7 all-gather.8
  218.1 72.0 all-gather.10
  362.8 72.7 reduce-scatter.18
  457.8 86.4 reduce-scatter.14
  548.2 74.1 reduce-scatter.16
  626.5 87.2 reduce-scatter.12

commit v2 on v1

v2 whole, which is shorter than its diff:
```python
import functools

import jax
import jax.numpy as jnp
from jax import lax
from jax.experimental import pallas as pl
from jax.experimental.pallas import tpu as pltpu
from jax.sharding import PartitionSpec as P

HQ = 8
HD = 64
HS = 24
PH = 64
NS = 128
LAYERS = 2
EPS = 1e-05
ROPE_BASE = 100000000000.0
R = 128
QUARTERS = 4
DISTANCE = (1, 3, 0, 2)
F32 = jnp.float32
BF16 = jnp.bfloat16
EXACT = lax.Precision.HIGHEST
NEG = -1e30
VMEM_BYTES = 28 * 1024 * 1024


def dot_nn(left, right, **kw):
    return lax.dot_general(
        left, right, (((1,), (0,)), ((), ())), preferred_element_type=F32, **kw
    )


def dot_nt(left, right, **kw):
    return lax.dot_general(
        left, right, (((1,), (1,)), ((), ())), preferred_element_type=F32, **kw
    )


def dot_tn(left, right, **kw):
    return lax.dot_general(
        left, right, (((0,), (0,)), ((), ())), preferred_element_type=F32, **kw
    )


def iota(shape, dim):
    return lax.broadcasted_iota(jnp.int32, shape, dim)


def softplus(v):
    return jnp.maximum(v, 0.0) + jnp.log1p(jnp.exp(-jnp.abs(v)))


def partner(v, lane):
    return jnp.where(lane % HD < HD // 2, pltpu.roll(v, 96, 1), pltpu.roll(v, 32, 1))


def block_of(quarter, rank):
    k = quarter ^ rank
    return 2 - 2 * (k & 1) + (k >> 1)


def sds(shape, dtype):
    return jax.ShapeDtypeStruct(shape, dtype)


def whole(shape, *at):
    at = at or (0,) * len(shape)
    return pl.BlockSpec(shape, lambda *_: at)


SCALAR = pl.BlockSpec(memory_space=pltpu.SMEM)


def call(kernel, name, in_specs, out_shapes, flops, scratch=(), deps=()):
    if deps:
        base, skipped = kernel, range(len(in_specs), len(in_specs) + len(deps))

        def kernel(*refs):
            base(*(r for i, r in enumerate(refs) if i not in skipped))

        in_specs = list(in_specs) + [pl.BlockSpec(memory_space=pl.ANY)] * len(deps)
    many = sum(s.size * s.dtype.itemsize for s in out_shapes)
    made = pl.pallas_call(
        kernel,
        grid=(1,),
        in_specs=in_specs,
        out_specs=[whole(s.shape) for s in out_shapes],
        out_shape=out_shapes,
        scratch_shapes=list(scratch),
        compiler_params=pltpu.CompilerParams(
            dimension_semantics=("arbitrary",), vmem_limit_bytes=VMEM_BYTES
        ),
        cost_estimate=pl.CostEstimate(
            flops=int(flops), bytes_accessed=2 * many, transcendentals=10**5
        ),
        name=name,
    )
    return lambda *args: made(*args, *deps)


def rms(v, gain):
    return v * lax.rsqrt(jnp.mean(v * v, axis=-1, keepdims=True) + EPS) * gain


def rms_back(v, gain, grad):
    factor = lax.rsqrt(jnp.mean(v * v, axis=-1, keepdims=True) + EPS)
    weighted = grad * gain
    inner = jnp.mean(weighted * v, axis=-1, keepdims=True)
    scaled = v * factor
    return (
        factor * weighted - scaled * (factor * factor * inner),
        jnp.sum(grad * scaled, axis=0, keepdims=True),
    )


def step_kernel(x, keep, got, far, gain, x_o, h_o):
    total = keep[...].astype(F32) + got[...].astype(F32) + far[...].astype(F32)
    new = x[...].astype(F32) + total
    x_o[...] = new.astype(x_o.dtype)
    if h_o is not None:
        h_o[...] = rms(new, gain[0:1]).astype(BF16)


def last_kernel(x, keep, got, far, x_o):
    step_kernel(x, keep, got, far, None, x_o, None)


def take_step(x, keep, got, far, gain):
    w = x.shape[1]
    specs = [whole((R, w))] * 4
    if gain is None:
        return call(last_kernel, "last_step", specs, [sds((R, w), BF16)], 10**6)(
            x, keep, got, far
        )[0]
    return call(
        step_kernel, "step", specs + [whole((8, w))], [sds((R, w), F32), sds((R, w), BF16)], 10**6
    )(x, keep, got, far, gain)


def back_step_kernel(g, v, keep, got, far, gain, g_o, low_o, gg_o):
    grad = keep[...].astype(F32) + got[...].astype(F32) + far[...].astype(F32)
    through, gg = rms_back(v[...].astype(F32), gain[0:1], grad)
    new = g[...].astype(F32) + through
    g_o[...] = new
    low_o[...] = new.astype(BF16)
    gg_o[...] = jnp.broadcast_to(gg, gg_o.shape)


def back_step(g, v, keep, got, far, gain, deps=()):
    w = v.shape[1]
    return call(
        back_step_kernel,
        "back_step",
        [whole((R, w))] * 5 + [whole((8, w))],
        [sds((R, w), F32), sds((R, w), BF16), sds((8, w), F32)],
        10**6,
        deps=deps,
    )(g, v, keep, got, far, gain)


def input_kernel(first, depth, rank, oh, p0, p1, p2, p3, gain, w_in, *refs):
    shares, outs = refs[: len(refs) - 4], refs[len(refs) - 4 :]
    h_o, pa_o, dt_o, ps_o = outs
    if len(shares) > 1:
        *shares, w_sh = shares
        sq = depth // QUARTERS
        for distance, share in enumerate(shares):
            for dp in range(share.shape[0] // depth):
                at = pl.multiple_of(dp * depth + (rank[0] ^ distance) * sq, sq)
                for c in range(QUARTERS):
                    rows = slice(dp * depth + c * sq, dp * depth + (c + 1) * sq)
                    w_sh[pl.ds(at, sq), 128 * c : 128 * c + 128] = share[rows]
    else:
        w_sh = shares[0]
    h = jnp.concatenate([p0[...], p1[...], p2[...], p3[...]], axis=0)
    if first:
        h = rms(h.astype(F32), gain[0:1]).astype(BF16)
    h_o[...] = h
    pa = dot_nn(h, w_in[...])
    pa_o[...] = pa[:, 0:896].astype(BF16)
    dt_o[...] = pa[:, 896:1024]
    ps = dot_nn(h, w_sh[...])
    k, v = ps[:, 0:128], ps[:, 128:256]
    left = iota(k.shape, 1) < HD
    is_first = oh[0] == 0
    k = jnp.where(is_first, k, pltpu.roll(k, HD, 1))
    v = jnp.where(is_first, pltpu.roll(v, HD, 1), v)
    ps_o[:, 0:128] = jnp.where(left, k, v).astype(BF16)
    ps_o[:, 128:384] = ps[:, 256:512].astype(BF16)


def project_in(first, depth, rank, oh, pieces, gain, w_in, w_sh):
    w = pieces[0].shape[1]
    n = QUARTERS * R
    shares = w_sh if isinstance(w_sh, tuple) else (w_sh,)
    outs = [sds((n, w), BF16), sds((n, 896), BF16), sds((n, 128), F32), sds((n, 384), BF16)]
    if len(shares) > 1:
        outs = [sds((w, 512), BF16)] + outs
    return call(
        functools.partial(input_kernel, first, depth),
        "project_in",
        [SCALAR, SCALAR] + [whole((R, w))] * 4 + [whole((8, w)), whole((w, 1024))]
        + [whole(v.shape) for v in shares],
        outs,
        2 * n * w * 1536,
    )(rank, oh, *pieces, gain, w_in, *shares)


def input_back_kernel(da, ds, w_in, w_sh, send, keep):
    dh = (dot_nt(da[...], w_in[...]) + dot_nt(ds[...], w_sh[...])).astype(BF16)
    send[...] = dh[0 : 2 * R]
    keep[...] = dh[2 * R :]


def project_in_back(da, ds, w_in, w_sh, deps=()):
    n, w = da.shape[0], w_in.shape[0]
    return call(
        input_back_kernel,
        "project_in_back",
        [whole((n, 1024)), whole((n, 512)), whole((w, 1024)), whole((w, 512))],
        [sds((2 * R, w), BF16)] * 2,
        2 * n * w * 1536,
        deps=deps,
    )(da, ds, w_in, w_sh)


def column(row_ref, start):
    row = row_ref[:, pl.ds(pl.multiple_of(start, R), R)]
    return jnp.broadcast_to(row, (R, R)).T


def mix_kernel(half, rank, o, y, pa, fac, gain, w_mix, m_o, send, keep):
    m_o[:, 0:128] = o[...]
    for j in range(QUARTERS):
        rows = slice(j * R, (j + 1) * R)
        f = column(fac, half * QUARTERS * R + (rank[0] ^ DISTANCE[j]) * R)
        for p in range(3):
            z = pa[rows, 128 + 128 * p : 256 + 128 * p].astype(F32)
            u = y[rows, 128 * p : 128 * p + 128].astype(F32) * (z * jax.nn.sigmoid(z))
            m_o[rows, 128 + 128 * p : 256 + 128 * p] = (
                u * f * gain[0:1, 128 * p : 128 * p + 128]
            ).astype(BF16)
    mixed = dot_nt(m_o[...], w_mix[...]).astype(BF16)
    send[...] = mixed[0 : 2 * R]
    keep[...] = mixed[2 * R :]


def mix(half, rank, o, y, pa, fac, gain, w_mix):
    n, w = y.shape[0], w_mix.shape[0]
    return call(
        functools.partial(mix_kernel, half),
        "mix",
        [
            SCALAR, whole((n, 128)), whole((n, 384)), whole((n, 512)), whole(fac.shape),
            whole((8, 384)), whole((w, 512), 0, 2),
        ],
        [sds((n, 512), BF16), sds((2 * R, w), BF16), sds((2 * R, w), BF16)],
        2 * n * w * 512,
    )(rank, o, y, pa, fac, gain, w_mix)


def mix_back_kernel(rank, p0, p1, p2, p3, y, pa, gain, w_mix, dm_o, do_o, dyn_o, cross_o):
    dm = jnp.concatenate([p0[...], p1[...], p2[...], p3[...]], axis=0)
    dm_o[...] = dm
    d = dot_nn(dm, w_mix[...])
    do_o[...] = d[:, 0:128].astype(BF16)
    dyn_o[...] = d[:, 128:512]
    ones = jnp.ones((8, R), F32)
    for j in range(QUARTERS):
        rows = slice(j * R, (j + 1) * R)
        total = jnp.zeros((R, R), F32)
        for p in range(3):
            z = pa[rows, 128 + 128 * p : 256 + 128 * p].astype(F32)
            u = y[rows, 128 * p : 128 * p + 128].astype(F32) * (z * jax.nn.sigmoid(z))
            total = total + d[rows, 128 + 128 * p : 256 + 128 * p] * u * (
                gain[0:1, 128 * p : 128 * p + 128]
            )
        at = pl.multiple_of((rank[0] ^ DISTANCE[j]) * R, R)
        cross_o[:, pl.ds(at, R)] = dot_nt(ones, total, precision=EXACT)[0:1]


def mix_back(rank, pieces, y, pa, gain, w_mix):
    n, w = y.shape[0], w_mix.shape[0]
    return call(
        mix_back_kernel,
        "mix_back",
        [SCALAR] + [whole((R, w))] * 4
        + [whole((n, 384)), whole((n, 512)), whole((8, 384)), whole((w, 512), 0, 2)],
        [sds((n, w), BF16), sds((n, 128), BF16), sds((n, 384), F32), sds((1, n), F32)],
        2 * n * w * 512,
    )(rank, *pieces, y, pa, gain, w_mix)


def ffn_kernel(p0, p1, p2, p3, w_gu, w_dn, h_o, gu_o, act_o, send, keep):
    h = jnp.concatenate([p0[...], p1[...], p2[...], p3[...]], axis=0)
    h_o[...] = h
    gu = dot_nn(h, w_gu[...])
    gu_o[...] = gu.astype(BF16)
    g0 = gu[:, 0:512]
    act = (g0 * jax.nn.sigmoid(g0) * gu[:, 512:1024]).astype(BF16)
    act_o[...] = act
    out = dot_nt(act, w_dn[...]).astype(BF16)
    send[...] = out[0 : 2 * R]
    keep[...] = out[2 * R :]


def ffn(pieces, w_second):
    n, w = QUARTERS * R, pieces[0].shape[1]
    return call(
        ffn_kernel,
        "ffn",
        [whole((R, w))] * 4 + [whole((w, 1024)), whole((w, 512), 0, 2)],
        [
            sds((n, w), BF16), sds((n, 1024), BF16), sds((n, 512), BF16),
            sds((2 * R, w), BF16), sds((2 * R, w), BF16),
        ],
        2 * n * w * 1536,
    )(*pieces, w_second, w_second)


def ffn_back_kernel(p0, p1, p2, p3, gu, w_gu, w_dn, df_o, dgu_o, send, keep):
    df = jnp.concatenate([p0[...], p1[...], p2[...], p3[...]], axis=0)
    df_o[...] = df
    da = dot_nn(df, w_dn[...])
    g0, g1 = gu[:, 0:512].astype(F32), gu[:, 512:1024].astype(F32)
    sg = jax.nn.sigmoid(g0)
    dgu_o[:, 0:512] = (da * g1 * sg * (1.0 + g0 * (1.0 - sg))).astype(BF16)
    dgu_o[:, 512:1024] = (da * g0 * sg).astype(BF16)
    out = dot_nt(dgu_o[...], w_gu[...]).astype(BF16)
    send[...] = out[0 : 2 * R]
    keep[...] = out[2 * R :]


def ffn_back(pieces, gu, w_second, deps=()):
    n, w = QUARTERS * R, pieces[0].shape[1]
    return call(
        ffn_back_kernel,
        "ffn_back",
        [whole((R, w))] * 4 + [whole((n, 1024)), whole((w, 1024)), whole((w, 512), 0, 2)],
        [sds((n, w), BF16), sds((n, 1024), BF16), sds((2 * R, w), BF16), sds((2 * R, w), BF16)],
        2 * n * w * 1536,
        deps=deps,
    )(*pieces, gu, w_second, w_second)


def weight_grad_kernel(widths, *refs):
    out = refs[-1]
    at = 0
    for i, width in enumerate(widths):
        la, lb, ra, rb = refs[4 * i : 4 * i + 4]
        g = dot_tn(la[...], ra[...]) + dot_tn(lb[...], rb[...])
        out[:, at : at + width] = g.astype(BF16)
        at += width


def weight_grads(name, groups, deps=()):
    n, w = groups[0][0][0].shape
    widths = [right[0].shape[1] for _, right in groups]
    specs, args = [], []
    for (la, lb), (ra, rb) in groups:
        specs += [whole(la.shape)] * 2 + [whole(ra.shape)] * 2
        args += [la, lb, ra, rb]
    return call(
        functools.partial(weight_grad_kernel, widths),
        name,
        specs,
        [sds((w, sum(widths)), BF16)],
        4 * n * w * sum(widths),
        deps=deps,
    )(*args)[0]


def chunk_terms(act, raw_step, tok, seg_row, par):
    row, lane = iota((R, R), 0), iota((R, R), 1)
    b, c = act[:, 384:512], act[:, 512:640]
    bb, cb = b.astype(BF16), c.astype(BF16)
    dt = softplus(raw_step + par[1:2])
    tri = (row >= lane).astype(F32)
    cum = dot_nn(tri, dt * par[0:1], precision=EXACT)
    last = cum[R - 1 : R]
    okay = (row >= lane) & (tok[:, 5:6] == seg_row)
    inner = jnp.where(okay, dot_nt(cb, bb), 0.0)
    enter = jnp.exp(cum) * tok[:, 3:4]
    tail = jnp.exp(jnp.minimum(last - cum, 0.0)) * tok[:, 4:5]
    return b, c, bb, cb, dt, cum, cum.T, dt.T, okay, inner, enter, tail


def ssm_fwd_chunk(pa, raw, ps, tok, seg_row, cos, sin, taps, par, skip, y_o, pre_o, st_o, q_o, kv_o, state, hist):
    lane = iota((R, R), 1)
    half = lane < PH
    xin = jnp.concatenate([pa[:, 512:896], ps[:, 128:384]], axis=1).astype(F32)
    ext = jnp.concatenate([hist[...], xin], axis=0)
    hist[...] = xin[R - 8 :]
    pre = taps[4:5] + xin * taps[3:4]
    for k in (1, 2, 3):
        pre = pre + ext[8 - k : 8 - k + R] * tok[:, k - 1 : k] * taps[3 - k : 4 - k]
    pre_o[...] = pre.astype(BF16)
    act = pre * jax.nn.sigmoid(pre)
    b, c, bb, cb, dt, cum, cum_t, dt_t, okay, inner, enter, tail = chunk_terms(
        act, raw[...], tok, seg_row, par
    )
    tail = tail * dt
    keep = enter[R - 1 : R]
    b_t = b.T.astype(BF16)
    squares = jnp.zeros((R, R), F32)
    for p in range(3):
        h0, h1 = 2 * p, 2 * p + 1
        cols = slice(128 * p, 128 * p + 128)
        xp = act[:, cols]
        xb = xp.astype(BF16)
        sp = state[:, cols]
        st_o[:, cols] = sp.astype(BF16)

        def weights(h):
            gap = jnp.minimum(cum[:, h : h + 1] - cum_t[h : h + 1], 0.0)
            return (inner * jnp.exp(gap) * dt_t[h : h + 1]).astype(BF16)

        y = jnp.where(half, dot_nn(weights(h0), xb), dot_nn(weights(h1), xb))
        y = y + dot_nn(cb, sp.astype(BF16)) * jnp.where(
            half, enter[:, h0 : h0 + 1], enter[:, h1 : h1 + 1]
        )
        y = y + skip[0:1, cols] * xp
        y_o[:, cols] = y.astype(BF16)
        tp = jnp.where(half, tail[:, h0 : h0 + 1], tail[:, h1 : h1 + 1])
        kp = jnp.where(half[0:1], keep[:, h0 : h0 + 1], keep[:, h1 : h1 + 1])
        state[:, cols] = kp * sp + dot_nn(b_t, (tp * xp).astype(BF16))
        z = pa[:, 128 + 128 * p : 256 + 128 * p].astype(F32)
        u = y * z * jax.nn.sigmoid(z)
        squares = squares + u * u
    q = pa[:, 0:128].astype(F32)
    q_o[...] = (q * cos + partner(q, lane) * sin).astype(BF16)
    kv = ps[:, 0:128].astype(F32)
    kv_o[...] = jnp.where(half, kv * cos + partner(kv, lane) * sin, kv).astype(BF16)
    return dot_nt(jnp.ones((8, R), F32), squares, precision=EXACT)[0:1]


def ssm_fwd_kernel(
    rank, pa0, pa1, raw0, raw1, ps0, ps1, tok_r, seg_r, cos_r, sin_r, taps, par, skip,
    y0, y1, pre0, pre1, st_o, sq_o, q_o, kv_o, state, hist,
):
    i = pl.program_id(0)

    @pl.when(i == 0)
    def _():
        state[...] = jnp.zeros_like(state)
        hist[...] = jnp.zeros_like(hist)

    halves = ((pa0, raw0, ps0, y0, pre0), (pa1, raw1, ps1, y1, pre1))
    for half, (pa, raw, ps, y_o, pre_o) in enumerate(halves):
        rows = slice(half * R, (half + 1) * R)
        at = pl.multiple_of(half * QUARTERS * R + i * R, R)
        sq_o[:, pl.ds(at, R)] = ssm_fwd_chunk(
            pa, raw, ps, tok_r[rows], seg_r[0:1, rows], cos_r[rows], sin_r[rows], taps, par, skip,
            y_o, pre_o, st_o.at[half], q_o.at[rows], kv_o.at[rows], state, hist,
        )


def wire(width, reverse=False):
    def at(i, rank):
        i = QUARTERS - 1 - i if reverse else i
        return (block_of(i, rank[0]), 0)

    return pl.BlockSpec((R, width), at)


def in_order(shape, dim=0, reverse=False):
    def at(i, rank):
        i = QUARTERS - 1 - i if reverse else i
        return tuple(i if d == dim else 0 for d in range(len(shape)))

    return pl.BlockSpec(shape, at)


def ssm_forward(rank, pa, raw, ps, tok, seg_rows, cos, sin, taps, par, skip):
    n = QUARTERS * R
    t = 2 * n
    return pl.pallas_call(
        ssm_fwd_kernel,
        grid_spec=pltpu.PrefetchScalarGridSpec(
            num_scalar_prefetch=1,
            grid=(QUARTERS,),
            in_specs=[
                wire(896), wire(896), wire(128), wire(128), wire(384), wire(384),
                in_order((2 * R, 8)), in_order((8, 2 * R), 1),
                in_order((2 * R, 128)), in_order((2 * R, 128)), whole((8, 640)), whole((8, 128)), whole((8, 384)),
            ],
            out_specs=[
                wire(384), wire(384), wire(640), wire(640), in_order((2, NS, 384)), whole((1, t)),
                in_order((2 * R, 128)), in_order((2 * R, 128)),
            ],
            scratch_shapes=[pltpu.VMEM((NS, 384), F32), pltpu.VMEM((8, 640), F32)],
        ),
        out_shape=[
            sds((n, 384), BF16), sds((n, 384), BF16), sds((n, 640), BF16), sds((n, 640), BF16),
            sds((2 * QUARTERS, NS, 384), BF16), sds((1, t), F32), sds((t, 128), BF16), sds((t, 128), BF16),
        ],
        compiler_params=pltpu.CompilerParams(
            dimension_semantics=("arbitrary",), vmem_limit_bytes=VMEM_BYTES
        ),
        cost_estimate=pl.CostEstimate(
            flops=4 * 10**9, bytes_accessed=20 * 2**20, transcendentals=3 * 10**6
        ),
        name="ssm_forward",
    )(rank, *pa, *raw, *ps, tok, seg_rows, cos, sin, taps, par, skip)


def ssm_bwd_chunk(
    pa, raw, ps, pre_r, y_r, st_r, dyn_r, r2, coef, dq, dkv, tok, seg_row, taps, par, skip, gain,
    da_o, ds_o, gt_o, gc_o, gh_o, dstate, nxt, own_first,
):
    row, lane = iota((R, R), 0), iota((R, R), 1)
    half = lane < PH
    sub = iota((8, R), 0)
    pre = pre_r[...].astype(F32)
    sg = jax.nn.sigmoid(pre)
    act = pre * sg
    b, c, bb, cb, dt, cum, cum_t, dt_t, okay, inner, enter, tail = chunk_terms(
        act, raw[...], tok, seg_row, par
    )
    tail_dt = tail * dt
    keep = enter[R - 1 : R]
    c_t = c.T.astype(BF16)
    db = jnp.zeros((R, R), F32)
    dc = jnp.zeros((R, R), F32)
    dinner = jnp.zeros((R, R), F32)
    dcum = jnp.zeros((R, R), F32)
    extra = jnp.zeros((R, R), F32)
    col_sum = jnp.zeros((8, R), F32)
    last_row = jnp.zeros((1, R), F32)
    dx_parts = []
    for p in range(3):
        cols = slice(128 * p, 128 * p + 128)
        z = pa[:, 128 + 128 * p : 256 + 128 * p].astype(F32)
        y, dyn = y_r[:, cols].astype(F32), dyn_r[:, cols]
        zs = jax.nn.sigmoid(z)
        sz = z * zs
        u = y * sz
        dn = dyn * r2
        gc_o[0:1, cols] += jnp.sum(dn * u, axis=0, keepdims=True)
        du = gain[0:1, cols] * dn - u * coef
        da_o[:, 128 + 128 * p : 256 + 128 * p] = (
            du * y * zs * (1.0 + z * (1.0 - zs))
        ).astype(BF16)
        dy = du * sz
        dyb = dy.astype(BF16)
        xp = act[:, cols]
        xb = xp.astype(BF16)
        gc_o[1:2, cols] += jnp.sum(dy * xp, axis=0, keepdims=True)
        sb = st_r[:, cols]
        sp = sb.astype(F32)
        dsp = dstate[:, cols]
        dsb = dsp.astype(BF16)
        h0, h1 = 2 * p, 2 * p + 1
        ep = jnp.where(half, enter[:, h0 : h0 + 1], enter[:, h1 : h1 + 1])
        tp = jnp.where(half, tail_dt[:, h0 : h0 + 1], tail_dt[:, h1 : h1 + 1])
        kp = jnp.where(half[0:1], keep[:, h0 : h0 + 1], keep[:, h1 : h1 + 1])
        cdb = (ep * dy).astype(BF16)
        through = dy * ep * dot_nn(cb, sb)
        bds = dot_nn(bb, dsb)
        qx = xp * bds
        kept = jnp.sum(dsp * sp, axis=0, keepdims=True) * kp
        dxi = []
        for h in (h0, h1):
            mine = half if h == h0 else ~half
            gap = jnp.minimum(cum[:, h : h + 1] - cum_t[h : h + 1], 0.0)
            decay = jnp.where(okay, jnp.exp(gap), 0.0)
            dt_row = dt_t[h : h + 1]
            dg = dot_nt(jnp.where(mine, dy, 0.0).astype(BF16), xb)
            t1 = dg * decay
            dinner = dinner + t1 * dt_row
            w0 = t1 * inner
            col_sum = col_sum + jnp.where(sub == h, jnp.sum(w0, axis=0, keepdims=True), 0.0)
            w1 = w0 * dt_row + jnp.where(mine, through, 0.0)
            dcum = dcum + jnp.where(lane == h, jnp.sum(w1, axis=1, keepdims=True), 0.0)
            e = jnp.sum(jnp.where(mine, qx, 0.0), axis=1, keepdims=True)
            extra = extra + jnp.where(lane == h, e, 0.0)
            k = jnp.sum(jnp.where(mine[0:1], kept, 0.0), axis=1, keepdims=True)
            last_row = last_row + jnp.where(lane[0:1] == h, k, 0.0)
            dxi.append(dot_tn((decay * inner * dt_row).astype(BF16), dyb))
        dx_parts.append(jnp.where(half, dxi[0], dxi[1]) + tp * bds + skip[0:1, cols] * dy)
        dc = dc + dot_nt(cdb, sb)
        db = db + dot_nt((tp * xp).astype(BF16), dsb)
        dstate[:, cols] = kp * dsp + dot_nn(c_t, cdb)
    col_sum = jnp.concatenate([col_sum, jnp.zeros((R - 8, R), F32)], axis=0).T
    moved = tail_dt * extra
    last_row = last_row + jnp.sum(moved, axis=0, keepdims=True)
    dcum = dcum - col_sum * dt - moved + jnp.where(row == R - 1, last_row, 0.0)
    dlog = dot_nn((row <= lane).astype(F32), dcum, precision=EXACT)
    ddt = col_sum + tail * extra + par[0:1] * dlog
    gh_o[0:1] += jnp.sum(dt * dlog, axis=0, keepdims=True)
    ddr = ddt * jax.nn.sigmoid(raw[...] + par[1:2])
    gh_o[1:2] += jnp.sum(ddr, axis=0, keepdims=True)
    da_o[:, 896:1024] = ddr.astype(BF16)
    dib = dinner.astype(BF16)
    dc = dc + dot_nn(dib, bb)
    db = db + dot_tn(dib, cb)
    dact = jnp.concatenate([*dx_parts, db, dc], axis=1)
    dpre = dact * sg * (1.0 + pre * (1.0 - sg))
    xin = jnp.concatenate([pa[:, 512:896], ps[:, 128:384]], axis=1).astype(F32)
    dxin = dpre * taps[3:4]
    gt_o[3:4] += jnp.sum(dpre * xin, axis=0, keepdims=True)
    gt_o[4:5] += jnp.sum(dpre, axis=0, keepdims=True)
    for k in (1, 2, 3):
        zk = dpre * tok[:, k - 1 : k]
        later = nxt.at[k - 1]
        moved_up = jnp.concatenate([zk, later[...]], axis=0)[k : k + R]
        later[...] = zk[0:8]
        dxin = dxin + moved_up * taps[3 - k : 4 - k]
        gt_o[3 - k : 4 - k] += jnp.sum(moved_up * xin, axis=0, keepdims=True)
    da_o[:, 512:896] = dxin[:, 0:384].astype(BF16)
    ds_o[:, 256:512] = dxin[:, 384:640].astype(BF16)
    da_o[:, 0:128] = dq
    other = pltpu.roll(dkv, HD, 1)
    mine = half == own_first
    ds_o[:, 0:128] = jnp.where(mine, jnp.where(half, dkv, other), 0.0).astype(BF16)
    ds_o[:, 128:256] = jnp.where(mine, jnp.where(half, other, dkv), 0.0).astype(BF16)


def ssm_bwd_kernel(
    rank, oh, pa0, pa1, raw0, raw1, ps0, ps1, pre0, pre1, y0, y1, st_r, dyn0, dyn1, fac_r, coef_r, dq_r, dkv_r,
    tok_r, seg_r, taps, par, skip, gain,
    da0, da1, ds0, ds1, gt_o, gc_o, gh_o, dstate, nxt,
):
    i = pl.program_id(0)

    @pl.when(i == 0)
    def _():
        dstate[...] = jnp.zeros_like(dstate)
        nxt[...] = jnp.zeros_like(nxt)
        gt_o[...] = jnp.zeros_like(gt_o)
        gc_o[...] = jnp.zeros_like(gc_o)
        gh_o[...] = jnp.zeros_like(gh_o)

    quarter = QUARTERS - 1 - i
    halves = (
        (pa0, raw0, ps0, pre0, y0, dyn0, da0, ds0),
        (pa1, raw1, ps1, pre1, y1, dyn1, da1, ds1),
    )
    for half in (1, 0):
        pa, raw, ps, pre, y, dyn, da, ds = halves[half]
        rows = slice(half * R, (half + 1) * R)
        start = half * QUARTERS * R + quarter * R
        ssm_bwd_chunk(
            pa, raw, ps, pre, y, st_r.at[half], dyn, column(fac_r, start), column(coef_r, start),
            dq_r[rows], dkv_r[rows].astype(F32), tok_r[rows], seg_r[0:1, rows], taps, par, skip, gain,
            da, ds, gt_o, gc_o, gh_o, dstate, nxt, oh[0] == 0,
        )


def ssm_backward(
    rank, oh, pa, raw, ps, pre, y, states, dyn, fac, coef, dq, dkv, tok, seg_rows, taps, par, skip, gain
):
    n = QUARTERS * R
    t = 2 * n
    back = {"reverse": True}
    return pl.pallas_call(
        lambda r, *refs: ssm_bwd_kernel(r, *refs),
        grid_spec=pltpu.PrefetchScalarGridSpec(
            num_scalar_prefetch=1,
            grid=(QUARTERS,),
            in_specs=[
                SCALAR, wire(896, **back), wire(896, **back), wire(128, **back), wire(128, **back),
                wire(384, **back), wire(384, **back),
                wire(640, **back), wire(640, **back), wire(384, **back), wire(384, **back),
                in_order((2, NS, 384), **back), wire(384, **back), wire(384, **back),
                whole((1, t)), whole((1, t)), in_order((2 * R, 128), **back), in_order((2 * R, 128), **back),
                in_order((2 * R, 8), **back), in_order((8, 2 * R), 1, **back),
                whole((8, 640)), whole((8, 128)), whole((8, 384)), whole((8, 384)),
            ],
            out_specs=[
                wire(1024, **back), wire(1024, **back), wire(512, **back), wire(512, **back),
                whole((8, 640)), whole((8, 384)), whole((8, 128)),
            ],
            scratch_shapes=[pltpu.VMEM((NS, 384), F32), pltpu.VMEM((3, 8, 640), F32)],
        ),
        out_shape=[
            sds((n, 1024), BF16), sds((n, 1024), BF16), sds((n, 512), BF16), sds((n, 512), BF16),
            sds((8, 640), F32), sds((8, 384), F32), sds((8, 128), F32),
        ],
        compiler_params=pltpu.CompilerParams(
            dimension_semantics=("arbitrary",), vmem_limit_bytes=VMEM_BYTES
        ),
        cost_estimate=pl.CostEstimate(
            flops=8 * 10**9, bytes_accessed=30 * 2**20, transcendentals=4 * 10**6
        ),
        name="ssm_backward",
    )(
        rank, oh, *pa, *raw, *ps, *pre, *y, states, *dyn, fac, coef, dq, dkv, tok, seg_rows, taps, par, skip, gain
    )


def head_views(kv, lane):
    zero = jnp.zeros_like(kv)
    left = lane < HD
    k0 = jnp.where(left, kv, zero)
    v1 = jnp.where(left, zero, kv)
    k1 = pltpu.roll(k0.astype(F32), HD, 1).astype(BF16)
    v0 = pltpu.roll(v1.astype(F32), HD, 1).astype(BF16)
    return (k0, k1), (v0, v1)


def allowed_keys(tok_r, seg_r, start, rows, keys):
    return (iota((rows, keys), 1) <= start + iota((rows, keys), 0)) & (
        tok_r[start : start + rows, 5:6] == seg_r[0:1, 0:keys]
    )


def attend_fwd_kernel(rank, q_r, kv_r, tok_r, seg_r, o0, o1, lse_o):
    n = q_r.shape[0]
    ks, vs = head_views(kv_r[...], iota((n, 2 * HD), 1))
    lane = iota((2 * R, 128), 1)
    for quarter in range(QUARTERS):
        start, keys = quarter * 2 * R, (quarter + 1) * 2 * R
        q = q_r[start:keys]
        okay = allowed_keys(tok_r, seg_r, start, 2 * R, keys)
        out = jnp.zeros((2 * R, 2 * HD), F32)
        stats = []
        for h in range(2):
            s = jnp.where(okay, dot_nt(q, ks[h][0:keys]) * HD**-0.5, NEG)
            top = jnp.max(s, axis=1, keepdims=True)
            e = jnp.exp(s - top)
            total = jnp.sum(e, axis=1, keepdims=True)
            out = out + dot_nn((e * (1.0 / total)).astype(BF16), vs[h][0:keys])
            stats.append(top + jnp.log(total))
        at = pl.ds(pl.multiple_of(block_of(quarter, rank[0]) * R, R), R)
        o0[at] = out[0:R].astype(BF16)
        o1[at] = out[R:].astype(BF16)
        lse_o[start:keys] = jnp.where(lane == 0, stats[0], stats[1])


def attend_bwd_kernel(
    rank, q_r, kv_r, do0, do1, lse_r, tok_r, seg_r, cos_r, sin_r, dq_o, dkv_o, dk_acc, dv_acc
):
    n = q_r.shape[0]
    ks, vs = head_views(kv_r[...], iota((n, 2 * HD), 1))
    lane = iota((2 * R, 128), 1)
    left = lane < HD
    dk_acc[...] = jnp.zeros_like(dk_acc)
    dv_acc[...] = jnp.zeros_like(dv_acc)
    for quarter in range(QUARTERS):
        start, keys = quarter * 2 * R, (quarter + 1) * 2 * R
        q = q_r[start:keys]
        at = pl.ds(pl.multiple_of(block_of(quarter, rank[0]) * R, R), R)
        do = jnp.concatenate([do0[at], do1[at]], axis=0)
        okay = allowed_keys(tok_r, seg_r, start, 2 * R, keys)
        lse = lse_r[start:keys]
        zero = jnp.zeros_like(q)
        dq = jnp.zeros((2 * R, 2 * HD), F32)
        for h in range(2):
            mine = left if h == 0 else ~left
            s = dot_nt(q, ks[h][0:keys]) * HD**-0.5
            p = jnp.where(okay, jnp.exp(s - lse[:, h : h + 1]), 0.0)
            dp = dot_nt(do, vs[h][0:keys])
            dot_sum = jnp.sum(p * dp, axis=1, keepdims=True)
            ds = (p * (dp - dot_sum)).astype(BF16)
            dq = dq + dot_nn(ds, ks[h][0:keys])
            dk_acc[0:keys] += dot_tn(ds, jnp.where(mine, q, zero))
            dv_acc[0:keys] += dot_tn(p.astype(BF16), jnp.where(mine, do, zero))
        dq = dq * HD**-0.5
        dq_o[start:keys] = (
            dq * cos_r[start:keys] - partner(dq, lane) * sin_r[start:keys]
        ).astype(BF16)
    for start in range(0, n, 2 * R):
        rows = slice(start, start + 2 * R)
        dk, dv = dk_acc[rows], dv_acc[rows]
        dk = (dk + pltpu.roll(dk, HD, 1)) * HD**-0.5
        dv = dv + pltpu.roll(dv, HD, 1)
        dk = dk * cos_r[rows] - partner(dk, lane) * sin_r[rows]
        dkv_o[rows] = jnp.where(left, dk, dv).astype(BF16)


def attend_forward(rank, q, kv, tok, seg_rows):
    t = q.shape[0]
    return call(
        attend_fwd_kernel,
        "attend_forward",
        [SCALAR, whole((t, 128)), whole((t, 128)), whole((t, 8)), whole((8, t))],
        [sds((t // 2, 128), BF16), sds((t // 2, 128), BF16), sds((t, 128), F32)],
        2 * 10**9,
    )(rank, q, kv, tok, seg_rows)


def attend_backward(rank, q, kv, do, lse, tok, seg_rows, cos, sin, deps=()):
    t = q.shape[0]
    full = whole((t, 128))
    return call(
        attend_bwd_kernel,
        "attend_backward",
        [SCALAR, full, full, whole((t // 2, 128)), whole((t // 2, 128)), full,
         whole((t, 8)), whole((8, t)), full, full],
        [sds((t, 128), BF16), sds((t, 128), BF16)],
        4 * 10**9,
        [pltpu.VMEM((t, 128), F32), pltpu.VMEM((t, 128), F32)],
        deps,
    )(rank, q, kv, *do, lse, tok, seg_rows, cos, sin)


def swap(values, axis, distance):
    size = lax.axis_size(axis)
    return lax.ppermute(values, axis, [(i, i ^ distance) for i in range(size)])


def bits_of(axis):
    size = lax.axis_size(axis)
    return [1 << b for b in range(size.bit_length() - 1)]


def sum_over(values, axes):
    for axis in axes:
        for bit in bits_of(axis):
            values = values + swap(values, axis, bit)
    return values


def sum_rows(values):
    return values + sum(swap(values, "tensor", d) for d in (1, 2, 3))


def gather_half(own):
    far = swap(own, "tensor", 2)
    near = swap(own, "tensor", 1)
    return near, swap(far, "tensor", 1), own, far


def scatter_half(send, keep):
    got = swap(send, "tensor", 1)
    far = swap((keep[R:].astype(F32) + got[R:].astype(F32)).astype(BF16), "tensor", 2)
    return keep, got, far


def gather_everywhere(own):
    held = own[:, None]
    for axis in ("dp", "tensor"):
        place = lax.axis_index(axis)
        for bit in bits_of(axis):
            upper = (place & bit) != 0
            other = swap(held, axis, bit)
            low, high = jnp.where(upper, other, held), jnp.where(upper, held, other)
            held = jnp.concatenate([low, high], axis=0 if axis == "dp" else 1)
    return held.reshape(-1, *own.shape[1:])


def gather_dp(v):
    return lax.all_gather(v, "dp", axis=0, tiled=True)


def scatter_dp(v):
    return lax.psum_scatter(v, "dp", scatter_dimension=0, tiled=True)


def pad_rows(v, rows=8):
    return jnp.pad(v, ((0, rows - v.shape[0]), (0, 0)))


def body(
    inputs, cotangent, segment_ids, norm_gains, w_query, key_value_weight, w_gate_in, w_state_in,
    w_step, ssm_channel, conv_state, head_params, w_attn_out, w_ssm_out, w_gate_up, w_down,
):
    width = inputs.shape[2]
    n = segment_ids.shape[1]
    tp_size = lax.axis_size("tensor")
    tensor = lax.axis_index("tensor")
    slot = lax.axis_index("dp") * tp_size + tensor
    kv_cols = key_value_weight.shape[2]
    kv_heads = kv_cols // (2 * HD)
    own_head = tensor * (w_query.shape[2] // HD) // (HQ // kv_heads)
    ssm_heads = w_step.shape[2]
    channels = ssm_heads * PH
    hidden = w_gate_up.shape[3]
    depth = w_query.shape[1]
    rank = tensor.reshape(1).astype(jnp.int32)
    oh = own_head.reshape(1).astype(jnp.int32)

    halves = [inputs[0, :R], inputs[0, R:]]
    x_pieces = [gather_half(v) for v in halves]

    shared = jnp.concatenate([key_value_weight, w_state_in], axis=2)
    sq, wide = shared.shape[1:]
    shares = [
        shared[layer].reshape(sq, wide // 128, 128).swapaxes(0, 1).reshape(depth, 128)
        for layer in range(LAYERS)
    ]

    def exchange(share):
        far = swap(share, "tensor", 2)
        return share, swap(share, "tensor", 1), far, swap(far, "tensor", 1)

    w_first, w_second, w_shared = [], [], []
    for layer in range(LAYERS):
        first = [
            w_query[layer],
            w_gate_in[layer].reshape(depth, 2 * channels),
            jnp.pad(w_step[layer], ((0, 0), (0, 128 - ssm_heads))),
            w_attn_out[layer].T,
            w_ssm_out[layer].T,
        ]
        second = [w_gate_up[layer].reshape(depth, 2 * hidden), w_down[layer].T]
        first = gather_dp(jnp.concatenate(first + (shares if layer == 0 else []), axis=1))
        if layer == 0:
            w_shared = [exchange(first[:, c : c + 128]) for c in range(1536, 1536 + 128 * LAYERS, 128)]
        w_first.append(first)
        w_second.append(gather_dp(jnp.concatenate(second, axis=1)))

    small = jnp.concatenate([norm_gains.reshape(-1), conv_state.reshape(-1)])[None, :]
    small_all = gather_everywhere(small).astype(F32)
    gain_count = norm_gains.size
    gains = (
        small_all[:, :gain_count]
        .reshape(-1, LAYERS, 2, norm_gains.shape[2])
        .transpose(1, 2, 0, 3)
        .reshape(LAYERS, 2, width)
    )
    conv_flat = (
        small_all[:, gain_count : gain_count + conv_state.size]
        .reshape(-1, LAYERS, conv_state.shape[1])
        .transpose(1, 0, 2)
        .reshape(LAYERS, 5, 2 * NS)
    )

    seg = segment_ids[0]
    segf = seg.astype(F32)
    index = jnp.arange(n, dtype=jnp.int32)
    places = index - jnp.sum((seg[None, :] < seg[:, None]).astype(jnp.int32), axis=1)
    freq = ROPE_BASE ** (-jnp.arange(HD // 2, dtype=F32) / (HD // 2))
    angle = places.astype(F32)[:, None] * freq[None, :]
    cos_one, sin_one = jnp.cos(angle), jnp.sin(angle)
    cos = jnp.concatenate([cos_one] * 4, axis=1)
    sin = jnp.concatenate([-sin_one, sin_one] * 2, axis=1)
    shifted = [
        (jnp.pad(seg, (k, 0), constant_values=-1)[:n] == seg).astype(F32) for k in (1, 2, 3)
    ]
    ends = seg.reshape(-1, R)[:, -1]
    before = jnp.concatenate([jnp.full((1,), -1, jnp.int32), ends[:-1]])
    enters = (seg.reshape(-1, R) == before[:, None]).astype(F32).reshape(-1)
    leaves = (seg.reshape(-1, R) == ends[:, None]).astype(F32).reshape(-1)
    tok = jnp.stack([*shifted, enters, leaves, segf, segf, segf], axis=1)
    seg_rows = jnp.broadcast_to(segf[None, :], (8, n))

    residual = halves
    pieces = x_pieces
    saved = []
    for layer in range(LAYERS):
        channel, head = ssm_channel[layer], head_params[layer]
        taps = pad_rows(jnp.concatenate([channel[:5], conv_flat[layer]], axis=1))
        rate = -jnp.exp(head[0])
        par = pad_rows(jnp.pad(jnp.stack([rate, head[1]]), ((0, 0), (0, 128 - ssm_heads))))
        skip = pad_rows(jnp.repeat(head[2], PH)[None, :])
        gain_row = pad_rows(channel[5:6])
        gain_one = pad_rows(gains[layer, 0:1])
        gain_two = pad_rows(gains[layer, 1:2])
        wf, ws, wh = w_first[layer], w_second[layer], w_shared[layer]
        ins = functools.partial(project_in, layer == 0, depth, rank, oh)
        w_all, *half_0 = ins(pieces[0], gain_one, wf, wh)
        w_shared[layer] = w_all
        h, pa, raw, ps = zip(half_0, ins(pieces[1], gain_one, wf, w_all))
        y0, y1, pre0, pre1, states, sq, q_rot, kv_rot = ssm_forward(
            rank, pa, raw, ps, tok, seg_rows, cos, sin, taps, par, skip
        )
        y, pre = (y0, y1), (pre0, pre1)
        total = sum_rows(sq)
        o0, o1, lse = attend_forward(rank, q_rot, kv_rot, tok, seg_rows)
        factor = lax.rsqrt(total / (HS * PH) + EPS)
        mixed, middle, h2, gu, act, result, pieces = [], [], [], [], [], [], []
        parts = []
        for i, o in enumerate((o0, o1)):
            m, send, keep = mix(i, rank, o, y[i], pa[i], factor, gain_row, wf)
            mixed.append(m)
            parts.append(scatter_half(send, keep))
        gathered = []
        for i in range(2):
            x1, low = take_step(residual[i], *parts[i], gain_two)
            middle.append(x1)
            gathered.append(gather_half(low))
        parts = []
        for i in range(2):
            h2_i, gu_i, act_i, send, keep = ffn(gathered[i], ws)
            h2.append(h2_i)
            gu.append(gu_i)
            act.append(act_i)
            parts.append(scatter_half(send, keep))
        for i in range(2):
            if layer + 1 < LAYERS:
                x2, low = take_step(middle[i], *parts[i], pad_rows(gains[layer + 1, 0:1]))
                result.append(x2)
                pieces.append(gather_half(low))
            else:
                result.append(take_step(middle[i], *parts[i], None))
        saved.append(
            (residual, middle, h, pa, raw, ps, y, pre, states, q_rot, kv_rot, lse, factor, mixed, h2, gu, act,
             taps, par, skip, gain_row, gain_one, gain_two, rate)
        )
        residual = result
    output = jnp.concatenate(residual, axis=0)

    grad = [cotangent[0, :R], cotangent[0, R:]]
    low = list(grad)
    big, small_grads = [None] * LAYERS, [None] * LAYERS
    for layer in reversed(range(LAYERS)):
        (first_in, middle, h, pa, raw, ps, y, pre, states, q_rot, kv_rot, lse, factor, mixed, h2, gu, act,
         taps, par, skip, gain_row, gain_one, gain_two, rate) = saved[layer]
        wf, ws, wh = w_first[layer], w_second[layer], w_shared[layer]
        gathered = [gather_half(v) for v in low]
        df, dgu, dm, do, dyn, cross, parts = [], [], [], [], [], [], []
        deps = (big[layer + 1][0],) if layer + 1 < LAYERS else ()
        for i in range(2):
            df_i, dgu_i, send, keep = ffn_back(gathered[i], gu[i], ws, deps)
            df.append(df_i)
            dgu.append(dgu_i)
            parts.append(scatter_half(send, keep))
        g1 = weight_grads("grads_one", [(h2, dgu), (df, act)])
        gathered, dx1, dgain2, dgain1 = [], [], 0.0, 0.0
        for i in range(2):
            dx, low_i, gg = back_step(grad[i], middle[i], *parts[i], gain_two, () if i else (g1,))
            dx1.append(dx)
            dgain2 = dgain2 + gg[0]
            gathered.append(gather_half(low_i))
        for i in range(2):
            dm_i, do_i, dyn_i, cross_i = mix_back(rank, gathered[i], y[i], pa[i], gain_row, wf)
            dm.append(dm_i)
            do.append(do_i)
            dyn.append(dyn_i)
            cross.append(cross_i)
        cross = sum_rows(jnp.concatenate(cross, axis=1))
        dq, dkv = attend_backward(
            rank, q_rot, kv_rot, do, lse, tok, seg_rows, cos, sin
        )
        coef = factor**3 * cross / (HS * PH)
        da0, da1, ds0, ds1, g_taps, g_chan, g_head = ssm_backward(
            rank, oh, pa, raw, ps, pre, y, states, dyn, factor, coef, dq, dkv, tok, seg_rows, taps, par, skip,
            gain_row,
        )
        groups = [(h, (da0, da1)), (h, (ds0, ds1)), (dm, mixed)]
        deps = ()
        if layer == 0:
            g2 = weight_grads("grads_two", groups, (big[layer + 1][1],))
            deps = (g2,)
        sums = [project_in_back(da, ds, wf, wh, deps) for da, ds in ((da0, ds0), (da1, ds1))]
        parts = [scatter_half(*v) for v in sums]
        deps = ()
        if layer > 0:
            g2 = weight_grads("grads_two", groups, (sums[0][0], sums[1][0]))
            deps = (g2,)
        grad, low = [], []
        for i in range(2):
            g, low_i, gg = back_step(dx1[i], first_in[i], *parts[i], gain_one, () if i else deps)
            grad.append(g)
            low.append(low_i)
            dgain1 = dgain1 + gg[0]
        chan_grad = jnp.concatenate([g_taps[:5, :channels], g_chan[0:1]], axis=0)
        head_grad = jnp.stack(
            [
                g_head[0, :ssm_heads] * rate,
                g_head[1, :ssm_heads],
                jnp.sum(g_chan[1].reshape(ssm_heads, PH), axis=1),
            ]
        )
        big[layer] = (scatter_dp(g1), scatter_dp(g2))
        small_grads[layer] = (
            jnp.concatenate([dgain1, dgain2, g_taps[:5, channels:].reshape(-1)]),
            jnp.concatenate([chan_grad.reshape(-1), head_grad.reshape(-1)]),
        )
    input_grad = jnp.concatenate(grad, axis=0)

    wide_small = jnp.concatenate([small_grads[l][0] for l in range(LAYERS)])
    local_small = jnp.concatenate([small_grads[l][1] for l in range(LAYERS)])
    total = sum_over(jnp.concatenate([wide_small, local_small])[None, :], ("dp",))[0]
    wide_small = sum_over(total[None, : wide_small.shape[0]], ("tensor",))[0]
    wide_small = wide_small.reshape(LAYERS, -1)
    local_small = total[wide_small.size :].reshape(LAYERS, -1)
    gain_share = norm_gains.shape[2]
    conv_share = conv_state.shape[1]
    grad_gains = lax.dynamic_slice_in_dim(
        wide_small[:, : 2 * width].reshape(LAYERS, 2, width), slot * gain_share, gain_share, 2
    )
    grad_conv = lax.dynamic_slice_in_dim(wide_small[:, 2 * width :], slot * conv_share, conv_share, 1)
    grad_channel = local_small[:, : 6 * channels].reshape(LAYERS, 6, channels)
    grad_head = local_small[:, 6 * channels :].reshape(LAYERS, 3, ssm_heads)

    outs = {k: [] for k in ("q", "gate", "step", "attn", "ssm", "gu", "down", "kv", "state")}
    for layer in range(LAYERS):
        g1, g2 = (v.astype(F32) for v in big[layer])
        outs["gu"].append(g1[:, : 2 * hidden].reshape(depth, 2, hidden))
        outs["down"].append(g1[:, 2 * hidden : 3 * hidden].T)
        outs["attn"].append(g2[:, 1536:1664].T)
        outs["ssm"].append(g2[:, 1664:2048].T)
        outs["q"].append(g2[:, :128])
        outs["gate"].append(g2[:, 128 : 128 + 2 * channels].reshape(depth, 2, channels))
        outs["step"].append(g2[:, 896 : 896 + ssm_heads])
        sh = big[layer][1][:, 1024:1536]
        rows = sh.shape[0] // tp_size

        def part(distance):
            return lax.dynamic_slice_in_dim(sh, (tensor ^ distance) * rows, rows, 0).astype(F32)

        sh = part(0) + sum(swap(part(d), "tensor", d) for d in (1, 2, 3))
        outs["kv"].append(sh[:, :kv_cols])
        outs["state"].append(sh[:, kv_cols:])
    st = {k: jnp.stack(v) for k, v in outs.items()}
    return (
        output[None], input_grad[None], grad_gains, st["q"], st["kv"], st["gate"], st["state"],
        st["step"], grad_channel, grad_conv, grad_head, st["attn"], st["ssm"], st["gu"], st["down"],
    )


def solution(mesh):
    split = (
        P("dp", "tensor", None),
        P("dp", "tensor", None),
        P("dp", None),
        P(None, None, ("dp", "tensor")),
        P(None, "dp", "tensor"),
        P(None, ("dp", "tensor"), None),
        P(None, "dp", None, "tensor"),
        P(None, ("dp", "tensor"), None),
        P(None, "dp", "tensor"),
        P(None, None, "tensor"),
        P(None, ("dp", "tensor")),
        P(None, None, "tensor"),
        P(None, "tensor", "dp"),
        P(None, "tensor", "dp"),
        P(None, "dp", None, "tensor"),
        P(None, "tensor", "dp"),
    )
    out_split = split[:2] + split[3:]
    return jax.shard_map(body, mesh=mesh, in_specs=split, out_specs=out_split, check_vma=False)
```

time: 751 us -> 674 us (0.90)
  waiting for transfers between devices: 336 us -> 219 us
  Pallas kernels: 83 us -> 173 us
  matrix products: 76.6 us -> 0 us
  local copies, waits for them, and re-layouts: 98.9 us -> 141 us
  other arithmetic: 72.1 us -> 35.5 us
  starting transfers between devices: 56.2 us -> 77 us
    pallas_call x8 -> x52, Pallas kernels: 83 us -> 173 us  [the longest x48 107 us: call(): return lambda *args: made(*args, *deps)]
    dot_general x31 -> x0, matrix products: 76.6 us -> none  [the longest x10 31.4 us: dot_nn(): lax.dot_general(left, right, (((1,), (0,)), ((), ())), preferred_element_...]
    unnamed x12 -> x8, waiting for transfers between devices: 60.9 us -> 0.13 us
    unnamed x284 -> x593, local copies, waits for them, and re-layouts: 51.1 us -> 110 us
    ppermute x79 -> x114, waiting for transfers between devices: 190 us -> 132 us  [swap(): return lax.ppermute(values, axis, [(i, i ^ distance) for i in range(size)])]
    reduce_scatter x0 -> x4, waiting for transfers between devices: none -> 38.2 us  [scatter_dp(): return lax.psum_scatter(v, 'dp', scatter_dimension=0, tiled=True)]
    all_gather x4, waiting for transfers between devices: 84.7 us -> 48.1 us  [gather_dp(): return lax.all_gather(v, 'dp', axis=0, tiled=True)]
    ppermute x79 -> x114, starting transfers between devices: 55 us -> 76 us  [swap(): return lax.ppermute(values, axis, [(i, i ^ distance) for i in range(size)])]
  transfers between devices with their start and end apart: 87 -> 122, of which waited for: 38 -> 42; matrix products, arithmetic and copies ran while one was open for 29% -> 10% of each run, Pallas kernels for 11% -> 25%
where the time goes in v2:
time: 674 us; the launch traced here: 664 us
  waiting for transfers between devices  219 us (32%)
  Pallas kernels  173 us (26%)
  local copies, waits for them, and re-layouts  141 us (21%)
  starting transfers between devices  77 us (11%)
  other arithmetic  35.5 us (5%)
  between operations  17.8 us (3%)
    ppermute x114, waiting for transfers between devices, swap(): return lax.ppermute(values, axis, [(i, i ^ distance) for i in range(size)])  132 us
    unnamed x593, local copies, waits for them, and re-layouts  110 us
    pallas_call x48, Pallas kernels, call(): return lambda *args: made(*args, *deps)  107 us
    ppermute x114, starting transfers between devices, swap(): return lax.ppermute(values, axis, [(i, i ^ distance) for i in range(size)])  76 us
    all_gather x4, waiting for transfers between devices, gather_dp(): return lax.all_gather(v, 'dp', axis=0, tiled=True)  48.1 us
    pallas_call x2, Pallas kernels, ssm_backward(): pl.pallas_call(lambda r, *refs: ssm_bwd_kernel(r, *refs), grid_spec=pltpu...  39.5 us
    reduce_scatter x4, waiting for transfers between devices, scatter_dp(): return lax.psum_scatter(v, 'dp', scatter_dimension=0, tiled=True)  38.2 us
    pallas_call x2, Pallas kernels, ssm_forward(): pl.pallas_call(ssm_fwd_kernel, grid_spec=pltpu.PrefetchScalarGridSpec(num...  26.9 us
  transfers between devices with their start and end apart: 122, of which 42 were waited for; matrix products, arithmetic and copies ran while one was open for 10% of the time, Pallas kernels for 25%

profile of v2, /device:TPU:0, one launch (start us, length us, event | category | flops | bytes accessed | tf_op | source)
XLA Modules:
  0.0 663.6 jit_solution(17735467450560146307)
XLA Ops:
  26.9 3.0 fusion
  33.7 2.6 collective-permute-start.5
  36.4 2.9 pad_maximum_fusion.2
  42.2 42.6 %all-gather.5.cloned.1.call-done.w_in.w_mix.refs_2_ = bf16[1024,1792]{1,0:T(8,128)(2,1)} async-done(((bf16[128,1792]{1,0:T(8,128)(2,1)}), bf16[1024,1792]{1,0:T(8,128)(2,1)}) %all-gather.5.cloned.1.call-update) | async-done | bytes 3670032 | tf_op jit(solution)/shard_map/all_gather | solution.py:845
  97.3 3.4 project_in.4
  105.0 9.2 %ssm_forward.2 = (bf16[512,384]{1,0:T(8,128)(2,1)S(1)}, bf16[512,384]{1,0:T(8,128)(2,1)S(1)}, bf16[512,640]{1,0:T(8,128)(2,1)S(1)}, bf16[512,640]{1,0:T(8,128)(2...) custom-call(s32[1]{0:T(128)} %bitcast.1.rank.r, ...), custom_call_target="tpu_custom_call" | custom-call | flops 4000000000 | bytes 20971520 | tf_op jit(solution)/shard_map/ssm_forward/pallas_call | solution.py:478
  117.4 4.0 attend_forward.2
  132.0 7.0 %collective-permute-done.18.far = bf16[128,1024]{1,0:T(8,128)(2,1)S(1)} collective-permute-done((bf16[128,1024]{1,0:T(8,128)(2,1)S(1)}, bf16[128,1024]{1,0:T(8,128)(2,1)S(1)}, u32[]{:S(2)}, u32[]{:S(2)}) %collective-permute-start.18) | collective-permute-done | bytes 262176 | tf_op jit(solution)/shard_map/ppermute | solution.py:801
  141.5 3.1 collective-permute-done.31.far
  147.1 3.1 collective-permute-done.20.p3
  151.5 3.6 collective-permute-done.33.p3
  167.3 2.9 ffn.5
  175.5 5.3 collective-permute-done.23.far
  192.6 5.1 collective-permute-done.25.p3
  199.3 3.5 collective-permute-done.38.p3
  202.8 5.5 all-gather.9.cloned.1.call-done.w_in.w_mix
  210.2 3.5 project_in.6
  214.8 4.1 project_in.7
  219.9 17.7 %ssm_forward.3 = (bf16[512,384]{1,0:T(8,128)(2,1)S(1)}, bf16[512,384]{1,0:T(8,128)(2,1)S(1)}, bf16[512,640]{1,0:T(8,128)(2,1)S(1)}, bf16[512,640]{1,0:T(8,128)(2...) custom-call(s32[1]{0:T(128)} %bitcast.1.rank.r, ...), custom_call_target="tpu_custom_call" | custom-call | flops 4000000000 | bytes 20971520 | tf_op jit(solution)/shard_map/ssm_forward/pallas_call | solution.py:478
  240.8 4.0 attend_forward.3
  251.4 6.5 collective-permute-done.51.far
  271.3 3.5 collective-permute-done.63.p3
  274.8 5.6 collective-permute-done.46.p3
  291.3 3.0 ffn.6
  295.1 3.5 ffn_back.5
  300.3 3.4 ffn_back.4
  305.4 3.5 grads_one.2.refs_6_
  317.0 6.0 collective-permute-done.61.refs_4_
  331.5 5.2 collective-permute-done.66.p3
  337.2 3.2 collective-permute-done.71.p3
  345.6 6.2 attend_backward.2
  351.9 19.7 %ssm_backward.2 = (bf16[512,1024]{1,0:T(8,128)(2,1)S(1)}, bf16[512,1024]{1,0:T(8,128)(2,1)S(1)}, bf16[512,512]{1,0:T(8,128)(2,1)S(1)}, bf16[512,512]{1,0:T(8,128...) custom-call(s32[1]{0:T(128)} %bitcast.1.rank.r, s32[1]{0:T(128)} %bitcast.2.oh.refs_0_, ...), custom_call_target="tpu_custom_call" | custom-call | flops 8000000000 | bytes 31457280 | tf_op jit(solution)/shard_map/ssm_backward/pallas_call | solution.py:657
  377.0 4.5 grads_two.2.refs_6_
  391.2 6.0 collective-permute-done.84.far
  410.1 5.0 collective-permute-done.79.refs_3_
  424.5 3.5 ffn_back.6
  429.8 5.1 grads_one.3.refs_6_
  441.9 5.7 collective-permute-done.56.far
  448.8 4.0 collective-permute-done.49.far
  461.9 5.6 collective-permute-done.82.refs_4_
  495.9 6.2 attend_backward.3
  502.3 19.7 %ssm_backward.3 = (bf16[512,1024]{1,0:T(8,128)(2,1)S(1)}, bf16[512,1024]{1,0:T(8,128)(2,1)S(1)}, bf16[512,512]{1,0:T(8,128)(2,1)S(1)}, bf16[512,512]{1,0:T(8,128...) custom-call(s32[1]{0:T(128)} %bitcast.1.rank.r, s32[1]{0:T(128)} %bitcast.2.oh.refs_0_, ...), custom_call_target="tpu_custom_call" | custom-call | flops 8000000000 | bytes 31457280 | tf_op jit(solution)/shard_map/ssm_backward/pallas_call | solution.py:657
  538.2 4.5 grads_two.3.refs_4_
  561.4 6.3 collective-permute-done.102.far
  568.8 3.8 collective-permute-done.100.far
  581.8 3.9 collective-permute-done.104
  586.1 8.3 %collective-permute-done.105 = f32[1,11300]{1,0:T(1,128)S(1)} collective-permute-done((f32[1,11300]{1,0:T(1,128)S(1)}, f32[1,11300]{1,0:T(1,128)S(1)}, u32[]{:S(2)}, u32[]{:S(2)}) %collective-permute-start.105) | collective-permute-done | bytes 45232 | tf_op jit(solution)/shard_map/ppermute | solution.py:801
  607.1 38.2 %reduce-scatter.9.cloned.1.call-done = bf16[128,2048]{1,0:T(8,128)(2,1)} async-done(((bf16[1024,2048]{1,0:T(8,128)(2,1)}), bf16[128,2048]{1,0:T(8,128)(2,1)}) %reduce-scatter.9.cloned.1.call-update) | async-done | bytes 524304 | tf_op jit(solution)/shard_map/reduce_scatter | solution.py:849
  (1037 shorter events, 309.8 us)
Async XLA Ops:
  7.2 77.6 %all-gather.5.cloned.1.call-start = ((), (), s32[]{:S(2)}) async-start(), calls=%async_computation.4 | async-start | bytes 4128768 | tf_op jit(solution)/shard_map/all_gather | solution.py:845
  15.0 140.1 %all-gather.7.cloned.1.call-start = ((), (), s32[]{:S(2)}) async-start(), calls=%async_computation.5 | async-start | bytes 3538944 | tf_op jit(solution)/shard_map/all_gather | solution.py:845
  17.8 190.6 %all-gather.9.cloned.1.call-start = ((), (), s32[]{:S(2)}) async-start(), calls=%async_computation.6 | async-start | bytes 3538944 | tf_op jit(solution)/shard_map/all_gather | solution.py:845
  17.9 76.6 %collective-permute-start = (bf16[128,1024]{1,0:T(8,128)(2,1)S(1)}, bf16[128,1024]{1,0:T(8,128)(2,1)S(1)}, u32[]{:S(2)}, u32[]{:S(2)}) collective-permute-start(bf16[128,1024]{1,0:T(8,128)(2,1)S(1)} %get-tuple-element.430.p2.x.v), channel_id=1, source_target_pairs={{0,1},{1,0},{2,3},{3,2},{4,5},{5,4},{6,7},{7,6},{8,9},{9,8},{10,11... | collective-permute-start | bytes 786440 | tf_op jit(solution)/shard_map/ppermute | solution.py:801
  18.4 72.9 %collective-permute-start.1 = (bf16[128,1024]{1,0:T(8,128)(2,1)S(1)}, bf16[128,1024]{1,0:T(8,128)(2,1)S(1)}, u32[]{:S(2)}, u32[]{:S(2)}) collective-permute-start(bf16[128,1024]{1,0:T(8,128)(2,1)S(1)} %get-tuple-element.430.p2.x.v), channel_id=1, source_target_pairs={{0,2},{1,3},{2,0},{3,1},{4,6},{5,7},{6,4},{7,5},{8,10},{9,11},{10,... | collective-permute-start | bytes 786440 | tf_op jit(solution)/shard_map/ppermute | solution.py:801
  22.7 72.3 %collective-permute-start.12 = (bf16[128,1024]{1,0:T(8,128)(2,1)S(1)}, bf16[128,1024]{1,0:T(8,128)(2,1)S(1)}, u32[]{:S(2)}, u32[]{:S(2)}) collective-permute-start(bf16[128,1024]{1,0:T(8,128)(2,1)S(1)} %get-tuple-element.431.p2.x.v), channel_id=1, source_target_pairs={{0,2},{1,3},{2,0},{3,1},{4,6},{5,7},{6,4},{7,5},{8,10},{9,11},{10,... | collective-permute-start | bytes 786440 | tf_op jit(solution)/shard_map/ppermute | solution.py:801
  24.5 257.9 %all-gather.11.cloned.1.call-start = ((), (), s32[]{:S(2)}) async-start(), calls=%async_computation.7 | async-start | bytes 3538944 | tf_op jit(solution)/shard_map/all_gather | solution.py:845
  40.6 47.4 %collective-permute-start.7 = (bf16[8,2,208]{2,1,0:T(2,128)(2,1)S(1)}, bf16[8,2,208]{2,1,0:T(2,128)(2,1)S(1)}, u32[]{:S(2)}, u32[]{:S(2)}) collective-permute-start(bf16[8,2,208]{2,1,0:T(2,128)(2,1)S(1)} %pad_maximum_fusion.15), channel_id=1, source_target_pairs={{0,2},{1,3},{2,0},{3,1},{4,6},{5,7},{6,4},{7,5},{8,10},{9,11},{10,... | collective-permute-start | bytes 19976 | tf_op jit(solution)/shard_map/ppermute | solution.py:801
  129.6 286.8 %reduce-scatter.5.cloned.1.call-start = ((), (), s32[]{:S(2)}) async-start(), calls=%async_computation.8 | async-start | bytes 3538944 | tf_op jit(solution)/shard_map/reduce_scatter | solution.py:849
  131.3 13.3 %collective-permute-start.31 = (bf16[128,1024]{1,0:T(8,128)(2,1)S(1)}, bf16[128,1024]{1,0:T(8,128)(2,1)S(1)}, u32[]{:S(2)}, u32[]{:S(2)}) collective-permute-start(bf16[128,1024]{1,0:T(8,128)(2,1)S(1)} %add_convert_fusion.13), channel_id=1, source_target_pairs={{0,2},{1,3},{2,0},{3,1},{4,6},{5,7},{6,4},{7,5},{8,10},{9,11},{10,... | collective-permute-start | bytes 786440 | tf_op jit(solution)/shard_map/ppermute | solution.py:801
  140.0 10.2 %collective-permute-start.20 = (bf16[128,1024]{1,0:T(8,128)(2,1)S(1)}, bf16[128,1024]{1,0:T(8,128)(2,1)S(1)}, u32[]{:S(2)}, u32[]{:S(2)}) collective-permute-start(bf16[128,1024]{1,0:T(8,128)(2,1)S(1)} %get-tuple-element.194.p2), channel_id=1, source_target_pairs={{0,2},{1,3},{2,0},{3,1},{4,6},{5,7},{6,4},{7,5},{8,10},{9,11},{10,... | collective-permute-start | bytes 786440 | tf_op jit(solution)/shard_map/ppermute | solution.py:801
  151.0 16.4 %collective-permute-start.32 = (bf16[128,1024]{1,0:T(8,128)(2,1)S(1)}, bf16[128,1024]{1,0:T(8,128)(2,1)}, u32[]{:S(2)}, u32[]{:S(2)}) collective-permute-start(bf16[128,1024]{1,0:T(8,128)(2,1)S(1)} %get-tuple-element.205.p2), channel_id=1, source_target_pairs={{0,1},{1,0},{2,3},{3,2},{4,5},{5,4},{6,7},{7,6},{8,9},{9,8},{10,11... | collective-permute-start | bytes 786440 | tf_op jit(solution)/shard_map/ppermute | solution.py:801
  155.1 12.3 %collective-permute-start.34 = (bf16[128,1024]{1,0:T(8,128)(2,1)}, bf16[128,1024]{1,0:T(8,128)(2,1)}, u32[]{:S(2)}, u32[]{:S(2)}) collective-permute-start(bf16[128,1024]{1,0:T(8,128)(2,1)} %collective-permute-done.33.p3), channel_id=1, source_target_pairs={{0,1},{1,0},{2,3},{3,2},{4,5},{5,4},{6,7},{7,6},{8,9},{9,8},{10,11... | collective-permute-start | bytes 786440 | tf_op jit(solution)/shard_map/ppermute | solution.py:801
  173.3 13.0 %collective-permute-start.36 = (bf16[128,1024]{1,0:T(8,128)(2,1)S(1)}, bf16[128,1024]{1,0:T(8,128)(2,1)S(1)}, u32[]{:S(2)}, u32[]{:S(2)}) collective-permute-start(bf16[128,1024]{1,0:T(8,128)(2,1)S(1)} %add_convert_fusion.12), channel_id=1, source_target_pairs={{0,2},{1,3},{2,0},{3,1},{4,6},{5,7},{6,4},{7,5},{8,10},{9,11},{10,... | collective-permute-start | bytes 786440 | tf_op jit(solution)/shard_map/ppermute | solution.py:801
  175.0 17.1 %collective-permute-start.28 = (bf16[1024,128]{1,0:T(8,128)(2,1)}, bf16[1024,128]{1,0:T(8,128)(2,1)}, u32[]{:S(2)}, u32[]{:S(2)}) collective-permute-start(bf16[1024,128]{1,0:T(8,128)(2,1)} %get-tuple-element.420.refs_0_), channel_id=1, source_target_pairs={{0,2},{1,3},{2,0},{3,1},{4,6},{5,7},{6,4},{7,5},{8,10},{9,11},{10,... | collective-permute-start | bytes 786440 | tf_op jit(solution)/shard_map/ppermute | solution.py:801
  182.5 15.2 %collective-permute-start.25 = (bf16[128,1024]{1,0:T(8,128)(2,1)}, bf16[128,1024]{1,0:T(8,128)(2,1)}, u32[]{:S(2)}, u32[]{:S(2)}) collective-permute-start(bf16[128,1024]{1,0:T(8,128)(2,1)} %get-tuple-element.198.p2), channel_id=1, source_target_pairs={{0,2},{1,3},{2,0},{3,1},{4,6},{5,7},{6,4},{7,5},{8,10},{9,11},{10,... | collective-permute-start | bytes 786440 | tf_op jit(solution)/shard_map/ppermute | solution.py:801
  184.1 14.6 %collective-permute-start.27 = (bf16[1024,128]{1,0:T(8,128)(2,1)}, bf16[1024,128]{1,0:T(8,128)(2,1)}, u32[]{:S(2)}, u32[]{:S(2)}) collective-permute-start(bf16[1024,128]{1,0:T(8,128)(2,1)} %get-tuple-element.420.refs_0_), channel_id=1, source_target_pairs={{0,1},{1,0},{2,3},{3,2},{4,5},{5,4},{6,7},{7,6},{8,9},{9,8},{10,11... | collective-permute-start | bytes 786440 | tf_op jit(solution)/shard_map/ppermute | solution.py:801
  188.1 14.7 %collective-permute-start.38 = (bf16[128,1024]{1,0:T(8,128)(2,1)}, bf16[128,1024]{1,0:T(8,128)(2,1)}, u32[]{:S(2)}, u32[]{:S(2)}) collective-permute-start(bf16[128,1024]{1,0:T(8,128)(2,1)} %get-tuple-element.208.p2), channel_id=1, source_target_pairs={{0,2},{1,3},{2,0},{3,1},{4,6},{5,7},{6,4},{7,5},{8,10},{9,11},{10,... | collective-permute-start | bytes 786440 | tf_op jit(solution)/shard_map/ppermute | solution.py:801
  192.1 16.2 %collective-permute-start.29 = (bf16[1024,128]{1,0:T(8,128)(2,1)}, bf16[1024,128]{1,0:T(8,128)(2,1)}, u32[]{:S(2)}, u32[]{:S(2)}) collective-permute-start(bf16[1024,128]{1,0:T(8,128)(2,1)} %collective-permute-done.28.refs_2_), channel_id=1, source_target_pairs={{0,1},{1,0},{2,3},{3,2},{4,5},{5,4},{6,7},{7,6},{8,9},{9,8},{10,11... | collective-permute-start | bytes 786440 | tf_op jit(solution)/shard_map/ppermute | solution.py:801
  192.1 16.2 %collective-permute-start.24 = (bf16[128,1024]{1,0:T(8,128)(2,1)}, bf16[128,1024]{1,0:T(8,128)(2,1)}, u32[]{:S(2)}, u32[]{:S(2)}) collective-permute-start(bf16[128,1024]{1,0:T(8,128)(2,1)} %get-tuple-element.198.p2), channel_id=1, source_target_pairs={{0,1},{1,0},{2,3},{3,2},{4,5},{5,4},{6,7},{7,6},{8,9},{9,8},{10,11... | collective-permute-start | bytes 786440 | tf_op jit(solution)/shard_map/ppermute | solution.py:801
  197.7 10.6 %collective-permute-start.26 = (bf16[128,1024]{1,0:T(8,128)(2,1)}, bf16[128,1024]{1,0:T(8,128)(2,1)}, u32[]{:S(2)}, u32[]{:S(2)}) collective-permute-start(bf16[128,1024]{1,0:T(8,128)(2,1)} %collective-permute-done.25.p3), channel_id=1, source_target_pairs={{0,1},{1,0},{2,3},{3,2},{4,5},{5,4},{6,7},{7,6},{8,9},{9,8},{10,11... | collective-permute-start | bytes 786440 | tf_op jit(solution)/shard_map/ppermute | solution.py:801
  198.7 16.0 %collective-permute-start.37 = (bf16[128,1024]{1,0:T(8,128)(2,1)}, bf16[128,1024]{1,0:T(8,128)(2,1)}, u32[]{:S(2)}, u32[]{:S(2)}) collective-permute-start(bf16[128,1024]{1,0:T(8,128)(2,1)} %get-tuple-element.208.p2), channel_id=1, source_target_pairs={{0,1},{1,0},{2,3},{3,2},{4,5},{5,4},{6,7},{7,6},{8,9},{9,8},{10,11... | collective-permute-start | bytes 786440 | tf_op jit(solution)/shard_map/ppermute | solution.py:801
  202.8 12.0 %collective-permute-start.39 = (bf16[128,1024]{1,0:T(8,128)(2,1)}, bf16[128,1024]{1,0:T(8,128)(2,1)}, u32[]{:S(2)}, u32[]{:S(2)}) collective-permute-start(bf16[128,1024]{1,0:T(8,128)(2,1)} %collective-permute-done.38.p3), channel_id=1, source_target_pairs={{0,1},{1,0},{2,3},{3,2},{4,5},{5,4},{6,7},{7,6},{8,9},{9,8},{10,11... | collective-permute-start | bytes 786440 | tf_op jit(solution)/shard_map/ppermute | solution.py:801
  250.3 13.2 %collective-permute-start.44 = (bf16[128,1024]{1,0:T(8,128)(2,1)S(1)}, bf16[128,1024]{1,0:T(8,128)(2,1)S(1)}, u32[]{:S(2)}, u32[]{:S(2)}) collective-permute-start(bf16[128,1024]{1,0:T(8,128)(2,1)S(1)} %add_convert_fusion.11), channel_id=1, source_target_pairs={{0,2},{1,3},{2,0},{3,1},{4,6},{5,7},{6,4},{7,5},{8,10},{9,11},{10,... | collective-permute-start | bytes 786440 | tf_op jit(solution)/shard_map/ppermute | solution.py:801
  258.1 11.0 %collective-permute-start.53 = (bf16[128,1024]{1,0:T(8,128)(2,1)S(1)}, bf16[128,1024]{1,0:T(8,128)(2,1)S(1)}, u32[]{:S(2)}, u32[]{:S(2)}) collective-permute-start(bf16[128,1024]{1,0:T(8,128)(2,1)S(1)} %get-tuple-element.232.p2), channel_id=1, source_target_pairs={{0,2},{1,3},{2,0},{3,1},{4,6},{5,7},{6,4},{7,5},{8,10},{9,11},{10,... | collective-permute-start | bytes 786440 | tf_op jit(solution)/shard_map/ppermute | solution.py:801
  260.4 14.4 %collective-permute-start.63 = (bf16[128,1024]{1,0:T(8,128)(2,1)}, bf16[128,1024]{1,0:T(8,128)(2,1)}, u32[]{:S(2)}, u32[]{:S(2)}) collective-permute-start(bf16[128,1024]{1,0:T(8,128)(2,1)} %get-tuple-element.427.p2.g), channel_id=1, source_target_pairs={{0,2},{1,3},{2,0},{3,1},{4,6},{5,7},{6,4},{7,5},{8,10},{9,11},{10,... | collective-permute-start | bytes 786440 | tf_op jit(solution)/shard_map/ppermute | solution.py:801
  265.2 15.2 %collective-permute-start.46 = (bf16[128,1024]{1,0:T(8,128)(2,1)}, bf16[128,1024]{1,0:T(8,128)(2,1)}, u32[]{:S(2)}, u32[]{:S(2)}) collective-permute-start(bf16[128,1024]{1,0:T(8,128)(2,1)} %get-tuple-element.223.p2), channel_id=1, source_target_pairs={{0,2},{1,3},{2,0},{3,1},{4,6},{5,7},{6,4},{7,5},{8,10},{9,11},{10,... | collective-permute-start | bytes 786440 | tf_op jit(solution)/shard_map/ppermute | solution.py:801
  266.7 13.8 %collective-permute-start.52 = (bf16[128,1024]{1,0:T(8,128)(2,1)S(1)}, bf16[128,1024]{1,0:T(8,128)(2,1)S(1)}, u32[]{:S(2)}, u32[]{:S(2)}) collective-permute-start(bf16[128,1024]{1,0:T(8,128)(2,1)S(1)} %get-tuple-element.232.p2), channel_id=1, source_target_pairs={{0,1},{1,0},{2,3},{3,2},{4,5},{5,4},{6,7},{7,6},{8,9},{9,8},{10,11... | collective-permute-start | bytes 786440 | tf_op jit(solution)/shard_map/ppermute | solution.py:801
  269.1 12.6 %collective-permute-start.54 = (bf16[128,1024]{1,0:T(8,128)(2,1)S(1)}, bf16[128,1024]{1,0:T(8,128)(2,1)S(1)}, u32[]{:S(2)}, u32[]{:S(2)}) collective-permute-start(bf16[128,1024]{1,0:T(8,128)(2,1)S(1)} %collective-permute-done.53.p3), channel_id=1, source_target_pairs={{0,1},{1,0},{2,3},{3,2},{4,5},{5,4},{6,7},{7,6},{8,9},{9,8},{10,11... | collective-permute-start | bytes 786440 | tf_op jit(solution)/shard_map/ppermute | solution.py:801
  269.8 20.9 %collective-permute-start.58 = (bf16[128,1024]{1,0:T(8,128)(2,1)S(1)}, bf16[128,1024]{1,0:T(8,128)(2,1)}, u32[]{:S(2)}, u32[]{:S(2)}) collective-permute-start(bf16[128,1024]{1,0:T(8,128)(2,1)S(1)} %get-tuple-element.426.p2.refs_0_), channel_id=1, source_target_pairs={{0,2},{1,3},{2,0},{3,1},{4,6},{5,7},{6,4},{7,5},{8,10},{9,11},{10,... | collective-permute-start | bytes 786440 | tf_op jit(solution)/shard_map/ppermute | solution.py:801
  274.8 16.4 %collective-permute-start.45 = (bf16[128,1024]{1,0:T(8,128)(2,1)}, bf16[128,1024]{1,0:T(8,128)(2,1)}, u32[]{:S(2)}, u32[]{:S(2)}) collective-permute-start(bf16[128,1024]{1,0:T(8,128)(2,1)} %get-tuple-element.223.p2), channel_id=1, source_target_pairs={{0,1},{1,0},{2,3},{3,2},{4,5},{5,4},{6,7},{7,6},{8,9},{9,8},{10,11... | collective-permute-start | bytes 786440 | tf_op jit(solution)/shard_map/ppermute | solution.py:801
  280.4 10.9 %collective-permute-start.47 = (bf16[128,1024]{1,0:T(8,128)(2,1)}, bf16[128,1024]{1,0:T(8,128)(2,1)}, u32[]{:S(2)}, u32[]{:S(2)}) collective-permute-start(bf16[128,1024]{1,0:T(8,128)(2,1)} %collective-permute-done.46.p3), channel_id=1, source_target_pairs={{0,1},{1,0},{2,3},{3,2},{4,5},{5,4},{6,7},{7,6},{8,9},{9,8},{10,11... | collective-permute-start | bytes 786440 | tf_op jit(solution)/shard_map/ppermute | solution.py:801
  281.2 14.0 %collective-permute-start.62 = (bf16[128,1024]{1,0:T(8,128)(2,1)}, bf16[128,1024]{1,0:T(8,128)(2,1)}, u32[]{:S(2)}, u32[]{:S(2)}) collective-permute-start(bf16[128,1024]{1,0:T(8,128)(2,1)} %get-tuple-element.427.p2.g), channel_id=1, source_target_pairs={{0,1},{1,0},{2,3},{3,2},{4,5},{5,4},{6,7},{7,6},{8,9},{9,8},{10,11... | collective-permute-start | bytes 786440 | tf_op jit(solution)/shard_map/ppermute | solution.py:801
  282.4 12.7 %collective-permute-start.64 = (bf16[128,1024]{1,0:T(8,128)(2,1)}, bf16[128,1024]{1,0:T(8,128)(2,1)}, u32[]{:S(2)}, u32[]{:S(2)}) collective-permute-start(bf16[128,1024]{1,0:T(8,128)(2,1)} %collective-permute-done.63.p3), channel_id=1, source_target_pairs={{0,1},{1,0},{2,3},{3,2},{4,5},{5,4},{6,7},{7,6},{8,9},{9,8},{10,11... | collective-permute-start | bytes 786440 | tf_op jit(solution)/shard_map/ppermute | solution.py:801
  290.7 9.6 %collective-permute-start.57 = (bf16[128,1024]{1,0:T(8,128)(2,1)S(1)}, bf16[128,1024]{1,0:T(8,128)(2,1)S(1)}, u32[]{:S(2)}, u32[]{:S(2)}) collective-permute-start(bf16[128,1024]{1,0:T(8,128)(2,1)S(1)} %get-tuple-element.426.p2.refs_0_), channel_id=1, source_target_pairs={{0,1},{1,0},{2,3},{3,2},{4,5},{5,4},{6,7},{7,6},{8,9},{9,8},{10,11... | collective-permute-start | bytes 786440 | tf_op jit(solution)/shard_map/ppermute | solution.py:801
  310.5 216.1 %reduce-scatter.7.cloned.1.call-start = ((), (), s32[]{:S(2)}) async-start(), calls=%async_computation.9 | async-start | bytes 4718592 | tf_op jit(solution)/shard_map/reduce_scatter | solution.py:849
  316.4 12.6 %collective-permute-start.69 = (bf16[128,1024]{1,0:T(8,128)(2,1)S(1)}, bf16[128,1024]{1,0:T(8,128)(2,1)S(1)}, u32[]{:S(2)}, u32[]{:S(2)}) collective-permute-start(bf16[128,1024]{1,0:T(8,128)(2,1)S(1)} %add_convert_fusion.6), channel_id=1, source_target_pairs={{0,2},{1,3},{2,0},{3,1},{4,6},{5,7},{6,4},{7,5},{8,10},{9,11},{10,... | collective-permute-start | bytes 786440 | tf_op jit(solution)/shard_map/ppermute | solution.py:801
  330.4 10.0 %collective-permute-start.71 = (bf16[128,1024]{1,0:T(8,128)(2,1)S(1)}, bf16[128,1024]{1,0:T(8,128)(2,1)S(1)}, u32[]{:S(2)}, u32[]{:S(2)}) collective-permute-start(bf16[128,1024]{1,0:T(8,128)(2,1)S(1)} %get-tuple-element.255.p2), channel_id=1, source_target_pairs={{0,2},{1,3},{2,0},{3,1},{4,6},{5,7},{6,4},{7,5},{8,10},{9,11},{10,... | collective-permute-start | bytes 786440 | tf_op jit(solution)/shard_map/ppermute | solution.py:801
  384.5 217.5 %reduce-scatter.11.cloned.1.call-start = ((), (), s32[]{:S(2)}) async-start(), calls=%async_computation.11 | async-start | bytes 3538944 | tf_op jit(solution)/shard_map/reduce_scatter | solution.py:849
  390.6 13.0 %collective-permute-start.77 = (bf16[128,1024]{1,0:T(8,128)(2,1)S(1)}, bf16[128,1024]{1,0:T(8,128)(2,1)S(1)}, u32[]{:S(2)}, u32[]{:S(2)}) collective-permute-start(bf16[128,1024]{1,0:T(8,128)(2,1)S(1)} %add_convert_fusion.5), channel_id=1, source_target_pairs={{0,2},{1,3},{2,0},{3,1},{4,6},{5,7},{6,4},{7,5},{8,10},{9,11},{10,... | collective-permute-start | bytes 786440 | tf_op jit(solution)/shard_map/ppermute | solution.py:801
  410.1 14.4 %collective-permute-start.78 = (bf16[128,1024]{1,0:T(8,128)(2,1)}, bf16[128,1024]{1,0:T(8,128)(2,1)}, u32[]{:S(2)}, u32[]{:S(2)}) collective-permute-start(bf16[128,1024]{1,0:T(8,128)(2,1)} %get-tuple-element.278.refs_2_), channel_id=1, source_target_pairs={{0,1},{1,0},{2,3},{3,2},{4,5},{5,4},{6,7},{7,6},{8,9},{9,8},{10,11... | collective-permute-start | bytes 786440 | tf_op jit(solution)/shard_map/ppermute | solution.py:801
  415.1 9.4 %collective-permute-start.80 = (bf16[128,1024]{1,0:T(8,128)(2,1)}, bf16[128,1024]{1,0:T(8,128)(2,1)}, u32[]{:S(2)}, u32[]{:S(2)}) collective-permute-start(bf16[128,1024]{1,0:T(8,128)(2,1)} %collective-permute-done.79.refs_3_), channel_id=1, source_target_pairs={{0,1},{1,0},{2,3},{3,2},{4,5},{5,4},{6,7},{7,6},{8,9},{9,8},{10,11... | collective-permute-start | bytes 786440 | tf_op jit(solution)/shard_map/ppermute | solution.py:801
  434.9 210.4 %reduce-scatter.9.cloned.1.call-start = ((), (), s32[]{:S(2)}) async-start(), calls=%async_computation.10 | async-start | bytes 4718592 | tf_op jit(solution)/shard_map/reduce_scatter | solution.py:849
  441.0 11.8 %collective-permute-start.49 = (bf16[128,1024]{1,0:T(8,128)(2,1)}, bf16[128,1024]{1,0:T(8,128)(2,1)}, u32[]{:S(2)}, u32[]{:S(2)}) collective-permute-start(bf16[128,1024]{1,0:T(8,128)(2,1)} %add_convert_fusion.10), channel_id=1, source_target_pairs={{0,2},{1,3},{2,0},{3,1},{4,6},{5,7},{6,4},{7,5},{8,10},{9,11},{10,... | collective-permute-start | bytes 786440 | tf_op jit(solution)/shard_map/ppermute | solution.py:801
  441.9 15.4 %collective-permute-start.81 = (bf16[256,1024]{1,0:T(8,128)(2,1)}, bf16[256,1024]{1,0:T(8,128)(2,1)}, u32[]{:S(2)}, u32[]{:S(2)}) collective-permute-start(bf16[256,1024]{1,0:T(8,128)(2,1)} %copy-done.197), channel_id=1, source_target_pairs={{0,1},{1,0},{2,3},{3,2},{4,5},{5,4},{6,7},{7,6},{8,9},{9,8},{10,11... | collective-permute-start | bytes 1572872 | tf_op jit(solution)/shard_map/ppermute | solution.py:801
  460.3 13.0 %collective-permute-start.92 = (bf16[128,1024]{1,0:T(8,128)(2,1)}, bf16[128,1024]{1,0:T(8,128)(2,1)}, u32[]{:S(2)}, u32[]{:S(2)}) collective-permute-start(bf16[128,1024]{1,0:T(8,128)(2,1)} %add_convert_fusion.2), channel_id=1, source_target_pairs={{0,2},{1,3},{2,0},{3,1},{4,6},{5,7},{6,4},{7,5},{8,10},{9,11},{10,... | collective-permute-start | bytes 786440 | tf_op jit(solution)/shard_map/ppermute | solution.py:801
  469.6 10.3 %collective-permute-start.89 = (bf16[128,1024]{1,0:T(8,128)(2,1)S(1)}, bf16[128,1024]{1,0:T(8,128)(2,1)}, u32[]{:S(2)}, u32[]{:S(2)}) collective-permute-start(bf16[128,1024]{1,0:T(8,128)(2,1)S(1)} %get-tuple-element.298.p2), channel_id=1, source_target_pairs={{0,2},{1,3},{2,0},{3,1},{4,6},{5,7},{6,4},{7,5},{8,10},{9,11},{10,... | collective-permute-start | bytes 786440 | tf_op jit(solution)/shard_map/ppermute | solution.py:801
  559.9 12.7 %collective-permute-start.100 = (bf16[128,1024]{1,0:T(8,128)(2,1)S(1)}, bf16[128,1024]{1,0:T(8,128)(2,1)S(1)}, u32[]{:S(2)}, u32[]{:S(2)}) collective-permute-start(bf16[128,1024]{1,0:T(8,128)(2,1)S(1)} %add_convert_fusion.1), channel_id=1, source_target_pairs={{0,2},{1,3},{2,0},{3,1},{4,6},{5,7},{6,4},{7,5},{8,10},{9,11},{10,... | collective-permute-start | bytes 786440 | tf_op jit(solution)/shard_map/ppermute | solution.py:801
  (355 other events, 3071.8 us)
Sparse Core Ops, SparseCore 0:
  15.1 69.6 all-gather.4
  87.5 58.8 all-gather.6
  149.2 59.0 all-gather.8
  210.4 59.0 all-gather.10
  310.6 73.1 reduce-scatter.4
  387.3 86.9 reduce-scatter.6
  478.3 74.0 reduce-scatter.10
  556.5 88.8 reduce-scatter.8

commit v3 on v2

--- a/solution.py
+++ b/solution.py
@@ -22,7 +22,8 @@
 BF16 = jnp.bfloat16
 EXACT = lax.Precision.HIGHEST
 NEG = -1e30
-VMEM_BYTES = 28 * 1024 * 1024
+VMEM_BYTES = 16 * 1024 * 1024
+GRADS_BYTES = 24 * 1024 * 1024
 
 
 def dot_nn(left, right, **kw):
@@ -66,13 +67,28 @@
 
 def whole(shape, *at):
     at = at or (0,) * len(shape)
-    return pl.BlockSpec(shape, lambda *_: at)
+    return pl.BlockSpec(shape, lambda *_: at, pipeline_mode=pl.Buffered(1))
+
+
+def hbm(v):
+    return jax.tree.map(lambda x: pltpu.with_memory_space_constraint(x, pltpu.HBM), v)
+
+
+def far_out(shape, dtype):
+    return pltpu.HBM(shape, dtype)
+
+
+def bytes_of(made):
+    size = made.dtype.itemsize
+    for d in made.shape:
+        size *= d
+    return size
 
 
 SCALAR = pl.BlockSpec(memory_space=pltpu.SMEM)
 
 
-def call(kernel, name, in_specs, out_shapes, flops, scratch=(), deps=()):
+def call(kernel, name, in_specs, out_shapes, flops, scratch=(), deps=(), vmem=VMEM_BYTES):
     if deps:
         base, skipped = kernel, range(len(in_specs), len(in_specs) + len(deps))
 
@@ -80,7 +96,7 @@
             base(*(r for i, r in enumerate(refs) if i not in skipped))
 
         in_specs = list(in_specs) + [pl.BlockSpec(memory_space=pl.ANY)] * len(deps)
-    many = sum(s.size * s.dtype.itemsize for s in out_shapes)
+    many = sum(bytes_of(s) for s in out_shapes)
     made = pl.pallas_call(
         kernel,
         grid=(1,),
@@ -89,7 +105,7 @@
         out_shape=out_shapes,
         scratch_shapes=list(scratch),
         compiler_params=pltpu.CompilerParams(
-            dimension_semantics=("arbitrary",), vmem_limit_bytes=VMEM_BYTES
+            dimension_semantics=("arbitrary",), vmem_limit_bytes=vmem
         ),
         cost_estimate=pl.CostEstimate(
             flops=int(flops), bytes_accessed=2 * many, transcendentals=10**5
@@ -126,16 +142,16 @@
     step_kernel(x, keep, got, far, None, x_o, None)
 
 
-def take_step(x, keep, got, far, gain):
+def take_step(x, keep, got, far, gain, deps=()):
     w = x.shape[1]
     specs = [whole((R, w))] * 4
     if gain is None:
-        return call(last_kernel, "last_step", specs, [sds((R, w), BF16)], 10**6)(
-            x, keep, got, far
+        return call(last_kernel, "last_step", specs, [sds((R, w), BF16)], 10**6, deps=deps)(
+            hbm(x), *hbm((keep, got, far))
         )[0]
     return call(
-        step_kernel, "step", specs + [whole((8, w))], [sds((R, w), F32), sds((R, w), BF16)], 10**6
-    )(x, keep, got, far, gain)
+        step_kernel, "step", specs + [whole((8, w))], [far_out((R, w), F32), sds((R, w), BF16)], 10**6
+    )(hbm(x), *hbm((keep, got, far)), gain)
 
 
 def back_step_kernel(g, v, keep, got, far, gain, g_o, low_o, gg_o):
@@ -153,10 +169,10 @@
         back_step_kernel,
         "back_step",
         [whole((R, w))] * 5 + [whole((8, w))],
-        [sds((R, w), F32), sds((R, w), BF16), sds((8, w), F32)],
+        [far_out((R, w), F32), sds((R, w), BF16), sds((8, w), F32)],
         10**6,
         deps=deps,
-    )(g, v, keep, got, far, gain)
+    )(hbm(g), hbm(v), *hbm((keep, got, far)), gain)
 
 
 def input_kernel(first, depth, rank, oh, p0, p1, p2, p3, gain, w_in, *refs):
@@ -194,7 +210,7 @@
     w = pieces[0].shape[1]
     n = QUARTERS * R
     shares = w_sh if isinstance(w_sh, tuple) else (w_sh,)
-    outs = [sds((n, w), BF16), sds((n, 896), BF16), sds((n, 128), F32), sds((n, 384), BF16)]
+    outs = [far_out((n, w), BF16), sds((n, 896), BF16), sds((n, 128), F32), sds((n, 384), BF16)]
     if len(shares) > 1:
         outs = [sds((w, 512), BF16)] + outs
     return call(
@@ -204,7 +220,7 @@
         + [whole(v.shape) for v in shares],
         outs,
         2 * n * w * 1536,
-    )(rank, oh, *pieces, gain, w_in, *shares)
+    )(rank, oh, *hbm(pieces), gain, w_in, *shares)
 
 
 def input_back_kernel(da, ds, w_in, w_sh, send, keep):
@@ -222,7 +238,7 @@
         [sds((2 * R, w), BF16)] * 2,
         2 * n * w * 1536,
         deps=deps,
-    )(da, ds, w_in, w_sh)
+    )(hbm(da), hbm(ds), w_in, w_sh)
 
 
 def column(row_ref, start):
@@ -255,7 +271,7 @@
             SCALAR, whole((n, 128)), whole((n, 384)), whole((n, 512)), whole(fac.shape),
             whole((8, 384)), whole((w, 512), 0, 2),
         ],
-        [sds((n, 512), BF16), sds((2 * R, w), BF16), sds((2 * R, w), BF16)],
+        [far_out((n, 512), BF16), sds((2 * R, w), BF16), sds((2 * R, w), BF16)],
         2 * n * w * 512,
     )(rank, o, y, pa, fac, gain, w_mix)
 
@@ -287,9 +303,9 @@
         "mix_back",
         [SCALAR] + [whole((R, w))] * 4
         + [whole((n, 384)), whole((n, 512)), whole((8, 384)), whole((w, 512), 0, 2)],
-        [sds((n, w), BF16), sds((n, 128), BF16), sds((n, 384), F32), sds((1, n), F32)],
+        [far_out((n, w), BF16), sds((n, 128), BF16), far_out((n, 384), F32), sds((1, n), F32)],
         2 * n * w * 512,
-    )(rank, *pieces, y, pa, gain, w_mix)
+    )(rank, *hbm(pieces), hbm(y), hbm(pa), gain, w_mix)
 
 
 def ffn_kernel(p0, p1, p2, p3, w_gu, w_dn, h_o, gu_o, act_o, send, keep):
@@ -312,11 +328,11 @@
         "ffn",
         [whole((R, w))] * 4 + [whole((w, 1024)), whole((w, 512), 0, 2)],
         [
-            sds((n, w), BF16), sds((n, 1024), BF16), sds((n, 512), BF16),
+            far_out((n, w), BF16), far_out((n, 1024), BF16), far_out((n, 512), BF16),
             sds((2 * R, w), BF16), sds((2 * R, w), BF16),
         ],
         2 * n * w * 1536,
-    )(*pieces, w_second, w_second)
+    )(*hbm(pieces), w_second, w_second)
 
 
 def ffn_back_kernel(p0, p1, p2, p3, gu, w_gu, w_dn, df_o, dgu_o, send, keep):
@@ -338,37 +354,145 @@
         ffn_back_kernel,
         "ffn_back",
         [whole((R, w))] * 4 + [whole((n, 1024)), whole((w, 1024)), whole((w, 512), 0, 2)],
-        [sds((n, w), BF16), sds((n, 1024), BF16), sds((2 * R, w), BF16), sds((2 * R, w), BF16)],
+        [far_out((n, w), BF16), far_out((n, 1024), BF16), sds((2 * R, w), BF16), sds((2 * R, w), BF16)],
         2 * n * w * 1536,
         deps=deps,
-    )(*pieces, gu, w_second, w_second)
-
-
-def weight_grad_kernel(widths, *refs):
+    )(*hbm(pieces), hbm(gu), w_second, w_second)
+
+
+def weight_grad_kernel(widths, share, depth, sel, *refs):
     out = refs[-1]
     at = 0
     for i, width in enumerate(widths):
         la, lb, ra, rb = refs[4 * i : 4 * i + 4]
-        g = dot_tn(la[...], ra[...]) + dot_tn(lb[...], rb[...])
-        out[:, at : at + width] = g.astype(BF16)
+        total = 0.0
+        for left, right in ((la, ra), (lb, rb)):
+            if share is None:
+                rows = left[...]
+            else:
+                rows = left[:, pl.ds(pl.multiple_of(sel[0] * share, share), share)]
+            total = total + dot_tn(rows, right[...])
+        out[:, at : at + width] = total.astype(BF16)
         at += width
-
-
-def weight_grads(name, groups, deps=()):
+    if depth is None:
+        return
+    kept, got, far = refs[4 * len(widths) : 4 * len(widths) + 3]
+    sq = depth // QUARTERS
+    for d in range(out.shape[0] // depth):
+        start = pl.multiple_of((pl.program_id(0) * (out.shape[0] // depth) + d) * sq, sq)
+        rows = pl.ds(start, sq)
+        total = kept[rows].astype(F32) + got[rows].astype(F32) + far[rows].astype(F32)
+        for c in range(QUARTERS):
+            out[d * depth + c * sq : d * depth + (c + 1) * sq, at:] = total[
+                :, 128 * c : 128 * c + 128
+            ].astype(BF16)
+
+
+def weight_grads(name, groups, deps=(), share=None, sel=None, shared=None, depth=None):
     n, w = groups[0][0][0].shape
     widths = [right[0].shape[1] for _, right in groups]
+    step = 512 if share is None else 2 * share
+    rows = step if share is None else share
     specs, args = [], []
     for (la, lb), (ra, rb) in groups:
-        specs += [whole(la.shape)] * 2 + [whole(ra.shape)] * 2
+        specs += [pl.BlockSpec((n, step), lambda i: (0, i))] * 2 + [whole(ra.shape)] * 2
         args += [la, lb, ra, rb]
+    args = list(hbm(args))
+    total = sum(widths)
+    if shared is not None:
+        total += 128
+        some = shared[2].shape
+        specs += [whole(some)] * 3
+        args += list(shared)
+    taken = len(args)
+
+    def kernel(sel_ref, *refs):
+        weight_grad_kernel(widths, share, depth, sel_ref, *refs[:taken], refs[-1])
+
+    return pl.pallas_call(
+        kernel,
+        grid=(w // step,),
+        in_specs=[SCALAR] + specs + [pl.BlockSpec(memory_space=pl.ANY)] * len(deps),
+        out_specs=pl.BlockSpec((rows, total), lambda i: (i, 0)),
+        out_shape=far_out((w // step * rows, total), BF16),
+        compiler_params=pltpu.CompilerParams(
+            dimension_semantics=("arbitrary",), vmem_limit_bytes=GRADS_BYTES
+        ),
+        cost_estimate=pl.CostEstimate(
+            flops=4 * n * w * total, bytes_accessed=2**20 * 12, transcendentals=0
+        ),
+        name=name,
+    )(jnp.zeros((1,), jnp.int32) if sel is None else sel, *args, *deps)
+
+
+def shared_grad_kernel(depth, rank, ha, hb, da, db, send, keep, made):
+    made[...] = (dot_tn(ha[...], da[...]) + dot_tn(hb[...], db[...])).astype(BF16)
+    sq, count = depth // QUARTERS, made.shape[0] // depth
+    for j, distance in enumerate(DISTANCE):
+        to = send if j < 2 else keep
+        for d in range(count):
+            at = pl.multiple_of(d * depth + (rank[0] ^ distance) * sq, sq)
+            start = ((j % 2) * count + d) * sq
+            to[start : start + sq] = made[pl.ds(at, sq)]
+
+
+def shared_grads(depth, rank, h, ds):
+    n, w = h[0].shape
+    cols = ds[0].shape[1]
+    send, keep = call(
+        functools.partial(shared_grad_kernel, depth),
+        "shared_grads",
+        [SCALAR] + [whole((n, w))] * 2 + [whole((n, cols))] * 2,
+        [sds((w // 2, cols), BF16)] * 2,
+        4 * n * w * cols,
+        [pltpu.VMEM((w, cols), BF16)],
+    )(rank, *hbm(tuple(h)), *hbm(tuple(ds)))
+    got = swap(send, "tensor", 1)
+    half = w // 4
+    far = swap((keep[half:].astype(F32) + got[half:].astype(F32)).astype(BF16), "tensor", 2)
+    return keep, got, far
+
+
+def gate(v, *deps):
+    return pl.pallas_call(
+        lambda *refs: None,
+        in_specs=[pl.BlockSpec(memory_space=pl.ANY)] * (1 + len(deps)),
+        out_specs=pl.BlockSpec(memory_space=pl.ANY),
+        out_shape=far_out(v.shape, v.dtype),
+        input_output_aliases={0: 0},
+        name="gate",
+    )(hbm(v), *deps)
+
+
+def finish_kernel(a0, a1, b0, b1, gu, down, q, gate, step, attn, ssm, kv, state):
+    sq = kv.shape[1]
+    for layer, (a, b) in enumerate(((a0, b0), (a1, b1))):
+        gu[layer] = a[:, 0:1024].astype(F32)
+        down[layer] = a[:, 1024:1536].astype(F32).T
+        q[layer] = b[:, 0:128].astype(F32)
+        gate[layer] = b[:, 128:896].astype(F32)
+        step[layer] = b[:, 896:1024].astype(F32)
+        attn[layer] = b[:, 1024:1152].astype(F32).T
+        ssm[layer] = b[:, 1152:1536].astype(F32).T
+        share = b[:, 1536:1664].astype(F32)
+        for c in range(QUARTERS):
+            to = kv if c < 2 else state
+            to[layer, :, 128 * (c % 2) : 128 * (c % 2) + 128] = share[c * sq : (c + 1) * sq]
+
+
+def finish(firsts, seconds):
+    d = firsts[0].shape[0]
     return call(
-        functools.partial(weight_grad_kernel, widths),
-        name,
-        specs,
-        [sds((w, sum(widths)), BF16)],
-        4 * n * w * sum(widths),
-        deps=deps,
-    )(*args)[0]
+        finish_kernel,
+        "finish",
+        [whole((d, 1536))] * 2 + [whole((d, 1664))] * 2,
+        [
+            sds((2, d, 1024), F32), sds((2, 512, d), F32), sds((2, d, 128), F32), sds((2, d, 768), F32),
+            sds((2, d, 128), F32), sds((2, 128, d), F32), sds((2, 384, d), F32),
+            sds((2, d // QUARTERS, 256), F32), sds((2, d // QUARTERS, 256), F32),
+        ],
+        10**6,
+    )(*firsts, *seconds)
 
 
 def chunk_terms(act, raw_step, tok, seg_row, par):
@@ -492,8 +616,8 @@
             scratch_shapes=[pltpu.VMEM((NS, 384), F32), pltpu.VMEM((8, 640), F32)],
         ),
         out_shape=[
-            sds((n, 384), BF16), sds((n, 384), BF16), sds((n, 640), BF16), sds((n, 640), BF16),
-            sds((2 * QUARTERS, NS, 384), BF16), sds((1, t), F32), sds((t, 128), BF16), sds((t, 128), BF16),
+            sds((n, 384), BF16), sds((n, 384), BF16), far_out((n, 640), BF16), far_out((n, 640), BF16),
+            far_out((2 * QUARTERS, NS, 384), BF16), sds((1, t), F32), sds((t, 128), BF16), sds((t, 128), BF16),
         ],
         compiler_params=pltpu.CompilerParams(
             dimension_semantics=("arbitrary",), vmem_limit_bytes=VMEM_BYTES
@@ -675,7 +799,7 @@
             scratch_shapes=[pltpu.VMEM((NS, 384), F32), pltpu.VMEM((3, 8, 640), F32)],
         ),
         out_shape=[
-            sds((n, 1024), BF16), sds((n, 1024), BF16), sds((n, 512), BF16), sds((n, 512), BF16),
+            far_out((n, 1024), BF16), far_out((n, 1024), BF16), far_out((n, 512), BF16), far_out((n, 512), BF16),
             sds((8, 640), F32), sds((8, 384), F32), sds((8, 128), F32),
         ],
         compiler_params=pltpu.CompilerParams(
@@ -686,7 +810,7 @@
         ),
         name="ssm_backward",
     )(
-        rank, oh, *pa, *raw, *ps, *pre, *y, states, *dyn, fac, coef, dq, dkv, tok, seg_rows, taps, par, skip, gain
+        rank, oh, *hbm(pa), *hbm(raw), *hbm(ps), *hbm(pre), *hbm(y), hbm(states), *hbm(dyn), fac, coef, dq, dkv, tok, seg_rows, taps, par, skip, gain
     )
 
 
@@ -776,7 +900,7 @@
         attend_fwd_kernel,
         "attend_forward",
         [SCALAR, whole((t, 128)), whole((t, 128)), whole((t, 8)), whole((8, t))],
-        [sds((t // 2, 128), BF16), sds((t // 2, 128), BF16), sds((t, 128), F32)],
+        [sds((t // 2, 128), BF16), sds((t // 2, 128), BF16), far_out((t, 128), F32)],
         2 * 10**9,
     )(rank, q, kv, tok, seg_rows)
 
@@ -793,7 +917,7 @@
         4 * 10**9,
         [pltpu.VMEM((t, 128), F32), pltpu.VMEM((t, 128), F32)],
         deps,
-    )(rank, q, kv, *do, lse, tok, seg_rows, cos, sin)
+    )(rank, hbm(q), hbm(kv), *do, hbm(lse), tok, seg_rows, cos, sin)
 
 
 def swap(values, axis, distance):
@@ -823,10 +947,11 @@
     return near, swap(far, "tensor", 1), own, far
 
 
-def scatter_half(send, keep):
+def scatter_half(send, keep, on_the_way):
     got = swap(send, "tensor", 1)
-    far = swap((keep[R:].astype(F32) + got[R:].astype(F32)).astype(BF16), "tensor", 2)
-    return keep, got, far
+    given = (keep[R:].astype(F32) + got[R:].astype(F32)).astype(BF16)
+    on_the_way.append(given)
+    return keep, got, swap(given, "tensor", 2)
 
 
 def gather_everywhere(own):
@@ -847,6 +972,27 @@
 
 def scatter_dp(v):
     return lax.psum_scatter(v, "dp", scatter_dimension=0, tiled=True)
+
+
+def pairs_of_dp(share):
+    size = lax.axis_size("dp")
+    return share % 128 == 0 and size % 2 == 0 and size >= 4
+
+
+def merge_kernel(a, b, o):
+    o[...] = (a[...].astype(F32) + b[...].astype(F32)).astype(BF16)
+
+
+def merge(a, b, deps):
+    return call(merge_kernel, "merge", [whole(a.shape)] * 2, [far_out(a.shape, BF16)], 10**6, deps=deps)(
+        hbm(a), hbm(b)
+    )[0]
+
+
+def scatter_lines(v):
+    size = lax.axis_size("dp")
+    lines = [[i for i in range(size) if i % 2 == s] for s in range(2)]
+    return lax.psum_scatter(v, "dp", scatter_dimension=0, tiled=True, axis_index_groups=lines)
 
 
 def pad_rows(v, rows=8):
@@ -937,7 +1083,7 @@
     tok = jnp.stack([*shifted, enters, leaves, segf, segf, segf], axis=1)
     seg_rows = jnp.broadcast_to(segf[None, :], (8, n))
 
-    residual = halves
+    residual, last_parts, sent_on = halves, [], []
     pieces = x_pieces
     saved = []
     for layer in range(LAYERS):
@@ -966,7 +1112,7 @@
         for i, o in enumerate((o0, o1)):
             m, send, keep = mix(i, rank, o, y[i], pa[i], factor, gain_row, wf)
             mixed.append(m)
-            parts.append(scatter_half(send, keep))
+            parts.append(scatter_half(send, keep, sent_on))
         gathered = []
         for i in range(2):
             x1, low = take_step(residual[i], *parts[i], gain_two)
@@ -978,20 +1124,19 @@
             h2.append(h2_i)
             gu.append(gu_i)
             act.append(act_i)
-            parts.append(scatter_half(send, keep))
+            parts.append(scatter_half(send, keep, sent_on))
         for i in range(2):
             if layer + 1 < LAYERS:
                 x2, low = take_step(middle[i], *parts[i], pad_rows(gains[layer + 1, 0:1]))
                 result.append(x2)
                 pieces.append(gather_half(low))
             else:
-                result.append(take_step(middle[i], *parts[i], None))
+                last_parts.append((middle[i], *parts[i], None))
         saved.append(
             (residual, middle, h, pa, raw, ps, y, pre, states, q_rot, kv_rot, lse, factor, mixed, h2, gu, act,
              taps, par, skip, gain_row, gain_one, gain_two, rate)
         )
         residual = result
-    output = jnp.concatenate(residual, axis=0)
 
     grad = [cotangent[0, :R], cotangent[0, R:]]
     low = list(grad)
@@ -1007,11 +1152,21 @@
             df_i, dgu_i, send, keep = ffn_back(gathered[i], gu[i], ws, deps)
             df.append(df_i)
             dgu.append(dgu_i)
-            parts.append(scatter_half(send, keep))
-        g1 = weight_grads("grads_one", [(h2, dgu), (df, act)])
+            parts.append(scatter_half(send, keep, sent_on))
+        groups = [(h2, dgu), (df, act)]
+        paired = layer == 0 and pairs_of_dp(depth)
+        if paired:
+            side = (lax.axis_index("dp") % 2).reshape(1).astype(jnp.int32)
+            given = weight_grads("grads_one_sent", groups, sent_on[-2:], depth, 1 - side)
+            kept = weight_grads("grads_one_kept", groups, (given,), depth, side)
+            sent = swap(given, "dp", 1)
+            early = [(given,), (kept,)]
+        else:
+            g1 = weight_grads("grads_one", groups, sent_on[-2:])
+            early = [(g1,), ()]
         gathered, dx1, dgain2, dgain1 = [], [], 0.0, 0.0
         for i in range(2):
-            dx, low_i, gg = back_step(grad[i], middle[i], *parts[i], gain_two, () if i else (g1,))
+            dx, low_i, gg = back_step(grad[i], middle[i], *parts[i], gain_two, early[i])
             dx1.append(dx)
             dgain2 = dgain2 + gg[0]
             gathered.append(gather_half(low_i))
@@ -1030,16 +1185,21 @@
             rank, oh, pa, raw, ps, pre, y, states, dyn, factor, coef, dq, dkv, tok, seg_rows, taps, par, skip,
             gain_row,
         )
-        groups = [(h, (da0, da1)), (h, (ds0, ds1)), (dm, mixed)]
-        deps = ()
+        groups = [(h, (da0, da1)), (dm, mixed)]
+        shared_sum = shared_grads(depth, rank, h, (ds0, ds1))
+        grads_two = functools.partial(
+            weight_grads, "grads_two", groups, shared=shared_sum, depth=depth
+        )
         if layer == 0:
-            g2 = weight_grads("grads_two", groups, (big[layer + 1][1],))
-            deps = (g2,)
-        sums = [project_in_back(da, ds, wf, wh, deps) for da, ds in ((da0, ds0), (da1, ds1))]
-        parts = [scatter_half(*v) for v in sums]
+            g2 = grads_two((big[layer + 1][1],))
+            if paired:
+                g1 = scatter_lines(merge(kept, sent, tuple(do)))
+                g2 = gate(g2, g1)
+        sums = [project_in_back(da, ds, wf, wh) for da, ds in ((da0, ds0), (da1, ds1))]
+        parts = [scatter_half(*v, sent_on) for v in sums]
         deps = ()
         if layer > 0:
-            g2 = weight_grads("grads_two", groups, (sums[0][0], sums[1][0]))
+            g2 = grads_two(sent_on[-2:])
             deps = (g2,)
         grad, low = [], []
         for i in range(2):
@@ -1055,12 +1215,13 @@
                 jnp.sum(g_chan[1].reshape(ssm_heads, PH), axis=1),
             ]
         )
-        big[layer] = (scatter_dp(g1), scatter_dp(g2))
+        big[layer] = (g1 if paired else scatter_dp(g1), scatter_dp(g2))
         small_grads[layer] = (
             jnp.concatenate([dgain1, dgain2, g_taps[:5, channels:].reshape(-1)]),
             jnp.concatenate([chan_grad.reshape(-1), head_grad.reshape(-1)]),
         )
     input_grad = jnp.concatenate(grad, axis=0)
+    output = jnp.concatenate([take_step(*v, (da0,)) for v in last_parts], axis=0)
 
     wide_small = jnp.concatenate([small_grads[l][0] for l in range(LAYERS)])
     local_small = jnp.concatenate([small_grads[l][1] for l in range(LAYERS)])
@@ -1077,29 +1238,11 @@
     grad_channel = local_small[:, : 6 * channels].reshape(LAYERS, 6, channels)
     grad_head = local_small[:, 6 * channels :].reshape(LAYERS, 3, ssm_heads)
 
-    outs = {k: [] for k in ("q", "gate", "step", "attn", "ssm", "gu", "down", "kv", "state")}
-    for layer in range(LAYERS):
-        g1, g2 = (v.astype(F32) for v in big[layer])
-        outs["gu"].append(g1[:, : 2 * hidden].reshape(depth, 2, hidden))
-        outs["down"].append(g1[:, 2 * hidden : 3 * hidden].T)
-        outs["attn"].append(g2[:, 1536:1664].T)
-        outs["ssm"].append(g2[:, 1664:2048].T)
-        outs["q"].append(g2[:, :128])
-        outs["gate"].append(g2[:, 128 : 128 + 2 * channels].reshape(depth, 2, channels))
-        outs["step"].append(g2[:, 896 : 896 + ssm_heads])
-        sh = big[layer][1][:, 1024:1536]
-        rows = sh.shape[0] // tp_size
-
-        def part(distance):
-            return lax.dynamic_slice_in_dim(sh, (tensor ^ distance) * rows, rows, 0).astype(F32)
-
-        sh = part(0) + sum(swap(part(d), "tensor", d) for d in (1, 2, 3))
-        outs["kv"].append(sh[:, :kv_cols])
-        outs["state"].append(sh[:, kv_cols:])
-    st = {k: jnp.stack(v) for k, v in outs.items()}
+    gu, down, q, gate_in, step, attn, ssm, kv, state = finish(*zip(*big))
     return (
-        output[None], input_grad[None], grad_gains, st["q"], st["kv"], st["gate"], st["state"],
-        st["step"], grad_channel, grad_conv, grad_head, st["attn"], st["ssm"], st["gu"], st["down"],
+        output[None], input_grad[None], grad_gains, q, kv, gate_in.reshape(LAYERS, depth, 2, channels),
+        state, step[:, :, :ssm_heads], grad_channel, grad_conv, grad_head, attn, ssm,
+        gu.reshape(LAYERS, depth, 2, hidden), down,
     )
 
 

time: 674 us -> 658 us (0.976)
  Pallas kernels: 173 us -> 253 us
  local copies, waits for them, and re-layouts: 141 us -> 73.2 us
  other arithmetic: 35.5 us -> 19.8 us
  waiting for transfers between devices: 219 us -> 205 us
    unnamed x593 -> x339, local copies, waits for them, and re-layouts: 110 us -> 56.7 us
    pallas_call x48, Pallas kernels: 107 us -> 151 us  [call(): return lambda *args: made(*args, *deps)]
    pallas_call x0 -> x6, Pallas kernels: none -> 35.8 us  [the longest x5 35.8 us: weight_grads(): pl.pallas_call(kernel, grid=(w // step,), in_specs=[SCALAR] + specs + [pl...]
    ppermute x114 -> x113, waiting for transfers between devices: 132 us -> 121 us  [swap(): return lax.ppermute(values, axis, [(i, i ^ distance) for i in range(size)])]
    reduce_scatter x4 -> x3, waiting for transfers between devices: 38.2 us -> 29.6 us  [scatter_dp(): return lax.psum_scatter(v, 'dp', scatter_dimension=0, tiled=True)]
    pallas_call x2, Pallas kernels: 26.9 us -> 19.8 us  [ssm_forward(): pl.pallas_call(ssm_fwd_kernel, grid_spec=pltpu.PrefetchScalarGridSpec(num...]
    ppermute x114 -> x113, starting transfers between devices: 76 us -> 78.9 us  [swap(): return lax.ppermute(values, axis, [(i, i ^ distance) for i in range(size)])]
  transfers between devices with their start and end apart: 122 -> 121, of which waited for: 42 -> 43; matrix products, arithmetic and copies ran while one was open for 10% -> 5% of each run, Pallas kernels for 25% -> 38%
where the time goes in v3:
time: 658 us; the launch traced here: 648 us
  Pallas kernels  253 us (38%)
  waiting for transfers between devices  205 us (31%)
  starting transfers between devices  80 us (12%)
  local copies, waits for them, and re-layouts  73.2 us (11%)
  other arithmetic  19.8 us (3%)
  between operations  16.8 us (3%)
    pallas_call x48, Pallas kernels, call(): return lambda *args: made(*args, *deps)  151 us
    ppermute x113, waiting for transfers between devices, swap(): return lax.ppermute(values, axis, [(i, i ^ distance) for i in range(size)])  121 us
    ppermute x113, starting transfers between devices, swap(): return lax.ppermute(values, axis, [(i, i ^ distance) for i in range(size)])  78.9 us
    unnamed x339, local copies, waits for them, and re-layouts  56.7 us
    all_gather x4, waiting for transfers between devices, gather_dp(): return lax.all_gather(v, 'dp', axis=0, tiled=True)  54.6 us
    pallas_call x2, Pallas kernels, ssm_backward(): pl.pallas_call(lambda r, *refs: ssm_bwd_kernel(r, *refs), grid_spec=pltpu...  46.2 us
    pallas_call x5, Pallas kernels, weight_grads(): pl.pallas_call(kernel, grid=(w // step,), in_specs=[SCALAR] + specs + [pl...  35.8 us
    reduce_scatter x3, waiting for transfers between devices, scatter_dp(): return lax.psum_scatter(v, 'dp', scatter_dimension=0, tiled=True)  29.6 us
  transfers between devices with their start and end apart: 121, of which 43 were waited for; matrix products, arithmetic and copies ran while one was open for 5% of the time, Pallas kernels for 38%

profile of v3, /device:TPU:0, one launch (start us, length us, event | category | flops | bytes accessed | tf_op | source)
XLA Modules:
  0.0 647.7 jit_solution(6951710637631098847)
XLA Ops:
  39.5 45.2 %all-gather.5.cloned.1.call-done.w_in.w_mix = bf16[1024,1792]{1,0:T(8,128)(2,1)} async-done(((bf16[128,1792]{1,0:T(8,128)(2,1)}), bf16[1024,1792]{1,0:T(8,128)(2,1)}) %all-gather.5.cloned.1.call-update) | async-done | bytes 3670032 | tf_op jit(solution)/shard_map/all_gather | solution.py:970
  88.3 4.6 collective-permute-done.9.refs_2_
  96.6 3.5 project_in.4
  101.0 3.5 project_in.5
  104.6 9.9 %ssm_forward.2 = (bf16[512,384]{1,0:T(8,128)(2,1)S(1)}, bf16[512,384]{1,0:T(8,128)(2,1)S(1)}, bf16[512,640]{1,0:T(8,128)(2,1)}, bf16[512,640]{1,0:T(8,128)(2,1)}...) custom-call(s32[1]{0:T(128)} %bitcast.1.rank.r, ...), custom_call_target="tpu_custom_call" | custom-call | flops 4000000000 | bytes 20971520 | tf_op jit(solution)/shard_map/ssm_forward/pallas_call | solution.py:602
  116.8 4.6 attend_forward.2
  133.4 6.0 collective-permute-done.18.far
  151.1 4.2 collective-permute-done.33.p3
  157.4 3.7 ffn.4
  163.0 3.6 ffn.5
  170.8 5.3 collective-permute-done.23.far
  187.9 5.2 collective-permute-done.25.p3
  194.0 4.3 collective-permute-done.38.p3
  198.2 9.4 %all-gather.9.cloned.1.call-done.w_in.w_mix = bf16[1024,1536]{1,0:T(8,128)(2,1)} async-done(((bf16[128,1536]{1,0:T(8,128)(2,1)}), bf16[1024,1536]{1,0:T(8,128)(2,1)}) %all-gather.9.cloned.1.call-update) | async-done | bytes 3145744 | tf_op jit(solution)/shard_map/all_gather | solution.py:970
  209.5 4.1 project_in.6
  213.6 4.9 project_in.7
  218.5 9.9 %ssm_forward.3 = (bf16[512,384]{1,0:T(8,128)(2,1)S(1)}, bf16[512,384]{1,0:T(8,128)(2,1)S(1)}, bf16[512,640]{1,0:T(8,128)(2,1)}, bf16[512,640]{1,0:T(8,128)(2,1)}...) custom-call(s32[1]{0:T(128)} %bitcast.1.rank.r, ...), custom_call_target="tpu_custom_call" | custom-call | flops 4000000000 | bytes 20971520 | tf_op jit(solution)/shard_map/ssm_forward/pallas_call | solution.py:602
  231.8 4.6 attend_forward.3
  242.4 6.4 collective-permute-done.44.far
  261.4 5.2 collective-permute-done.51.p3
  268.1 4.2 collective-permute-done.58.p3
  276.1 3.8 ffn.6
  280.5 3.7 ffn_back.4
  284.3 3.6 ffn.7
  290.4 3.7 ffn_back.5
  297.0 7.5 %grads_one.1.refs_6_ = bf16[1024,1536]{1,0:T(8,128)(2,1)} custom-call(s32[1]{0:T(128)} %constant.65.clone.1.sel_ref, bf16[512,1024]{1,0:T(8,128)(2,1)} %get-tuple-element.245.refs_0_, bf16[512,1024]{1,0:T(8,128)(2,1)} %get-tuple-element.252.refs_1_, bf16[512,1024]{1,0:T(8,128)(2,1)} %get-tuple-element.253.refs_2_, ...), custom_call_target="tpu_custom_call" | custom-call | flops 3221225472 | bytes 12582912 | tf_op jit(solution)/shard_map/grads_one/pallas_call | solution.py:412
  306.7 7.3 %collective-permute-done.54.refs_4_ = bf16[128,1024]{1,0:T(8,128)(2,1)S(1)} collective-permute-done((bf16[128,1024]{1,0:T(8,128)(2,1)}, bf16[128,1024]{1,0:T(8,128)(2,1)S(1)}, u32[]{:S(2)}, u32[]{:S(2)}) %collective-permute-start.54) | collective-permute-done | bytes 262176 | tf_op jit(solution)/shard_map/ppermute | solution.py:925
  328.0 3.9 collective-permute-done.69.p3
  343.7 7.3 %attend_backward.2 = (bf16[1024,128]{1,0:T(8,128)(2,1)S(1)}, bf16[1024,128]{1,0:T(8,128)(2,1)S(1)}) custom-call(s32[1]{0:T(128)} %bitcast.1.rank.r, bf16[1024,128]{1,0:T(8,128)(2,1)} %copy-done.86, bf16[1024,128]{1,0:T(8,128)(2,1)} %copy-done.87, bf16[512,128]{1,0:T(8,128)(2,1)S(1)} %get-tuple-element.273.do0, bf16[512,128]{1,0:T(8,128)(2,1)S(1)} %get-tuple-element.274.do1, ...), custom_call_target="tpu_custom_call" | custom-call | flops 4000000000 | bytes 1048576 | tf_op jit(solution)/shard_map/attend_backward/pallas_call | solution.py:115
  351.1 23.2 %ssm_backward.2 = (bf16[512,1024]{1,0:T(8,128)(2,1)}, bf16[512,1024]{1,0:T(8,128)(2,1)}, bf16[512,512]{1,0:T(8,128)(2,1)}, bf16[512,512]{1,0:T(8,128)(2,1)}, f32...) custom-call(s32[1]{0:T(128)} %bitcast.1.rank.r, s32[1]{0:T(128)} %bitcast.2.oh.refs_0_, ...), custom_call_target="tpu_custom_call" | custom-call | flops 8000000000 | bytes 31457280 | tf_op jit(solution)/shard_map/ssm_backward/pallas_call | solution.py:781
  387.5 6.0 collective-permute-done.77.refs_10_
  393.6 7.5 %grads_two.2.refs_6_ = bf16[1024,1664]{1,0:T(8,128)(2,1)} custom-call(s32[1]{0:T(128)} %constant.65.clone.1.sel_ref, bf16[512,1024]{1,0:T(8,128)(2,1)} %get-tuple-element.282.ha.refs_0_, bf16[512,1024]{1,0:T(8,128)(2,1)} %get-tuple-element.283.hb.refs_1_, bf16[512,1024]{1,0:T(8,128)(2,1)} %get-tuple-element.278.da.refs_2_, ...), custom_call_target="tpu_custom_call" | custom-call | flops 3489660928 | bytes 12582912 | tf_op jit(solution)/shard_map/grads_two/pallas_call | solution.py:412
  403.4 7.2 %collective-permute-done.75.refs_4_ = bf16[128,1024]{1,0:T(8,128)(2,1)S(1)} collective-permute-done((bf16[128,1024]{1,0:T(8,128)(2,1)S(1)}, bf16[128,1024]{1,0:T(8,128)(2,1)S(1)}, u32[]{:S(2)}, u32[]{:S(2)}) %collective-permute-start.75) | collective-permute-done | bytes 262176 | tf_op jit(solution)/shard_map/ppermute | solution.py:925
  424.8 3.4 collective-permute-done.86.refs_3_
  429.9 4.4 ffn_back.6
  435.6 4.4 ffn_back.7
  444.2 6.5 %grads_one_sent.1.refs_6_.refs_8_ = bf16[512,1536]{1,0:T(8,128)(2,1)} custom-call(s32[1]{0:T(128)S(6)} %sub.16.sel_ref, bf16[512,1024]{1,0:T(8,128)(2,1)} %get-tuple-element.299.refs_0_, bf16[512,1024]{1,0:T(8,128)(2,1)} %get-tuple-element.300.refs_1_, bf16[512,1024]{1,0:T(8,128)(2,1)} %get-tuple-element.301.refs_2_, ...), custom_call_target="tpu_custom_call" | custom-call | flops 3221225472 | bytes 12582912 | tf_op jit(solution)/shard_map/grads_one_sent/pallas_call | solution.py:412
  453.4 7.2 %collective-permute-done.83.refs_4_ = bf16[128,1024]{1,0:T(8,128)(2,1)S(1)} collective-permute-done((bf16[128,1024]{1,0:T(8,128)(2,1)S(1)}, bf16[128,1024]{1,0:T(8,128)(2,1)S(1)}, u32[]{:S(2)}, u32[]{:S(2)}) %collective-permute-start.83) | collective-permute-done | bytes 262176 | tf_op jit(solution)/shard_map/ppermute | solution.py:925
  466.7 6.4 grads_one_kept.1.refs_6_.refs_0_
  479.9 4.3 collective-permute-done.94.p3
  492.2 3.3 mix_back.7
  495.6 3.5 merge.1
  501.6 7.4 %attend_backward.3 = (bf16[1024,128]{1,0:T(8,128)(2,1)S(1)}, bf16[1024,128]{1,0:T(8,128)(2,1)S(1)}) custom-call(s32[1]{0:T(128)} %bitcast.1.rank.r, bf16[1024,128]{1,0:T(8,128)(2,1)} %copy-done.84, bf16[1024,128]{1,0:T(8,128)(2,1)} %copy-done.85, bf16[512,128]{1,0:T(8,128)(2,1)S(1)} %get-tuple-element.319.do0.refs_2_, ...), custom_call_target="tpu_custom_call" | custom-call | flops 4000000000 | bytes 1048576 | tf_op jit(solution)/shard_map/attend_backward/pallas_call | solution.py:115
  509.0 23.0 %ssm_backward.3 = (bf16[512,1024]{1,0:T(8,128)(2,1)}, bf16[512,1024]{1,0:T(8,128)(2,1)}, bf16[512,512]{1,0:T(8,128)(2,1)}, bf16[512,512]{1,0:T(8,128)(2,1)}, f32...) custom-call(s32[1]{0:T(128)} %bitcast.1.rank.r, s32[1]{0:T(128)} %bitcast.2.oh.refs_0_, ...), custom_call_target="tpu_custom_call" | custom-call | flops 8000000000 | bytes 31457280 | tf_op jit(solution)/shard_map/ssm_backward/pallas_call | solution.py:781
  541.4 3.9 project_in_back.7
  547.6 7.8 %grads_two.3.refs_0_ = bf16[1024,1664]{1,0:T(8,128)(2,1)} custom-call(s32[1]{0:T(128)} %constant.65.clone.1.sel_ref, bf16[512,1024]{1,0:T(8,128)(2,1)} %get-tuple-element.352.ha.refs_0_, bf16[512,1024]{1,0:T(8,128)(2,1)} %get-tuple-element.353.hb.refs_1_, bf16[512,1024]{1,0:T(8,128)(2,1)} %get-tuple-element.324.refs_4_.da.refs_2_, ...), custom_call_target="tpu_custom_call" | custom-call | flops 3489660928 | bytes 12582912 | tf_op jit(solution)/shard_map/grads_two/pallas_call | solution.py:412
  566.4 5.7 collective-permute-done.104.far
  604.8 29.6 %reduce-scatter.11.cloned.1.call-done.b0 = bf16[128,1664]{1,0:T(8,128)(2,1)} async-done(((bf16[1024,1664]{1,0:T(8,128)(2,1)}), bf16[128,1664]{1,0:T(8,128)(2,1)}) %reduce-scatter.11.cloned.1.call-update) | async-done | bytes 426000 | tf_op jit(solution)/shard_map/reduce_scatter | solution.py:974
  (752 shorter events, 273.1 us)
Async XLA Ops:
  7.2 77.6 %all-gather.5.cloned.1.call-start = ((), (), s32[]{:S(2)}) async-start(), calls=%async_computation.4 | async-start | bytes 4128768 | tf_op jit(solution)/shard_map/all_gather | solution.py:970
  15.0 140.4 %all-gather.7.cloned.1.call-start = ((), (), s32[]{:S(2)}) async-start(), calls=%async_computation.5 | async-start | bytes 3538944 | tf_op jit(solution)/shard_map/all_gather | solution.py:970
  17.1 190.5 %all-gather.9.cloned.1.call-start = ((), (), s32[]{:S(2)}) async-start(), calls=%async_computation.6 | async-start | bytes 3538944 | tf_op jit(solution)/shard_map/all_gather | solution.py:970
  17.9 75.4 %collective-permute-start = (bf16[128,1024]{1,0:T(8,128)(2,1)S(1)}, bf16[128,1024]{1,0:T(8,128)(2,1)}, u32[]{:S(2)}, u32[]{:S(2)}) collective-permute-start(bf16[128,1024]{1,0:T(8,128)(2,1)S(1)} %get-tuple-element.452.p2.x.v), channel_id=1, source_target_pairs={{0,1},{1,0},{2,3},{3,2},{4,5},{5,4},{6,7},{7,6},{8,9},{9,8},{10,11... | collective-permute-start | bytes 786440 | tf_op jit(solution)/shard_map/ppermute | solution.py:925
  18.4 69.3 %collective-permute-start.1 = (bf16[128,1024]{1,0:T(8,128)(2,1)S(1)}, bf16[128,1024]{1,0:T(8,128)(2,1)}, u32[]{:S(2)}, u32[]{:S(2)}) collective-permute-start(bf16[128,1024]{1,0:T(8,128)(2,1)S(1)} %get-tuple-element.452.p2.x.v), channel_id=1, source_target_pairs={{0,2},{1,3},{2,0},{3,1},{4,6},{5,7},{6,4},{7,5},{8,10},{9,11},{10,... | collective-permute-start | bytes 786440 | tf_op jit(solution)/shard_map/ppermute | solution.py:925
  22.7 71.2 %collective-permute-start.12 = (bf16[128,1024]{1,0:T(8,128)(2,1)}, bf16[128,1024]{1,0:T(8,128)(2,1)}, u32[]{:S(2)}, u32[]{:S(2)}) collective-permute-start(bf16[128,1024]{1,0:T(8,128)(2,1)} %get-tuple-element.453.p2.x.v), channel_id=1, source_target_pairs={{0,2},{1,3},{2,0},{3,1},{4,6},{5,7},{6,4},{7,5},{8,10},{9,11},{10,... | collective-permute-start | bytes 786440 | tf_op jit(solution)/shard_map/ppermute | solution.py:925
  24.4 249.8 %all-gather.11.cloned.1.call-start = ((), (), s32[]{:S(2)}) async-start(), calls=%async_computation.7 | async-start | bytes 3538944 | tf_op jit(solution)/shard_map/all_gather | solution.py:970
  38.0 49.4 %collective-permute-start.7 = (bf16[8,2,208]{2,1,0:T(2,128)(2,1)S(1)}, bf16[8,2,208]{2,1,0:T(2,128)(2,1)S(1)}, u32[]{:S(2)}, u32[]{:S(2)}) collective-permute-start(bf16[8,2,208]{2,1,0:T(2,128)(2,1)S(1)} %pad_maximum_fusion.7), channel_id=1, source_target_pairs={{0,2},{1,3},{2,0},{3,1},{4,6},{5,7},{6,4},{7,5},{8,10},{9,11},{10,... | collective-permute-start | bytes 19976 | tf_op jit(solution)/shard_map/ppermute | solution.py:925
  128.7 300.2 %reduce-scatter.5.cloned.1.call-start = ((), (), s32[]{:S(2)}) async-start(), calls=%async_computation.8 | async-start | bytes 3538944 | tf_op jit(solution)/shard_map/reduce_scatter | solution.py:974
  132.8 12.2 %collective-permute-start.31 = (bf16[128,1024]{1,0:T(8,128)(2,1)S(1)}, bf16[128,1024]{1,0:T(8,128)(2,1)S(1)}, u32[]{:S(2)}, u32[]{:S(2)}) collective-permute-start(bf16[128,1024]{1,0:T(8,128)(2,1)S(1)} %add_convert_fusion.15), channel_id=1, source_target_pairs={{0,2},{1,3},{2,0},{3,1},{4,6},{5,7},{6,4},{7,5},{8,10},{9,11},{10,... | collective-permute-start | bytes 786440 | tf_op jit(solution)/shard_map/ppermute | solution.py:925
  150.6 11.0 %collective-permute-start.32 = (bf16[128,1024]{1,0:T(8,128)(2,1)S(1)}, bf16[128,1024]{1,0:T(8,128)(2,1)S(1)}, u32[]{:S(2)}, u32[]{:S(2)}) collective-permute-start(bf16[128,1024]{1,0:T(8,128)(2,1)S(1)} %get-tuple-element.218.p2), channel_id=1, source_target_pairs={{0,1},{1,0},{2,3},{3,2},{4,5},{5,4},{6,7},{7,6},{8,9},{9,8},{10,11... | collective-permute-start | bytes 786440 | tf_op jit(solution)/shard_map/ppermute | solution.py:925
  168.7 13.0 %collective-permute-start.36 = (bf16[128,1024]{1,0:T(8,128)(2,1)S(1)}, bf16[128,1024]{1,0:T(8,128)(2,1)S(1)}, u32[]{:S(2)}, u32[]{:S(2)}) collective-permute-start(bf16[128,1024]{1,0:T(8,128)(2,1)S(1)} %add_convert_fusion.14), channel_id=1, source_target_pairs={{0,2},{1,3},{2,0},{3,1},{4,6},{5,7},{6,4},{7,5},{8,10},{9,11},{10,... | collective-permute-start | bytes 786440 | tf_op jit(solution)/shard_map/ppermute | solution.py:925
  170.4 17.0 %collective-permute-start.28 = (bf16[1024,128]{1,0:T(8,128)(2,1)S(1)}, bf16[1024,128]{1,0:T(8,128)(2,1)S(1)}, u32[]{:S(2)}, u32[]{:S(2)}) collective-permute-start(bf16[1024,128]{1,0:T(8,128)(2,1)S(1)} %get-tuple-element.446.refs_0_), channel_id=1, source_target_pairs={{0,2},{1,3},{2,0},{3,1},{4,6},{5,7},{6,4},{7,5},{8,10},{9,11},{10,... | collective-permute-start | bytes 786440 | tf_op jit(solution)/shard_map/ppermute | solution.py:925
  179.0 14.0 %collective-permute-start.25 = (bf16[128,1024]{1,0:T(8,128)(2,1)S(1)}, bf16[128,1024]{1,0:T(8,128)(2,1)}, u32[]{:S(2)}, u32[]{:S(2)}) collective-permute-start(bf16[128,1024]{1,0:T(8,128)(2,1)S(1)} %get-tuple-element.211.p2), channel_id=1, source_target_pairs={{0,2},{1,3},{2,0},{3,1},{4,6},{5,7},{6,4},{7,5},{8,10},{9,11},{10,... | collective-permute-start | bytes 786440 | tf_op jit(solution)/shard_map/ppermute | solution.py:925
  180.7 12.7 %collective-permute-start.27 = (bf16[1024,128]{1,0:T(8,128)(2,1)S(1)}, bf16[1024,128]{1,0:T(8,128)(2,1)S(1)}, u32[]{:S(2)}, u32[]{:S(2)}) collective-permute-start(bf16[1024,128]{1,0:T(8,128)(2,1)S(1)} %get-tuple-element.446.refs_0_), channel_id=1, source_target_pairs={{0,1},{1,0},{2,3},{3,2},{4,5},{5,4},{6,7},{7,6},{8,9},{9,8},{10,11... | collective-permute-start | bytes 786440 | tf_op jit(solution)/shard_map/ppermute | solution.py:925
  184.6 13.6 %collective-permute-start.38 = (bf16[128,1024]{1,0:T(8,128)(2,1)S(1)}, bf16[128,1024]{1,0:T(8,128)(2,1)}, u32[]{:S(2)}, u32[]{:S(2)}) collective-permute-start(bf16[128,1024]{1,0:T(8,128)(2,1)S(1)} %get-tuple-element.221.p2), channel_id=1, source_target_pairs={{0,2},{1,3},{2,0},{3,1},{4,6},{5,7},{6,4},{7,5},{8,10},{9,11},{10,... | collective-permute-start | bytes 786440 | tf_op jit(solution)/shard_map/ppermute | solution.py:925
  187.4 20.3 %collective-permute-start.29 = (bf16[1024,128]{1,0:T(8,128)(2,1)S(1)}, bf16[1024,128]{1,0:T(8,128)(2,1)S(1)}, u32[]{:S(2)}, u32[]{:S(2)}) collective-permute-start(bf16[1024,128]{1,0:T(8,128)(2,1)S(1)} %collective-permute-done.28.refs_2_), channel_id=1, source_target_pairs={{0,1},{1,0},{2,3},{3,2},{4,5},{5,4},{6,7},{7,6},{8,9},{9,8},{10,11... | collective-permute-start | bytes 786440 | tf_op jit(solution)/shard_map/ppermute | solution.py:925
  187.4 20.3 %collective-permute-start.24 = (bf16[128,1024]{1,0:T(8,128)(2,1)S(1)}, bf16[128,1024]{1,0:T(8,128)(2,1)}, u32[]{:S(2)}, u32[]{:S(2)}) collective-permute-start(bf16[128,1024]{1,0:T(8,128)(2,1)S(1)} %get-tuple-element.211.p2), channel_id=1, source_target_pairs={{0,1},{1,0},{2,3},{3,2},{4,5},{5,4},{6,7},{7,6},{8,9},{9,8},{10,11... | collective-permute-start | bytes 786440 | tf_op jit(solution)/shard_map/ppermute | solution.py:925
  193.1 14.5 %collective-permute-start.26 = (bf16[128,1024]{1,0:T(8,128)(2,1)}, bf16[128,1024]{1,0:T(8,128)(2,1)}, u32[]{:S(2)}, u32[]{:S(2)}) collective-permute-start(bf16[128,1024]{1,0:T(8,128)(2,1)} %collective-permute-done.25.p3), channel_id=1, source_target_pairs={{0,1},{1,0},{2,3},{3,2},{4,5},{5,4},{6,7},{7,6},{8,9},{9,8},{10,11... | collective-permute-start | bytes 786440 | tf_op jit(solution)/shard_map/ppermute | solution.py:925
  193.4 20.2 %collective-permute-start.37 = (bf16[128,1024]{1,0:T(8,128)(2,1)S(1)}, bf16[128,1024]{1,0:T(8,128)(2,1)}, u32[]{:S(2)}, u32[]{:S(2)}) collective-permute-start(bf16[128,1024]{1,0:T(8,128)(2,1)S(1)} %get-tuple-element.221.p2), channel_id=1, source_target_pairs={{0,1},{1,0},{2,3},{3,2},{4,5},{5,4},{6,7},{7,6},{8,9},{9,8},{10,11... | collective-permute-start | bytes 786440 | tf_op jit(solution)/shard_map/ppermute | solution.py:925
  198.2 15.4 %collective-permute-start.39 = (bf16[128,1024]{1,0:T(8,128)(2,1)}, bf16[128,1024]{1,0:T(8,128)(2,1)}, u32[]{:S(2)}, u32[]{:S(2)}) collective-permute-start(bf16[128,1024]{1,0:T(8,128)(2,1)} %collective-permute-done.38.p3), channel_id=1, source_target_pairs={{0,1},{1,0},{2,3},{3,2},{4,5},{5,4},{6,7},{7,6},{8,9},{9,8},{10,11... | collective-permute-start | bytes 786440 | tf_op jit(solution)/shard_map/ppermute | solution.py:925
  241.2 13.4 %collective-permute-start.56 = (bf16[128,1024]{1,0:T(8,128)(2,1)S(1)}, bf16[128,1024]{1,0:T(8,128)(2,1)S(1)}, u32[]{:S(2)}, u32[]{:S(2)}) collective-permute-start(bf16[128,1024]{1,0:T(8,128)(2,1)S(1)} %add_convert_fusion.10), channel_id=1, source_target_pairs={{0,2},{1,3},{2,0},{3,1},{4,6},{5,7},{6,4},{7,5},{8,10},{9,11},{10,... | collective-permute-start | bytes 786440 | tf_op jit(solution)/shard_map/ppermute | solution.py:925
  254.0 12.7 %collective-permute-start.51 = (bf16[128,1024]{1,0:T(8,128)(2,1)}, bf16[128,1024]{1,0:T(8,128)(2,1)}, u32[]{:S(2)}, u32[]{:S(2)}) collective-permute-start(bf16[128,1024]{1,0:T(8,128)(2,1)} %get-tuple-element.449.p2.refs_0_), channel_id=1, source_target_pairs={{0,2},{1,3},{2,0},{3,1},{4,6},{5,7},{6,4},{7,5},{8,10},{9,11},{10,... | collective-permute-start | bytes 786440 | tf_op jit(solution)/shard_map/ppermute | solution.py:925
  257.5 14.7 %collective-permute-start.58 = (bf16[128,1024]{1,0:T(8,128)(2,1)}, bf16[128,1024]{1,0:T(8,128)(2,1)}, u32[]{:S(2)}, u32[]{:S(2)}) collective-permute-start(bf16[128,1024]{1,0:T(8,128)(2,1)} %get-tuple-element.251.p2), channel_id=1, source_target_pairs={{0,2},{1,3},{2,0},{3,1},{4,6},{5,7},{6,4},{7,5},{8,10},{9,11},{10,... | collective-permute-start | bytes 786440 | tf_op jit(solution)/shard_map/ppermute | solution.py:925
  259.0 13.3 %collective-permute-start.45 = (bf16[128,1024]{1,0:T(8,128)(2,1)S(1)}, bf16[128,1024]{1,0:T(8,128)(2,1)S(1)}, u32[]{:S(2)}, u32[]{:S(2)}) collective-permute-start(bf16[128,1024]{1,0:T(8,128)(2,1)S(1)} %get-tuple-element.236.p2), channel_id=1, source_target_pairs={{0,1},{1,0},{2,3},{3,2},{4,5},{5,4},{6,7},{7,6},{8,9},{9,8},{10,11... | collective-permute-start | bytes 786440 | tf_op jit(solution)/shard_map/ppermute | solution.py:925
  260.9 11.9 %collective-permute-start.47 = (bf16[128,1024]{1,0:T(8,128)(2,1)S(1)}, bf16[128,1024]{1,0:T(8,128)(2,1)S(1)}, u32[]{:S(2)}, u32[]{:S(2)}) collective-permute-start(bf16[128,1024]{1,0:T(8,128)(2,1)S(1)} %collective-permute-done.46.p3), channel_id=1, source_target_pairs={{0,1},{1,0},{2,3},{3,2},{4,5},{5,4},{6,7},{7,6},{8,9},{9,8},{10,11... | collective-permute-start | bytes 786440 | tf_op jit(solution)/shard_map/ppermute | solution.py:925
  260.9 19.0 %collective-permute-start.50 = (bf16[128,1024]{1,0:T(8,128)(2,1)}, bf16[128,1024]{1,0:T(8,128)(2,1)}, u32[]{:S(2)}, u32[]{:S(2)}) collective-permute-start(bf16[128,1024]{1,0:T(8,128)(2,1)} %get-tuple-element.449.p2.refs_0_), channel_id=1, source_target_pairs={{0,1},{1,0},{2,3},{3,2},{4,5},{5,4},{6,7},{7,6},{8,9},{9,8},{10,11... | collective-permute-start | bytes 786440 | tf_op jit(solution)/shard_map/ppermute | solution.py:925
  266.6 13.4 %collective-permute-start.61 = (bf16[128,1024]{1,0:T(8,128)(2,1)}, bf16[128,1024]{1,0:T(8,128)(2,1)}, u32[]{:S(2)}, u32[]{:S(2)}) collective-permute-start(bf16[128,1024]{1,0:T(8,128)(2,1)} %get-tuple-element.448.p2.g), channel_id=1, source_target_pairs={{0,2},{1,3},{2,0},{3,1},{4,6},{5,7},{6,4},{7,5},{8,10},{9,11},{10,... | collective-permute-start | bytes 786440 | tf_op jit(solution)/shard_map/ppermute | solution.py:925
  272.3 12.1 %collective-permute-start.57 = (bf16[128,1024]{1,0:T(8,128)(2,1)}, bf16[128,1024]{1,0:T(8,128)(2,1)}, u32[]{:S(2)}, u32[]{:S(2)}) collective-permute-start(bf16[128,1024]{1,0:T(8,128)(2,1)} %get-tuple-element.251.p2), channel_id=1, source_target_pairs={{0,1},{1,0},{2,3},{3,2},{4,5},{5,4},{6,7},{7,6},{8,9},{9,8},{10,11... | collective-permute-start | bytes 786440 | tf_op jit(solution)/shard_map/ppermute | solution.py:925
  273.7 10.6 %collective-permute-start.59 = (bf16[128,1024]{1,0:T(8,128)(2,1)}, bf16[128,1024]{1,0:T(8,128)(2,1)}, u32[]{:S(2)}, u32[]{:S(2)}) collective-permute-start(bf16[128,1024]{1,0:T(8,128)(2,1)} %collective-permute-done.58.p3), channel_id=1, source_target_pairs={{0,1},{1,0},{2,3},{3,2},{4,5},{5,4},{6,7},{7,6},{8,9},{9,8},{10,11... | collective-permute-start | bytes 786440 | tf_op jit(solution)/shard_map/ppermute | solution.py:925
  279.9 9.7 %collective-permute-start.60 = (bf16[128,1024]{1,0:T(8,128)(2,1)}, bf16[128,1024]{1,0:T(8,128)(2,1)S(1)}, u32[]{:S(2)}, u32[]{:S(2)}) collective-permute-start(bf16[128,1024]{1,0:T(8,128)(2,1)} %get-tuple-element.448.p2.g), channel_id=1, source_target_pairs={{0,1},{1,0},{2,3},{3,2},{4,5},{5,4},{6,7},{7,6},{8,9},{9,8},{10,11... | collective-permute-start | bytes 786440 | tf_op jit(solution)/shard_map/ppermute | solution.py:925
  284.2 10.3 %collective-permute-start.53 = (bf16[256,1024]{1,0:T(8,128)(2,1)S(1)}, bf16[256,1024]{1,0:T(8,128)(2,1)S(1)}, u32[]{:S(2)}, u32[]{:S(2)}) collective-permute-start(bf16[256,1024]{1,0:T(8,128)(2,1)S(1)} %get-tuple-element.244), channel_id=1, source_target_pairs={{0,1},{1,0},{2,3},{3,2},{4,5},{5,4},{6,7},{7,6},{8,9},{9,8},{10,11... | collective-permute-start | bytes 1572872 | tf_op jit(solution)/shard_map/ppermute | solution.py:925
  304.5 240.8 %reduce-scatter.9.cloned.1.call-start = ((), (), s32[]{:S(2)}) async-start(), calls=%async_computation.10 | async-start | bytes 3833856 | tf_op jit(solution)/shard_map/reduce_scatter | solution.py:974
  306.1 14.5 %collective-permute-start.67 = (bf16[128,1024]{1,0:T(8,128)(2,1)}, bf16[128,1024]{1,0:T(8,128)(2,1)S(1)}, u32[]{:S(2)}, u32[]{:S(2)}) collective-permute-start(bf16[128,1024]{1,0:T(8,128)(2,1)} %copy-done.68), channel_id=1, source_target_pairs={{0,2},{1,3},{2,0},{3,1},{4,6},{5,7},{6,4},{7,5},{8,10},{9,11},{10,... | collective-permute-start | bytes 786440 | tf_op jit(solution)/shard_map/ppermute | solution.py:925
  341.4 9.6 %collective-permute-start.73 = (f32[1,1024]{1,0:T(1,128)S(1)}, f32[1,1024]{1,0:T(1,128)S(1)}, u32[]{:S(2)}, u32[]{:S(2)}) collective-permute-start(f32[1,1024]{1,0:T(1,128)S(1)} %constant_dynamic-update-slice_fusion.12), channel_id=1, source_target_pairs={{0,3},{1,2},{2,1},{3,0},{4,7},{5,6},{6,5},{7,4},{8,11},{9,10},{10,... | collective-permute-start | bytes 12296 | tf_op jit(solution)/shard_map/ppermute | solution.py:925
  401.1 154.3 %reduce-scatter.7.cloned.1.call-start = ((), (), s32[]{:S(2)}) async-start(), calls=%async_computation.9 | async-start | bytes 1966080 | tf_op jit(solution)/shard_map/reduce_scatter | solution.py:995
  402.9 14.6 %collective-permute-start.84 = (bf16[128,1024]{1,0:T(8,128)(2,1)}, bf16[128,1024]{1,0:T(8,128)(2,1)S(1)}, u32[]{:S(2)}, u32[]{:S(2)}) collective-permute-start(bf16[128,1024]{1,0:T(8,128)(2,1)} %add_convert_fusion.6.refs_12_), channel_id=1, source_target_pairs={{0,2},{1,3},{2,0},{3,1},{4,6},{5,7},{6,4},{7,5},{8,10},{9,11},{10,... | collective-permute-start | bytes 786440 | tf_op jit(solution)/shard_map/ppermute | solution.py:925
  424.3 11.4 %collective-permute-start.85 = (bf16[128,1024]{1,0:T(8,128)(2,1)}, bf16[128,1024]{1,0:T(8,128)(2,1)}, u32[]{:S(2)}, u32[]{:S(2)}) collective-permute-start(bf16[128,1024]{1,0:T(8,128)(2,1)} %get-tuple-element.303.refs_2_), channel_id=1, source_target_pairs={{0,1},{1,0},{2,3},{3,2},{4,5},{5,4},{6,7},{7,6},{8,9},{9,8},{10,11... | collective-permute-start | bytes 786440 | tf_op jit(solution)/shard_map/ppermute | solution.py:925
  450.7 44.9 %collective-permute-start.110 = (bf16[512,1536]{1,0:T(8,128)(2,1)}, bf16[512,1536]{1,0:T(8,128)(2,1)}, u32[]{:S(2)}, u32[]{:S(2)}) collective-permute-start(bf16[512,1536]{1,0:T(8,128)(2,1)} %grads_one_sent.1.refs_6_.refs_8_), channel_id=1, source_target_pairs={{0,4},{4,0},{8,12},{12,8},{16,20},{20,16},{24,28},{28,24},{1,5},{5... | collective-permute-start | bytes 4718600 | tf_op jit(solution)/shard_map/ppermute | solution.py:925
  452.7 26.3 %collective-permute-start.99 = (bf16[256,1024]{1,0:T(8,128)(2,1)S(1)}, bf16[256,1024]{1,0:T(8,128)(2,1)S(1)}, u32[]{:S(2)}, u32[]{:S(2)}) collective-permute-start(bf16[256,1024]{1,0:T(8,128)(2,1)S(1)} %copy-done.71), channel_id=1, source_target_pairs={{0,1},{1,0},{2,3},{3,2},{4,5},{5,4},{6,7},{7,6},{8,9},{9,8},{10,11... | collective-permute-start | bytes 1572872 | tf_op jit(solution)/shard_map/ppermute | solution.py:925
  452.7 20.4 %collective-permute-start.92 = (bf16[128,1024]{1,0:T(8,128)(2,1)S(1)}, bf16[128,1024]{1,0:T(8,128)(2,1)S(1)}, u32[]{:S(2)}, u32[]{:S(2)}) collective-permute-start(bf16[128,1024]{1,0:T(8,128)(2,1)S(1)} %add_convert_fusion.4.refs_9_), channel_id=1, source_target_pairs={{0,2},{1,3},{2,0},{3,1},{4,6},{5,7},{6,4},{7,5},{8,10},{9,11},{10,... | collective-permute-start | bytes 786440 | tf_op jit(solution)/shard_map/ppermute | solution.py:925
  465.3 13.2 %collective-permute-start.90 = (bf16[128,1024]{1,0:T(8,128)(2,1)S(1)}, bf16[128,1024]{1,0:T(8,128)(2,1)S(1)}, u32[]{:S(2)}, u32[]{:S(2)}) collective-permute-start(bf16[128,1024]{1,0:T(8,128)(2,1)S(1)} %get-tuple-element.312.p2), channel_id=1, source_target_pairs={{0,2},{1,3},{2,0},{3,1},{4,6},{5,7},{6,4},{7,5},{8,10},{9,11},{10,... | collective-permute-start | bytes 786440 | tf_op jit(solution)/shard_map/ppermute | solution.py:925
  479.9 10.9 %collective-permute-start.93 = (bf16[128,1024]{1,0:T(8,128)(2,1)S(1)}, bf16[128,1024]{1,0:T(8,128)(2,1)S(1)}, u32[]{:S(2)}, u32[]{:S(2)}) collective-permute-start(bf16[128,1024]{1,0:T(8,128)(2,1)S(1)} %get-tuple-element.315.p2), channel_id=1, source_target_pairs={{0,1},{1,0},{2,3},{3,2},{4,5},{5,4},{6,7},{7,6},{8,9},{9,8},{10,11... | collective-permute-start | bytes 786440 | tf_op jit(solution)/shard_map/ppermute | solution.py:925
  484.3 97.9 %collective-permute-start.48 = (bf16[256,1024]{1,0:T(8,128)(2,1)}, bf16[256,1024]{1,0:T(8,128)(2,1)}, u32[]{:S(2)}, u32[]{:S(2)}) collective-permute-start(bf16[256,1024]{1,0:T(8,128)(2,1)} %get-tuple-element.238), channel_id=1, source_target_pairs={{0,1},{1,0},{2,3},{3,2},{4,5},{5,4},{6,7},{7,6},{8,9},{9,8},{10,11... | collective-permute-start | bytes 1572872 | tf_op jit(solution)/shard_map/ppermute | solution.py:925
  484.8 101.7 %collective-permute-start.100 = (bf16[128,1024]{1,0:T(8,128)(2,1)}, bf16[128,1024]{1,0:T(8,128)(2,1)}, u32[]{:S(2)}, u32[]{:S(2)}) collective-permute-start(bf16[128,1024]{1,0:T(8,128)(2,1)} %add_convert_fusion.3), channel_id=1, source_target_pairs={{0,2},{1,3},{2,0},{3,1},{4,6},{5,7},{6,4},{7,5},{8,10},{9,11},{10,... | collective-permute-start | bytes 786440 | tf_op jit(solution)/shard_map/ppermute | solution.py:925
  499.1 135.3 %reduce-scatter.11.cloned.1.call-start = ((), (), s32[]{:S(2)}) async-start(), calls=%async_computation.11 | async-start | bytes 3833856 | tf_op jit(solution)/shard_map/reduce_scatter | solution.py:974
  545.3 16.4 %collective-permute-start.103 = (bf16[256,1024]{1,0:T(8,128)(2,1)}, bf16[256,1024]{1,0:T(8,128)(2,1)}, u32[]{:S(2)}, u32[]{:S(2)}) collective-permute-start(bf16[256,1024]{1,0:T(8,128)(2,1)} %get-tuple-element.336), channel_id=1, source_target_pairs={{0,1},{1,0},{2,3},{3,2},{4,5},{5,4},{6,7},{7,6},{8,9},{9,8},{10,11... | collective-permute-start | bytes 1572872 | tf_op jit(solution)/shard_map/ppermute | solution.py:925
  565.2 12.0 %collective-permute-start.102 = (bf16[128,1024]{1,0:T(8,128)(2,1)S(1)}, bf16[128,1024]{1,0:T(8,128)(2,1)S(1)}, u32[]{:S(2)}, u32[]{:S(2)}) collective-permute-start(bf16[128,1024]{1,0:T(8,128)(2,1)S(1)} %add_convert_fusion.2), channel_id=1, source_target_pairs={{0,2},{1,3},{2,0},{3,1},{4,6},{5,7},{6,4},{7,5},{8,10},{9,11},{10,... | collective-permute-start | bytes 786440 | tf_op jit(solution)/shard_map/ppermute | solution.py:925
  (228 other events, 2295.9 us)
Sparse Core Ops, SparseCore 0:
  15.1 69.6 all-gather.4
  87.5 58.7 all-gather.6
  148.5 59.0 all-gather.8
  209.7 59.0 all-gather.10
  304.6 73.0 reduce-scatter.4
  401.3 80.4 reduce-scatter.8
  499.2 34.9 reduce-scatter.6
  555.6 78.7 reduce-scatter.10

commit v4 on v3

--- a/solution.py
+++ b/solution.py
@@ -360,7 +360,7 @@
     )(*hbm(pieces), hbm(gu), w_second, w_second)
 
 
-def weight_grad_kernel(widths, share, depth, sel, *refs):
+def weight_grad_kernel(widths, share, sel, *refs):
     out = refs[-1]
     at = 0
     for i, width in enumerate(widths):
@@ -374,21 +374,39 @@
             total = total + dot_tn(rows, right[...])
         out[:, at : at + width] = total.astype(BF16)
         at += width
-    if depth is None:
-        return
-    kept, got, far = refs[4 * len(widths) : 4 * len(widths) + 3]
+
+
+def insert_kernel(depth, base, kept, got, far, *refs):
+    out = refs[-1]
     sq = depth // QUARTERS
-    for d in range(out.shape[0] // depth):
-        start = pl.multiple_of((pl.program_id(0) * (out.shape[0] // depth) + d) * sq, sq)
-        rows = pl.ds(start, sq)
+    count = out.shape[0] // depth
+    for d in range(count):
+        rows = pl.ds(pl.multiple_of((pl.program_id(0) * count + d) * sq, sq), sq)
         total = kept[rows].astype(F32) + got[rows].astype(F32) + far[rows].astype(F32)
         for c in range(QUARTERS):
-            out[d * depth + c * sq : d * depth + (c + 1) * sq, at:] = total[
+            out[d * depth + c * sq : d * depth + (c + 1) * sq] = total[
                 :, 128 * c : 128 * c + 128
             ].astype(BF16)
 
 
-def weight_grads(name, groups, deps=(), share=None, sel=None, shared=None, depth=None):
+def insert_shared(made, shared, depth, deps=()):
+    w, total = made.shape
+    keep_in_place = pl.BlockSpec(memory_space=pl.ANY)
+    return pl.pallas_call(
+        functools.partial(insert_kernel, depth),
+        grid=(w // 512,),
+        in_specs=[keep_in_place] + [whole(shared[2].shape)] * 3 + [keep_in_place] * len(deps),
+        out_specs=pl.BlockSpec((512, 128), lambda i: (i, total // 128 - 1)),
+        out_shape=far_out((w, total), BF16),
+        input_output_aliases={0: 0},
+        compiler_params=pltpu.CompilerParams(
+            dimension_semantics=("arbitrary",), vmem_limit_bytes=VMEM_BYTES
+        ),
+        name="insert_shared",
+    )(hbm(made), *shared, *deps)
+
+
+def weight_grads(name, groups, deps=(), share=None, sel=None, room=0):
     n, w = groups[0][0][0].shape
     widths = [right[0].shape[1] for _, right in groups]
     step = 512 if share is None else 2 * share
@@ -398,16 +416,11 @@
         specs += [pl.BlockSpec((n, step), lambda i: (0, i))] * 2 + [whole(ra.shape)] * 2
         args += [la, lb, ra, rb]
     args = list(hbm(args))
-    total = sum(widths)
-    if shared is not None:
-        total += 128
-        some = shared[2].shape
-        specs += [whole(some)] * 3
-        args += list(shared)
+    total = sum(widths) + room
     taken = len(args)
 
     def kernel(sel_ref, *refs):
-        weight_grad_kernel(widths, share, depth, sel_ref, *refs[:taken], refs[-1])
+        weight_grad_kernel(widths, share, sel_ref, *refs[:taken], refs[-1])
 
     return pl.pallas_call(
         kernel,
@@ -451,17 +464,6 @@
     half = w // 4
     far = swap((keep[half:].astype(F32) + got[half:].astype(F32)).astype(BF16), "tensor", 2)
     return keep, got, far
-
-
-def gate(v, *deps):
-    return pl.pallas_call(
-        lambda *refs: None,
-        in_specs=[pl.BlockSpec(memory_space=pl.ANY)] * (1 + len(deps)),
-        out_specs=pl.BlockSpec(memory_space=pl.ANY),
-        out_shape=far_out(v.shape, v.dtype),
-        input_output_aliases={0: 0},
-        name="gate",
-    )(hbm(v), *deps)
 
 
 def finish_kernel(a0, a1, b0, b1, gu, down, q, gate, step, attn, ssm, kv, state):
@@ -1187,19 +1189,19 @@
         )
         groups = [(h, (da0, da1)), (dm, mixed)]
         shared_sum = shared_grads(depth, rank, h, (ds0, ds1))
-        grads_two = functools.partial(
-            weight_grads, "grads_two", groups, shared=shared_sum, depth=depth
-        )
+        before = ()
         if layer == 0:
-            g2 = grads_two((big[layer + 1][1],))
+            g2 = weight_grads("grads_two", groups, (big[layer + 1][1],), room=128)
             if paired:
                 g1 = scatter_lines(merge(kept, sent, tuple(do)))
-                g2 = gate(g2, g1)
+                before = (g1,)
+            g2 = insert_shared(g2, shared_sum, depth, before)
         sums = [project_in_back(da, ds, wf, wh) for da, ds in ((da0, ds0), (da1, ds1))]
         parts = [scatter_half(*v, sent_on) for v in sums]
         deps = ()
         if layer > 0:
-            g2 = grads_two(sent_on[-2:])
+            g2 = weight_grads("grads_two", groups, sent_on[-2:], room=128)
+            g2 = insert_shared(g2, shared_sum, depth)
             deps = (g2,)
         grad, low = [], []
         for i in range(2):

time: 658 us -> 649 us (0.986)
  waiting for transfers between devices: 205 us -> 197 us
    ppermute x113, waiting for transfers between devices: 121 us -> 113 us  [swap(): return lax.ppermute(values, axis, [(i, i ^ distance) for i in range(size)])]
    unnamed x339 -> x341, local copies, waits for them, and re-layouts: 56.7 us -> 55.7 us
  transfers between devices with their start and end apart: 121 -> 121, of which waited for: 43 -> 41; matrix products, arithmetic and copies ran while one was open for 5% -> 5% of each run, Pallas kernels for 38% -> 38%
where the time goes in v4:
time: 649 us; the launch traced here: 639 us
  Pallas kernels  255 us (39%)
  waiting for transfers between devices  197 us (30%)
  starting transfers between devices  79.1 us (12%)
  local copies, waits for them, and re-layouts  72.2 us (11%)
  other arithmetic  19.2 us (3%)
  between operations  16.8 us (3%)
    pallas_call x48, Pallas kernels, call(): return lambda *args: made(*args, *deps)  151 us
    ppermute x113, waiting for transfers between devices, swap(): return lax.ppermute(values, axis, [(i, i ^ distance) for i in range(size)])  113 us
    ppermute x113, starting transfers between devices, swap(): return lax.ppermute(values, axis, [(i, i ^ distance) for i in range(size)])  78 us
    unnamed x341, local copies, waits for them, and re-layouts  55.7 us
    all_gather x4, waiting for transfers between devices, gather_dp(): return lax.all_gather(v, 'dp', axis=0, tiled=True)  54.6 us
    pallas_call x2, Pallas kernels, ssm_backward(): pl.pallas_call(lambda r, *refs: ssm_bwd_kernel(r, *refs), grid_spec=pltpu...  46.1 us
    pallas_call x5, Pallas kernels, weight_grads(): pl.pallas_call(kernel, grid=(w // step,), in_specs=[SCALAR] + specs + [pl...  35.5 us
    reduce_scatter x3, waiting for transfers between devices, scatter_dp(): return lax.psum_scatter(v, 'dp', scatter_dimension=0, tiled=True)  28.9 us
  transfers between devices with their start and end apart: 121, of which 41 were waited for; matrix products, arithmetic and copies ran while one was open for 5% of the time, Pallas kernels for 38%

profile of v4, /device:TPU:0, one launch (start us, length us, event | category | flops | bytes accessed | tf_op | source)
XLA Modules:
  0.0 638.8 jit_solution(15798376214369978880)
XLA Ops:
  39.5 45.3 %all-gather.5.cloned.1.call-done.w_in.w_mix = bf16[1024,1792]{1,0:T(8,128)(2,1)} async-done(((bf16[128,1792]{1,0:T(8,128)(2,1)}), bf16[1024,1792]{1,0:T(8,128)(2,1)}) %all-gather.5.cloned.1.call-update) | async-done | bytes 3670032 | tf_op jit(solution)/shard_map/all_gather | solution.py:972
  88.3 4.6 collective-permute-done.9.refs_2_
  96.6 3.5 project_in.4
  101.0 3.5 project_in.5
  104.6 9.9 %ssm_forward.2 = (bf16[512,384]{1,0:T(8,128)(2,1)S(1)}, bf16[512,384]{1,0:T(8,128)(2,1)S(1)}, bf16[512,640]{1,0:T(8,128)(2,1)}, bf16[512,640]{1,0:T(8,128)(2,1)}...) custom-call(s32[1]{0:T(128)} %bitcast.1.rank.r, ...), custom_call_target="tpu_custom_call" | custom-call | flops 4000000000 | bytes 20971520 | tf_op jit(solution)/shard_map/ssm_forward/pallas_call | solution.py:604
  116.8 4.6 attend_forward.2
  133.4 6.0 collective-permute-done.18.far
  151.1 4.2 collective-permute-done.33.p3
  157.4 3.7 ffn.4
  163.0 3.6 ffn.5
  170.8 5.3 collective-permute-done.23.far
  187.9 5.2 collective-permute-done.25.p3
  194.0 4.3 collective-permute-done.38.p3
  198.3 9.4 %all-gather.9.cloned.1.call-done.w_in.w_mix = bf16[1024,1536]{1,0:T(8,128)(2,1)} async-done(((bf16[128,1536]{1,0:T(8,128)(2,1)}), bf16[1024,1536]{1,0:T(8,128)(2,1)}) %all-gather.9.cloned.1.call-update) | async-done | bytes 3145744 | tf_op jit(solution)/shard_map/all_gather | solution.py:972
  209.5 4.1 project_in.6
  213.6 4.9 project_in.7
  218.5 9.9 %ssm_forward.3 = (bf16[512,384]{1,0:T(8,128)(2,1)S(1)}, bf16[512,384]{1,0:T(8,128)(2,1)S(1)}, bf16[512,640]{1,0:T(8,128)(2,1)}, bf16[512,640]{1,0:T(8,128)(2,1)}...) custom-call(s32[1]{0:T(128)} %bitcast.1.rank.r, ...), custom_call_target="tpu_custom_call" | custom-call | flops 4000000000 | bytes 20971520 | tf_op jit(solution)/shard_map/ssm_forward/pallas_call | solution.py:604
  231.8 4.6 attend_forward.3
  242.4 6.4 collective-permute-done.44.far
  261.4 5.2 collective-permute-done.51.p3
  268.1 4.2 collective-permute-done.58.p3
  276.1 3.8 ffn.6
  280.5 3.7 ffn_back.4
  284.3 3.6 ffn.7
  290.3 3.7 ffn_back.5
  297.0 7.5 %grads_one.1.refs_6_ = bf16[1024,1536]{1,0:T(8,128)(2,1)} custom-call(s32[1]{0:T(128)} %constant.65.clone.1.sel_ref, bf16[512,1024]{1,0:T(8,128)(2,1)} %get-tuple-element.245.refs_0_, bf16[512,1024]{1,0:T(8,128)(2,1)} %get-tuple-element.252.refs_1_, bf16[512,1024]{1,0:T(8,128)(2,1)} %get-tuple-element.253.refs_2_, ...), custom_call_target="tpu_custom_call" | custom-call | flops 3221225472 | bytes 12582912 | tf_op jit(solution)/shard_map/grads_one/pallas_call | solution.py:425
  306.7 7.3 %collective-permute-done.54.refs_4_ = bf16[128,1024]{1,0:T(8,128)(2,1)S(1)} collective-permute-done((bf16[128,1024]{1,0:T(8,128)(2,1)}, bf16[128,1024]{1,0:T(8,128)(2,1)S(1)}, u32[]{:S(2)}, u32[]{:S(2)}) %collective-permute-start.54) | collective-permute-done | bytes 262176 | tf_op jit(solution)/shard_map/ppermute | solution.py:927
  328.0 4.0 collective-permute-done.69.p3
  343.6 7.3 %attend_backward.2 = (bf16[1024,128]{1,0:T(8,128)(2,1)S(1)}, bf16[1024,128]{1,0:T(8,128)(2,1)S(1)}) custom-call(s32[1]{0:T(128)} %bitcast.1.rank.r, bf16[1024,128]{1,0:T(8,128)(2,1)} %copy-done.87, bf16[1024,128]{1,0:T(8,128)(2,1)} %copy-done.88, bf16[512,128]{1,0:T(8,128)(2,1)S(1)} %get-tuple-element.273.do0, bf16[512,128]{1,0:T(8,128)(2,1)S(1)} %get-tuple-element.274.do1, ...), custom_call_target="tpu_custom_call" | custom-call | flops 4000000000 | bytes 1048576 | tf_op jit(solution)/shard_map/attend_backward/pallas_call | solution.py:115
  351.0 23.2 %ssm_backward.2 = (bf16[512,1024]{1,0:T(8,128)(2,1)}, bf16[512,1024]{1,0:T(8,128)(2,1)}, bf16[512,512]{1,0:T(8,128)(2,1)}, bf16[512,512]{1,0:T(8,128)(2,1)}, f32...) custom-call(s32[1]{0:T(128)} %bitcast.1.rank.r, s32[1]{0:T(128)} %bitcast.2.oh.refs_0_, ...), custom_call_target="tpu_custom_call" | custom-call | flops 8000000000 | bytes 31457280 | tf_op jit(solution)/shard_map/ssm_backward/pallas_call | solution.py:783
  387.5 7.5 %grads_two.2.base = bf16[1024,1664]{1,0:T(8,128)(2,1)} custom-call(s32[1]{0:T(128)} %constant.65.clone.1.sel_ref, bf16[512,1024]{1,0:T(8,128)(2,1)} %get-tuple-element.282.refs_0_.ha, bf16[512,1024]{1,0:T(8,128)(2,1)} %get-tuple-element.283.refs_1_.hb, bf16[512,1024]{1,0:T(8,128)(2,1)} %get-tuple-element.278.da.refs_2_, ...), custom_call_target="tpu_custom_call" | custom-call | flops 3489660928 | bytes 12582912 | tf_op jit(solution)/shard_map/grads_two/pallas_call | solution.py:425
  398.2 7.1 %collective-permute-done.75.refs_4_ = bf16[128,1024]{1,0:T(8,128)(2,1)S(1)} collective-permute-done((bf16[128,1024]{1,0:T(8,128)(2,1)S(1)}, bf16[128,1024]{1,0:T(8,128)(2,1)S(1)}, u32[]{:S(2)}, u32[]{:S(2)}) %collective-permute-start.75) | collective-permute-done | bytes 262176 | tf_op jit(solution)/shard_map/ppermute | solution.py:927
  418.6 4.5 collective-permute-done.86.refs_3_
  424.8 4.4 ffn_back.6
  430.5 4.4 ffn_back.7
  439.1 6.5 %grads_one_sent.1.refs_6_.refs_8_ = bf16[512,1536]{1,0:T(8,128)(2,1)} custom-call(s32[1]{0:T(128)S(6)} %sub.16.sel_ref, bf16[512,1024]{1,0:T(8,128)(2,1)} %get-tuple-element.299.refs_0_, bf16[512,1024]{1,0:T(8,128)(2,1)} %get-tuple-element.300.refs_1_, bf16[512,1024]{1,0:T(8,128)(2,1)} %get-tuple-element.301.refs_2_, ...), custom_call_target="tpu_custom_call" | custom-call | flops 3221225472 | bytes 12582912 | tf_op jit(solution)/shard_map/grads_one_sent/pallas_call | solution.py:425
  448.4 7.2 %collective-permute-done.83.refs_4_ = bf16[128,1024]{1,0:T(8,128)(2,1)S(1)} collective-permute-done((bf16[128,1024]{1,0:T(8,128)(2,1)S(1)}, bf16[128,1024]{1,0:T(8,128)(2,1)S(1)}, u32[]{:S(2)}, u32[]{:S(2)}) %collective-permute-start.83) | collective-permute-done | bytes 262176 | tf_op jit(solution)/shard_map/ppermute | solution.py:927
  461.8 6.4 %grads_one_kept.1.refs_6_.refs_0_ = bf16[512,1536]{1,0:T(8,128)(2,1)} custom-call(s32[1]{0:T(128)} %bitcast.53.sel_ref, bf16[512,1024]{1,0:T(8,128)(2,1)} %get-tuple-element.299.refs_0_, bf16[512,1024]{1,0:T(8,128)(2,1)} %get-tuple-element.300.refs_1_, bf16[512,1024]{1,0:T(8,128)(2,1)} %get-tuple-element.301.refs_2_, ...), custom_call_target="tpu_custom_call" | custom-call | flops 3221225472 | bytes 12582912 | tf_op jit(solution)/shard_map/grads_one_kept/pallas_call | solution.py:425
  475.0 4.3 collective-permute-done.94.p3
  487.4 3.3 mix_back.7
  490.7 3.5 merge.1
  497.0 7.4 %attend_backward.3 = (bf16[1024,128]{1,0:T(8,128)(2,1)S(1)}, bf16[1024,128]{1,0:T(8,128)(2,1)S(1)}) custom-call(s32[1]{0:T(128)} %bitcast.1.rank.r, bf16[1024,128]{1,0:T(8,128)(2,1)} %copy-done.85, bf16[1024,128]{1,0:T(8,128)(2,1)} %copy-done.86, bf16[512,128]{1,0:T(8,128)(2,1)S(1)} %get-tuple-element.319.do0.refs_2_, ...), custom_call_target="tpu_custom_call" | custom-call | flops 4000000000 | bytes 1048576 | tf_op jit(solution)/shard_map/attend_backward/pallas_call | solution.py:115
  504.4 22.9 %ssm_backward.3 = (bf16[512,1024]{1,0:T(8,128)(2,1)}, bf16[512,1024]{1,0:T(8,128)(2,1)}, bf16[512,512]{1,0:T(8,128)(2,1)}, bf16[512,512]{1,0:T(8,128)(2,1)}, f32...) custom-call(s32[1]{0:T(128)} %bitcast.1.rank.r, s32[1]{0:T(128)} %bitcast.2.oh.refs_0_, ...), custom_call_target="tpu_custom_call" | custom-call | flops 8000000000 | bytes 31457280 | tf_op jit(solution)/shard_map/ssm_backward/pallas_call | solution.py:783
  527.3 3.3 shared_grads.3
  530.8 3.9 project_in_back.7
  537.8 7.5 %grads_two.3.base = bf16[1024,1664]{1,0:T(8,128)(2,1)} custom-call(s32[1]{0:T(128)} %constant.65.clone.1.sel_ref, bf16[512,1024]{1,0:T(8,128)(2,1)} %get-tuple-element.352.refs_0_.ha, bf16[512,1024]{1,0:T(8,128)(2,1)} %get-tuple-element.353.refs_1_.hb, bf16[512,1024]{1,0:T(8,128)(2,1)} %get-tuple-element.324.refs_4_.da.refs_2_, ...), custom_call_target="tpu_custom_call" | custom-call | flops 3489660928 | bytes 12582912 | tf_op jit(solution)/shard_map/grads_two/pallas_call | solution.py:425
  558.5 5.8 collective-permute-done.104.far
  596.5 28.9 %reduce-scatter.11.cloned.1.call-done.b0 = bf16[128,1664]{1,0:T(8,128)(2,1)} async-done(((bf16[1024,1664]{1,0:T(8,128)(2,1)}), bf16[128,1664]{1,0:T(8,128)(2,1)}) %reduce-scatter.11.cloned.1.call-update) | async-done | bytes 426000 | tf_op jit(solution)/shard_map/reduce_scatter | solution.py:976
  (755 shorter events, 266.6 us)
Async XLA Ops:
  7.2 77.6 %all-gather.5.cloned.1.call-start = ((), (), s32[]{:S(2)}) async-start(), calls=%async_computation.4 | async-start | bytes 4128768 | tf_op jit(solution)/shard_map/all_gather | solution.py:972
  15.0 140.4 %all-gather.7.cloned.1.call-start = ((), (), s32[]{:S(2)}) async-start(), calls=%async_computation.5 | async-start | bytes 3538944 | tf_op jit(solution)/shard_map/all_gather | solution.py:972
  17.1 190.5 %all-gather.9.cloned.1.call-start = ((), (), s32[]{:S(2)}) async-start(), calls=%async_computation.6 | async-start | bytes 3538944 | tf_op jit(solution)/shard_map/all_gather | solution.py:972
  17.9 75.4 %collective-permute-start = (bf16[128,1024]{1,0:T(8,128)(2,1)S(1)}, bf16[128,1024]{1,0:T(8,128)(2,1)}, u32[]{:S(2)}, u32[]{:S(2)}) collective-permute-start(bf16[128,1024]{1,0:T(8,128)(2,1)S(1)} %get-tuple-element.452.p2.x.v), channel_id=1, source_target_pairs={{0,1},{1,0},{2,3},{3,2},{4,5},{5,4},{6,7},{7,6},{8,9},{9,8},{10,11... | collective-permute-start | bytes 786440 | tf_op jit(solution)/shard_map/ppermute | solution.py:927
  18.4 69.4 %collective-permute-start.1 = (bf16[128,1024]{1,0:T(8,128)(2,1)S(1)}, bf16[128,1024]{1,0:T(8,128)(2,1)}, u32[]{:S(2)}, u32[]{:S(2)}) collective-permute-start(bf16[128,1024]{1,0:T(8,128)(2,1)S(1)} %get-tuple-element.452.p2.x.v), channel_id=1, source_target_pairs={{0,2},{1,3},{2,0},{3,1},{4,6},{5,7},{6,4},{7,5},{8,10},{9,11},{10,... | collective-permute-start | bytes 786440 | tf_op jit(solution)/shard_map/ppermute | solution.py:927
  22.6 71.2 %collective-permute-start.12 = (bf16[128,1024]{1,0:T(8,128)(2,1)}, bf16[128,1024]{1,0:T(8,128)(2,1)}, u32[]{:S(2)}, u32[]{:S(2)}) collective-permute-start(bf16[128,1024]{1,0:T(8,128)(2,1)} %get-tuple-element.453.p2.x.v), channel_id=1, source_target_pairs={{0,2},{1,3},{2,0},{3,1},{4,6},{5,7},{6,4},{7,5},{8,10},{9,11},{10,... | collective-permute-start | bytes 786440 | tf_op jit(solution)/shard_map/ppermute | solution.py:927
  24.4 249.8 %all-gather.11.cloned.1.call-start = ((), (), s32[]{:S(2)}) async-start(), calls=%async_computation.7 | async-start | bytes 3538944 | tf_op jit(solution)/shard_map/all_gather | solution.py:972
  38.0 49.4 %collective-permute-start.7 = (bf16[8,2,208]{2,1,0:T(2,128)(2,1)S(1)}, bf16[8,2,208]{2,1,0:T(2,128)(2,1)S(1)}, u32[]{:S(2)}, u32[]{:S(2)}) collective-permute-start(bf16[8,2,208]{2,1,0:T(2,128)(2,1)S(1)} %pad_maximum_fusion.7), channel_id=1, source_target_pairs={{0,2},{1,3},{2,0},{3,1},{4,6},{5,7},{6,4},{7,5},{8,10},{9,11},{10,... | collective-permute-start | bytes 19976 | tf_op jit(solution)/shard_map/ppermute | solution.py:927
  128.7 295.1 %reduce-scatter.5.cloned.1.call-start = ((), (), s32[]{:S(2)}) async-start(), calls=%async_computation.8 | async-start | bytes 3538944 | tf_op jit(solution)/shard_map/reduce_scatter | solution.py:976
  132.8 12.2 %collective-permute-start.31 = (bf16[128,1024]{1,0:T(8,128)(2,1)S(1)}, bf16[128,1024]{1,0:T(8,128)(2,1)S(1)}, u32[]{:S(2)}, u32[]{:S(2)}) collective-permute-start(bf16[128,1024]{1,0:T(8,128)(2,1)S(1)} %add_convert_fusion.15), channel_id=1, source_target_pairs={{0,2},{1,3},{2,0},{3,1},{4,6},{5,7},{6,4},{7,5},{8,10},{9,11},{10,... | collective-permute-start | bytes 786440 | tf_op jit(solution)/shard_map/ppermute | solution.py:927
  150.6 11.0 %collective-permute-start.32 = (bf16[128,1024]{1,0:T(8,128)(2,1)S(1)}, bf16[128,1024]{1,0:T(8,128)(2,1)S(1)}, u32[]{:S(2)}, u32[]{:S(2)}) collective-permute-start(bf16[128,1024]{1,0:T(8,128)(2,1)S(1)} %get-tuple-element.218.p2), channel_id=1, source_target_pairs={{0,1},{1,0},{2,3},{3,2},{4,5},{5,4},{6,7},{7,6},{8,9},{9,8},{10,11... | collective-permute-start | bytes 786440 | tf_op jit(solution)/shard_map/ppermute | solution.py:927
  168.8 13.0 %collective-permute-start.36 = (bf16[128,1024]{1,0:T(8,128)(2,1)S(1)}, bf16[128,1024]{1,0:T(8,128)(2,1)S(1)}, u32[]{:S(2)}, u32[]{:S(2)}) collective-permute-start(bf16[128,1024]{1,0:T(8,128)(2,1)S(1)} %add_convert_fusion.14), channel_id=1, source_target_pairs={{0,2},{1,3},{2,0},{3,1},{4,6},{5,7},{6,4},{7,5},{8,10},{9,11},{10,... | collective-permute-start | bytes 786440 | tf_op jit(solution)/shard_map/ppermute | solution.py:927
  170.4 17.0 %collective-permute-start.28 = (bf16[1024,128]{1,0:T(8,128)(2,1)S(1)}, bf16[1024,128]{1,0:T(8,128)(2,1)S(1)}, u32[]{:S(2)}, u32[]{:S(2)}) collective-permute-start(bf16[1024,128]{1,0:T(8,128)(2,1)S(1)} %get-tuple-element.446.refs_0_), channel_id=1, source_target_pairs={{0,2},{1,3},{2,0},{3,1},{4,6},{5,7},{6,4},{7,5},{8,10},{9,11},{10,... | collective-permute-start | bytes 786440 | tf_op jit(solution)/shard_map/ppermute | solution.py:927
  179.0 14.0 %collective-permute-start.25 = (bf16[128,1024]{1,0:T(8,128)(2,1)S(1)}, bf16[128,1024]{1,0:T(8,128)(2,1)}, u32[]{:S(2)}, u32[]{:S(2)}) collective-permute-start(bf16[128,1024]{1,0:T(8,128)(2,1)S(1)} %get-tuple-element.211.p2), channel_id=1, source_target_pairs={{0,2},{1,3},{2,0},{3,1},{4,6},{5,7},{6,4},{7,5},{8,10},{9,11},{10,... | collective-permute-start | bytes 786440 | tf_op jit(solution)/shard_map/ppermute | solution.py:927
  180.7 12.7 %collective-permute-start.27 = (bf16[1024,128]{1,0:T(8,128)(2,1)S(1)}, bf16[1024,128]{1,0:T(8,128)(2,1)S(1)}, u32[]{:S(2)}, u32[]{:S(2)}) collective-permute-start(bf16[1024,128]{1,0:T(8,128)(2,1)S(1)} %get-tuple-element.446.refs_0_), channel_id=1, source_target_pairs={{0,1},{1,0},{2,3},{3,2},{4,5},{5,4},{6,7},{7,6},{8,9},{9,8},{10,11... | collective-permute-start | bytes 786440 | tf_op jit(solution)/shard_map/ppermute | solution.py:927
  184.7 13.6 %collective-permute-start.38 = (bf16[128,1024]{1,0:T(8,128)(2,1)S(1)}, bf16[128,1024]{1,0:T(8,128)(2,1)}, u32[]{:S(2)}, u32[]{:S(2)}) collective-permute-start(bf16[128,1024]{1,0:T(8,128)(2,1)S(1)} %get-tuple-element.221.p2), channel_id=1, source_target_pairs={{0,2},{1,3},{2,0},{3,1},{4,6},{5,7},{6,4},{7,5},{8,10},{9,11},{10,... | collective-permute-start | bytes 786440 | tf_op jit(solution)/shard_map/ppermute | solution.py:927
  187.4 20.2 %collective-permute-start.29 = (bf16[1024,128]{1,0:T(8,128)(2,1)S(1)}, bf16[1024,128]{1,0:T(8,128)(2,1)S(1)}, u32[]{:S(2)}, u32[]{:S(2)}) collective-permute-start(bf16[1024,128]{1,0:T(8,128)(2,1)S(1)} %collective-permute-done.28.refs_2_), channel_id=1, source_target_pairs={{0,1},{1,0},{2,3},{3,2},{4,5},{5,4},{6,7},{7,6},{8,9},{9,8},{10,11... | collective-permute-start | bytes 786440 | tf_op jit(solution)/shard_map/ppermute | solution.py:927
  187.4 20.2 %collective-permute-start.24 = (bf16[128,1024]{1,0:T(8,128)(2,1)S(1)}, bf16[128,1024]{1,0:T(8,128)(2,1)}, u32[]{:S(2)}, u32[]{:S(2)}) collective-permute-start(bf16[128,1024]{1,0:T(8,128)(2,1)S(1)} %get-tuple-element.211.p2), channel_id=1, source_target_pairs={{0,1},{1,0},{2,3},{3,2},{4,5},{5,4},{6,7},{7,6},{8,9},{9,8},{10,11... | collective-permute-start | bytes 786440 | tf_op jit(solution)/shard_map/ppermute | solution.py:927
  193.1 14.5 %collective-permute-start.26 = (bf16[128,1024]{1,0:T(8,128)(2,1)}, bf16[128,1024]{1,0:T(8,128)(2,1)}, u32[]{:S(2)}, u32[]{:S(2)}) collective-permute-start(bf16[128,1024]{1,0:T(8,128)(2,1)} %collective-permute-done.25.p3), channel_id=1, source_target_pairs={{0,1},{1,0},{2,3},{3,2},{4,5},{5,4},{6,7},{7,6},{8,9},{9,8},{10,11... | collective-permute-start | bytes 786440 | tf_op jit(solution)/shard_map/ppermute | solution.py:927
  193.4 20.2 %collective-permute-start.37 = (bf16[128,1024]{1,0:T(8,128)(2,1)S(1)}, bf16[128,1024]{1,0:T(8,128)(2,1)}, u32[]{:S(2)}, u32[]{:S(2)}) collective-permute-start(bf16[128,1024]{1,0:T(8,128)(2,1)S(1)} %get-tuple-element.221.p2), channel_id=1, source_target_pairs={{0,1},{1,0},{2,3},{3,2},{4,5},{5,4},{6,7},{7,6},{8,9},{9,8},{10,11... | collective-permute-start | bytes 786440 | tf_op jit(solution)/shard_map/ppermute | solution.py:927
  198.2 15.4 %collective-permute-start.39 = (bf16[128,1024]{1,0:T(8,128)(2,1)}, bf16[128,1024]{1,0:T(8,128)(2,1)}, u32[]{:S(2)}, u32[]{:S(2)}) collective-permute-start(bf16[128,1024]{1,0:T(8,128)(2,1)} %collective-permute-done.38.p3), channel_id=1, source_target_pairs={{0,1},{1,0},{2,3},{3,2},{4,5},{5,4},{6,7},{7,6},{8,9},{9,8},{10,11... | collective-permute-start | bytes 786440 | tf_op jit(solution)/shard_map/ppermute | solution.py:927
  241.2 13.4 %collective-permute-start.56 = (bf16[128,1024]{1,0:T(8,128)(2,1)S(1)}, bf16[128,1024]{1,0:T(8,128)(2,1)S(1)}, u32[]{:S(2)}, u32[]{:S(2)}) collective-permute-start(bf16[128,1024]{1,0:T(8,128)(2,1)S(1)} %add_convert_fusion.10), channel_id=1, source_target_pairs={{0,2},{1,3},{2,0},{3,1},{4,6},{5,7},{6,4},{7,5},{8,10},{9,11},{10,... | collective-permute-start | bytes 786440 | tf_op jit(solution)/shard_map/ppermute | solution.py:927
  254.0 12.7 %collective-permute-start.51 = (bf16[128,1024]{1,0:T(8,128)(2,1)}, bf16[128,1024]{1,0:T(8,128)(2,1)}, u32[]{:S(2)}, u32[]{:S(2)}) collective-permute-start(bf16[128,1024]{1,0:T(8,128)(2,1)} %get-tuple-element.449.p2.refs_0_), channel_id=1, source_target_pairs={{0,2},{1,3},{2,0},{3,1},{4,6},{5,7},{6,4},{7,5},{8,10},{9,11},{10,... | collective-permute-start | bytes 786440 | tf_op jit(solution)/shard_map/ppermute | solution.py:927
  257.5 14.8 %collective-permute-start.58 = (bf16[128,1024]{1,0:T(8,128)(2,1)}, bf16[128,1024]{1,0:T(8,128)(2,1)}, u32[]{:S(2)}, u32[]{:S(2)}) collective-permute-start(bf16[128,1024]{1,0:T(8,128)(2,1)} %get-tuple-element.251.p2), channel_id=1, source_target_pairs={{0,2},{1,3},{2,0},{3,1},{4,6},{5,7},{6,4},{7,5},{8,10},{9,11},{10,... | collective-permute-start | bytes 786440 | tf_op jit(solution)/shard_map/ppermute | solution.py:927
  259.0 13.3 %collective-permute-start.45 = (bf16[128,1024]{1,0:T(8,128)(2,1)S(1)}, bf16[128,1024]{1,0:T(8,128)(2,1)S(1)}, u32[]{:S(2)}, u32[]{:S(2)}) collective-permute-start(bf16[128,1024]{1,0:T(8,128)(2,1)S(1)} %get-tuple-element.236.p2), channel_id=1, source_target_pairs={{0,1},{1,0},{2,3},{3,2},{4,5},{5,4},{6,7},{7,6},{8,9},{9,8},{10,11... | collective-permute-start | bytes 786440 | tf_op jit(solution)/shard_map/ppermute | solution.py:927
  260.9 11.9 %collective-permute-start.47 = (bf16[128,1024]{1,0:T(8,128)(2,1)S(1)}, bf16[128,1024]{1,0:T(8,128)(2,1)S(1)}, u32[]{:S(2)}, u32[]{:S(2)}) collective-permute-start(bf16[128,1024]{1,0:T(8,128)(2,1)S(1)} %collective-permute-done.46.p3), channel_id=1, source_target_pairs={{0,1},{1,0},{2,3},{3,2},{4,5},{5,4},{6,7},{7,6},{8,9},{9,8},{10,11... | collective-permute-start | bytes 786440 | tf_op jit(solution)/shard_map/ppermute | solution.py:927
  260.9 19.0 %collective-permute-start.50 = (bf16[128,1024]{1,0:T(8,128)(2,1)}, bf16[128,1024]{1,0:T(8,128)(2,1)}, u32[]{:S(2)}, u32[]{:S(2)}) collective-permute-start(bf16[128,1024]{1,0:T(8,128)(2,1)} %get-tuple-element.449.p2.refs_0_), channel_id=1, source_target_pairs={{0,1},{1,0},{2,3},{3,2},{4,5},{5,4},{6,7},{7,6},{8,9},{9,8},{10,11... | collective-permute-start | bytes 786440 | tf_op jit(solution)/shard_map/ppermute | solution.py:927
  266.6 13.3 %collective-permute-start.61 = (bf16[128,1024]{1,0:T(8,128)(2,1)}, bf16[128,1024]{1,0:T(8,128)(2,1)}, u32[]{:S(2)}, u32[]{:S(2)}) collective-permute-start(bf16[128,1024]{1,0:T(8,128)(2,1)} %get-tuple-element.448.p2.g), channel_id=1, source_target_pairs={{0,2},{1,3},{2,0},{3,1},{4,6},{5,7},{6,4},{7,5},{8,10},{9,11},{10,... | collective-permute-start | bytes 786440 | tf_op jit(solution)/shard_map/ppermute | solution.py:927
  272.3 12.0 %collective-permute-start.57 = (bf16[128,1024]{1,0:T(8,128)(2,1)}, bf16[128,1024]{1,0:T(8,128)(2,1)}, u32[]{:S(2)}, u32[]{:S(2)}) collective-permute-start(bf16[128,1024]{1,0:T(8,128)(2,1)} %get-tuple-element.251.p2), channel_id=1, source_target_pairs={{0,1},{1,0},{2,3},{3,2},{4,5},{5,4},{6,7},{7,6},{8,9},{9,8},{10,11... | collective-permute-start | bytes 786440 | tf_op jit(solution)/shard_map/ppermute | solution.py:927
  273.7 10.6 %collective-permute-start.59 = (bf16[128,1024]{1,0:T(8,128)(2,1)}, bf16[128,1024]{1,0:T(8,128)(2,1)}, u32[]{:S(2)}, u32[]{:S(2)}) collective-permute-start(bf16[128,1024]{1,0:T(8,128)(2,1)} %collective-permute-done.58.p3), channel_id=1, source_target_pairs={{0,1},{1,0},{2,3},{3,2},{4,5},{5,4},{6,7},{7,6},{8,9},{9,8},{10,11... | collective-permute-start | bytes 786440 | tf_op jit(solution)/shard_map/ppermute | solution.py:927
  284.2 10.3 %collective-permute-start.53 = (bf16[256,1024]{1,0:T(8,128)(2,1)S(1)}, bf16[256,1024]{1,0:T(8,128)(2,1)S(1)}, u32[]{:S(2)}, u32[]{:S(2)}) collective-permute-start(bf16[256,1024]{1,0:T(8,128)(2,1)S(1)} %get-tuple-element.244), channel_id=1, source_target_pairs={{0,1},{1,0},{2,3},{3,2},{4,5},{5,4},{6,7},{7,6},{8,9},{9,8},{10,11... | collective-permute-start | bytes 1572872 | tf_op jit(solution)/shard_map/ppermute | solution.py:927
  304.5 232.3 %reduce-scatter.9.cloned.1.call-start = ((), (), s32[]{:S(2)}) async-start(), calls=%async_computation.10 | async-start | bytes 3833856 | tf_op jit(solution)/shard_map/reduce_scatter | solution.py:976
  306.1 14.5 %collective-permute-start.67 = (bf16[128,1024]{1,0:T(8,128)(2,1)}, bf16[128,1024]{1,0:T(8,128)(2,1)S(1)}, u32[]{:S(2)}, u32[]{:S(2)}) collective-permute-start(bf16[128,1024]{1,0:T(8,128)(2,1)} %copy-done.69), channel_id=1, source_target_pairs={{0,2},{1,3},{2,0},{3,1},{4,6},{5,7},{6,4},{7,5},{8,10},{9,11},{10,... | collective-permute-start | bytes 786440 | tf_op jit(solution)/shard_map/ppermute | solution.py:927
  384.9 10.2 %collective-permute-start.78 = (bf16[256,512]{1,0:T(8,128)(2,1)S(1)}, bf16[256,512]{1,0:T(8,128)(2,1)S(1)}, u32[]{:S(2)}, u32[]{:S(2)}) collective-permute-start(bf16[256,512]{1,0:T(8,128)(2,1)S(1)} %add_convert_fusion.6), channel_id=1, source_target_pairs={{0,2},{1,3},{2,0},{3,1},{4,6},{5,7},{6,4},{7,5},{8,10},{9,11},{10,... | collective-permute-start | bytes 786440 | tf_op jit(solution)/shard_map/ppermute | solution.py:927
  395.9 149.5 %reduce-scatter.7.cloned.1.call-start = ((), (), s32[]{:S(2)}) async-start(), calls=%async_computation.9 | async-start | bytes 1966080 | tf_op jit(solution)/shard_map/reduce_scatter | solution.py:997
  397.6 14.6 %collective-permute-start.84 = (bf16[128,1024]{1,0:T(8,128)(2,1)}, bf16[128,1024]{1,0:T(8,128)(2,1)S(1)}, u32[]{:S(2)}, u32[]{:S(2)}) collective-permute-start(bf16[128,1024]{1,0:T(8,128)(2,1)} %add_convert_fusion.7.refs_9_), channel_id=1, source_target_pairs={{0,2},{1,3},{2,0},{3,1},{4,6},{5,7},{6,4},{7,5},{8,10},{9,11},{10,... | collective-permute-start | bytes 786440 | tf_op jit(solution)/shard_map/ppermute | solution.py:927
  418.1 12.4 %collective-permute-start.85 = (bf16[128,1024]{1,0:T(8,128)(2,1)}, bf16[128,1024]{1,0:T(8,128)(2,1)}, u32[]{:S(2)}, u32[]{:S(2)}) collective-permute-start(bf16[128,1024]{1,0:T(8,128)(2,1)} %get-tuple-element.303.refs_2_), channel_id=1, source_target_pairs={{0,1},{1,0},{2,3},{3,2},{4,5},{5,4},{6,7},{7,6},{8,9},{9,8},{10,11... | collective-permute-start | bytes 786440 | tf_op jit(solution)/shard_map/ppermute | solution.py:927
  445.6 45.2 %collective-permute-start.110 = (bf16[512,1536]{1,0:T(8,128)(2,1)}, bf16[512,1536]{1,0:T(8,128)(2,1)}, u32[]{:S(2)}, u32[]{:S(2)}) collective-permute-start(bf16[512,1536]{1,0:T(8,128)(2,1)} %grads_one_sent.1.refs_6_.refs_8_), channel_id=1, source_target_pairs={{0,4},{4,0},{8,12},{12,8},{16,20},{20,16},{24,28},{28,24},{1,5},{5... | collective-permute-start | bytes 4718600 | tf_op jit(solution)/shard_map/ppermute | solution.py:927
  447.8 26.2 %collective-permute-start.99 = (bf16[256,1024]{1,0:T(8,128)(2,1)S(1)}, bf16[256,1024]{1,0:T(8,128)(2,1)S(1)}, u32[]{:S(2)}, u32[]{:S(2)}) collective-permute-start(bf16[256,1024]{1,0:T(8,128)(2,1)S(1)} %copy-done.72), channel_id=1, source_target_pairs={{0,1},{1,0},{2,3},{3,2},{4,5},{5,4},{6,7},{7,6},{8,9},{9,8},{10,11... | collective-permute-start | bytes 1572872 | tf_op jit(solution)/shard_map/ppermute | solution.py:927
  447.8 20.4 %collective-permute-start.92 = (bf16[128,1024]{1,0:T(8,128)(2,1)S(1)}, bf16[128,1024]{1,0:T(8,128)(2,1)S(1)}, u32[]{:S(2)}, u32[]{:S(2)}) collective-permute-start(bf16[128,1024]{1,0:T(8,128)(2,1)S(1)} %add_convert_fusion.4.refs_9_), channel_id=1, source_target_pairs={{0,2},{1,3},{2,0},{3,1},{4,6},{5,7},{6,4},{7,5},{8,10},{9,11},{10,... | collective-permute-start | bytes 786440 | tf_op jit(solution)/shard_map/ppermute | solution.py:927
  460.4 13.2 %collective-permute-start.90 = (bf16[128,1024]{1,0:T(8,128)(2,1)S(1)}, bf16[128,1024]{1,0:T(8,128)(2,1)S(1)}, u32[]{:S(2)}, u32[]{:S(2)}) collective-permute-start(bf16[128,1024]{1,0:T(8,128)(2,1)S(1)} %get-tuple-element.312.p2), channel_id=1, source_target_pairs={{0,2},{1,3},{2,0},{3,1},{4,6},{5,7},{6,4},{7,5},{8,10},{9,11},{10,... | collective-permute-start | bytes 786440 | tf_op jit(solution)/shard_map/ppermute | solution.py:927
  474.9 11.1 %collective-permute-start.93 = (bf16[128,1024]{1,0:T(8,128)(2,1)S(1)}, bf16[128,1024]{1,0:T(8,128)(2,1)S(1)}, u32[]{:S(2)}, u32[]{:S(2)}) collective-permute-start(bf16[128,1024]{1,0:T(8,128)(2,1)S(1)} %get-tuple-element.315.p2), channel_id=1, source_target_pairs={{0,1},{1,0},{2,3},{3,2},{4,5},{5,4},{6,7},{7,6},{8,9},{9,8},{10,11... | collective-permute-start | bytes 786440 | tf_op jit(solution)/shard_map/ppermute | solution.py:927
  479.4 94.5 %collective-permute-start.48 = (bf16[256,1024]{1,0:T(8,128)(2,1)}, bf16[256,1024]{1,0:T(8,128)(2,1)}, u32[]{:S(2)}, u32[]{:S(2)}) collective-permute-start(bf16[256,1024]{1,0:T(8,128)(2,1)} %get-tuple-element.238), channel_id=1, source_target_pairs={{0,1},{1,0},{2,3},{3,2},{4,5},{5,4},{6,7},{7,6},{8,9},{9,8},{10,11... | collective-permute-start | bytes 1572872 | tf_op jit(solution)/shard_map/ppermute | solution.py:927
  480.1 98.1 %collective-permute-start.100 = (bf16[128,1024]{1,0:T(8,128)(2,1)}, bf16[128,1024]{1,0:T(8,128)(2,1)}, u32[]{:S(2)}, u32[]{:S(2)}) collective-permute-start(bf16[128,1024]{1,0:T(8,128)(2,1)} %add_convert_fusion.3), channel_id=1, source_target_pairs={{0,2},{1,3},{2,0},{3,1},{4,6},{5,7},{6,4},{7,5},{8,10},{9,11},{10,... | collective-permute-start | bytes 786440 | tf_op jit(solution)/shard_map/ppermute | solution.py:927
  494.2 131.2 %reduce-scatter.11.cloned.1.call-start = ((), (), s32[]{:S(2)}) async-start(), calls=%async_computation.11 | async-start | bytes 3833856 | tf_op jit(solution)/shard_map/reduce_scatter | solution.py:976
  534.7 19.1 %collective-permute-start.103 = (bf16[256,1024]{1,0:T(8,128)(2,1)}, bf16[256,1024]{1,0:T(8,128)(2,1)}, u32[]{:S(2)}, u32[]{:S(2)}) collective-permute-start(bf16[256,1024]{1,0:T(8,128)(2,1)} %get-tuple-element.336), channel_id=1, source_target_pairs={{0,1},{1,0},{2,3},{3,2},{4,5},{5,4},{6,7},{7,6},{8,9},{9,8},{10,11... | collective-permute-start | bytes 1572872 | tf_op jit(solution)/shard_map/ppermute | solution.py:927
  535.3 10.1 %collective-permute-start.112 = (bf16[256,512]{1,0:T(8,128)(2,1)S(1)}, bf16[256,512]{1,0:T(8,128)(2,1)S(1)}, u32[]{:S(2)}, u32[]{:S(2)}) collective-permute-start(bf16[256,512]{1,0:T(8,128)(2,1)S(1)} %add_convert_fusion), channel_id=1, source_target_pairs={{0,2},{1,3},{2,0},{3,1},{4,6},{5,7},{6,4},{7,5},{8,10},{9,11},{10,... | collective-permute-start | bytes 786440 | tf_op jit(solution)/shard_map/ppermute | solution.py:927
  556.5 12.7 %collective-permute-start.102 = (bf16[128,1024]{1,0:T(8,128)(2,1)S(1)}, bf16[128,1024]{1,0:T(8,128)(2,1)S(1)}, u32[]{:S(2)}, u32[]{:S(2)}) collective-permute-start(bf16[128,1024]{1,0:T(8,128)(2,1)S(1)} %add_convert_fusion.2), channel_id=1, source_target_pairs={{0,2},{1,3},{2,0},{3,1},{4,6},{5,7},{6,4},{7,5},{8,10},{9,11},{10,... | collective-permute-start | bytes 786440 | tf_op jit(solution)/shard_map/ppermute | solution.py:927
  (229 other events, 2316.8 us)
Sparse Core Ops, SparseCore 0:
  15.1 69.6 all-gather.4
  87.5 58.7 all-gather.6
  148.5 59.0 all-gather.8
  209.6 59.0 all-gather.10
  304.6 73.0 reduce-scatter.4
  396.0 80.4 reduce-scatter.8
  494.4 34.8 reduce-scatter.6
  547.6 77.7 reduce-scatter.10

commit v5 on v4

--- a/solution.py
+++ b/solution.py
@@ -1162,7 +1162,7 @@
             given = weight_grads("grads_one_sent", groups, sent_on[-2:], depth, 1 - side)
             kept = weight_grads("grads_one_kept", groups, (given,), depth, side)
             sent = swap(given, "dp", 1)
-            early = [(given,), (kept,)]
+            early = [(given,), ()]
         else:
             g1 = weight_grads("grads_one", groups, sent_on[-2:])
             early = [(g1,), ()]

time: 649 us -> 649 us (level)
    unnamed x341 -> x339, local copies, waits for them, and re-layouts: 55.7 us -> 52.2 us
  transfers between devices with their start and end apart: 121 -> 121, of which waited for: 41 -> 42; matrix products, arithmetic and copies ran while one was open for 5% -> 5% of each run, Pallas kernels for 38% -> 39%
where the time goes in v5:
time: 649 us; the launch traced here: 638 us
  Pallas kernels  255 us (39%)
  waiting for transfers between devices  198 us (31%)
  starting transfers between devices  81.2 us (13%)
  local copies, waits for them, and re-layouts  68.7 us (11%)
  other arithmetic  19.1 us (3%)
  between operations  16.8 us (3%)
    pallas_call x48, Pallas kernels, call(): return lambda *args: made(*args, *deps)  151 us
    ppermute x113, waiting for transfers between devices, swap(): return lax.ppermute(values, axis, [(i, i ^ distance) for i in range(size)])  114 us
    ppermute x113, starting transfers between devices, swap(): return lax.ppermute(values, axis, [(i, i ^ distance) for i in range(size)])  80.1 us
    all_gather x4, waiting for transfers between devices, gather_dp(): return lax.all_gather(v, 'dp', axis=0, tiled=True)  54.6 us
    unnamed x339, local copies, waits for them, and re-layouts  52.2 us
    pallas_call x2, Pallas kernels, ssm_backward(): pl.pallas_call(lambda r, *refs: ssm_bwd_kernel(r, *refs), grid_spec=pltpu...  46.2 us
    pallas_call x5, Pallas kernels, weight_grads(): pl.pallas_call(kernel, grid=(w // step,), in_specs=[SCALAR] + specs + [pl...  35.5 us
    reduce_scatter x3, waiting for transfers between devices, scatter_dp(): return lax.psum_scatter(v, 'dp', scatter_dimension=0, tiled=True)  29.6 us
  transfers between devices with their start and end apart: 121, of which 42 were waited for; matrix products, arithmetic and copies ran while one was open for 5% of the time, Pallas kernels for 39%

profile of v5, /device:TPU:0, one launch (start us, length us, event | category | flops | bytes accessed | tf_op | source)
XLA Modules:
  0.0 638.2 jit_solution(8023016262801995351)
XLA Ops:
  39.6 45.2 %all-gather.5.cloned.1.call-done.w_in.w_mix = bf16[1024,1792]{1,0:T(8,128)(2,1)} async-done(((bf16[128,1792]{1,0:T(8,128)(2,1)}), bf16[1024,1792]{1,0:T(8,128)(2,1)}) %all-gather.5.cloned.1.call-update) | async-done | bytes 3670032 | tf_op jit(solution)/shard_map/all_gather | solution.py:972
  88.3 4.6 collective-permute-done.9.refs_2_
  96.6 3.5 project_in.4
  101.0 3.5 project_in.5
  104.6 9.9 %ssm_forward.2 = (bf16[512,384]{1,0:T(8,128)(2,1)S(1)}, bf16[512,384]{1,0:T(8,128)(2,1)S(1)}, bf16[512,640]{1,0:T(8,128)(2,1)}, bf16[512,640]{1,0:T(8,128)(2,1)}...) custom-call(s32[1]{0:T(128)} %bitcast.1.rank.r, ...), custom_call_target="tpu_custom_call" | custom-call | flops 4000000000 | bytes 20971520 | tf_op jit(solution)/shard_map/ssm_forward/pallas_call | solution.py:604
  116.8 4.6 attend_forward.2
  133.4 6.0 collective-permute-done.18.far
  151.1 4.2 collective-permute-done.33.p3
  157.4 3.7 ffn.4
  163.0 3.7 ffn.5
  170.9 5.3 collective-permute-done.23.far
  187.9 5.2 collective-permute-done.25.p3
  194.0 4.3 collective-permute-done.38.p3
  198.3 9.3 %all-gather.9.cloned.1.call-done.w_in.w_mix = bf16[1024,1536]{1,0:T(8,128)(2,1)} async-done(((bf16[128,1536]{1,0:T(8,128)(2,1)}), bf16[1024,1536]{1,0:T(8,128)(2,1)}) %all-gather.9.cloned.1.call-update) | async-done | bytes 3145744 | tf_op jit(solution)/shard_map/all_gather | solution.py:972
  209.5 4.1 project_in.6
  213.6 4.8 project_in.7
  218.5 9.9 %ssm_forward.3 = (bf16[512,384]{1,0:T(8,128)(2,1)S(1)}, bf16[512,384]{1,0:T(8,128)(2,1)S(1)}, bf16[512,640]{1,0:T(8,128)(2,1)}, bf16[512,640]{1,0:T(8,128)(2,1)}...) custom-call(s32[1]{0:T(128)} %bitcast.1.rank.r, ...), custom_call_target="tpu_custom_call" | custom-call | flops 4000000000 | bytes 20971520 | tf_op jit(solution)/shard_map/ssm_forward/pallas_call | solution.py:604
  231.7 4.6 attend_forward.3
  242.4 6.4 collective-permute-done.44.far
  261.4 5.2 collective-permute-done.51.p3
  268.1 4.1 collective-permute-done.58.p3
  276.1 3.8 ffn.6
  280.4 3.7 ffn_back.4
  284.3 3.6 ffn.7
  290.3 3.7 ffn_back.5
  296.9 7.5 %grads_one.1.refs_6_ = bf16[1024,1536]{1,0:T(8,128)(2,1)} custom-call(s32[1]{0:T(128)} %constant.65.clone.1.sel_ref, bf16[512,1024]{1,0:T(8,128)(2,1)} %get-tuple-element.245.refs_0_, bf16[512,1024]{1,0:T(8,128)(2,1)} %get-tuple-element.252.refs_1_, bf16[512,1024]{1,0:T(8,128)(2,1)} %get-tuple-element.253.refs_2_, ...), custom_call_target="tpu_custom_call" | custom-call | flops 3221225472 | bytes 12582912 | tf_op jit(solution)/shard_map/grads_one/pallas_call | solution.py:425
  306.6 7.3 %collective-permute-done.54.refs_4_ = bf16[128,1024]{1,0:T(8,128)(2,1)S(1)} collective-permute-done((bf16[128,1024]{1,0:T(8,128)(2,1)}, bf16[128,1024]{1,0:T(8,128)(2,1)S(1)}, u32[]{:S(2)}, u32[]{:S(2)}) %collective-permute-start.54) | collective-permute-done | bytes 262176 | tf_op jit(solution)/shard_map/ppermute | solution.py:927
  327.9 4.0 collective-permute-done.69.p3
  343.6 7.4 %attend_backward.2 = (bf16[1024,128]{1,0:T(8,128)(2,1)S(1)}, bf16[1024,128]{1,0:T(8,128)(2,1)S(1)}) custom-call(s32[1]{0:T(128)} %bitcast.1.rank.r, bf16[1024,128]{1,0:T(8,128)(2,1)} %copy-done.86, bf16[1024,128]{1,0:T(8,128)(2,1)} %copy-done.87, bf16[512,128]{1,0:T(8,128)(2,1)S(1)} %get-tuple-element.273.do0, bf16[512,128]{1,0:T(8,128)(2,1)S(1)} %get-tuple-element.274.do1, ...), custom_call_target="tpu_custom_call" | custom-call | flops 4000000000 | bytes 1048576 | tf_op jit(solution)/shard_map/attend_backward/pallas_call | solution.py:115
  351.1 23.2 %ssm_backward.2 = (bf16[512,1024]{1,0:T(8,128)(2,1)}, bf16[512,1024]{1,0:T(8,128)(2,1)}, bf16[512,512]{1,0:T(8,128)(2,1)}, bf16[512,512]{1,0:T(8,128)(2,1)}, f32...) custom-call(s32[1]{0:T(128)} %bitcast.1.rank.r, s32[1]{0:T(128)} %bitcast.2.oh.refs_0_, ...), custom_call_target="tpu_custom_call" | custom-call | flops 8000000000 | bytes 31457280 | tf_op jit(solution)/shard_map/ssm_backward/pallas_call | solution.py:783
  387.5 7.5 %grads_two.2.base = bf16[1024,1664]{1,0:T(8,128)(2,1)} custom-call(s32[1]{0:T(128)} %constant.65.clone.1.sel_ref, bf16[512,1024]{1,0:T(8,128)(2,1)} %get-tuple-element.282.refs_0_.ha, bf16[512,1024]{1,0:T(8,128)(2,1)} %get-tuple-element.283.refs_1_.hb, bf16[512,1024]{1,0:T(8,128)(2,1)} %get-tuple-element.278.da.refs_2_, ...), custom_call_target="tpu_custom_call" | custom-call | flops 3489660928 | bytes 12582912 | tf_op jit(solution)/shard_map/grads_two/pallas_call | solution.py:425
  398.2 7.1 %collective-permute-done.75.refs_4_ = bf16[128,1024]{1,0:T(8,128)(2,1)S(1)} collective-permute-done((bf16[128,1024]{1,0:T(8,128)(2,1)S(1)}, bf16[128,1024]{1,0:T(8,128)(2,1)S(1)}, u32[]{:S(2)}, u32[]{:S(2)}) %collective-permute-start.75) | collective-permute-done | bytes 262176 | tf_op jit(solution)/shard_map/ppermute | solution.py:927
  418.6 4.5 collective-permute-done.86.refs_3_
  424.8 4.4 ffn_back.6
  430.5 4.4 ffn_back.7
  439.1 6.5 %grads_one_sent.1.refs_6_.refs_8_ = bf16[512,1536]{1,0:T(8,128)(2,1)} custom-call(s32[1]{0:T(128)S(6)} %sub.16.sel_ref, bf16[512,1024]{1,0:T(8,128)(2,1)} %get-tuple-element.299.refs_0_, bf16[512,1024]{1,0:T(8,128)(2,1)} %get-tuple-element.300.refs_1_, bf16[512,1024]{1,0:T(8,128)(2,1)} %get-tuple-element.301.refs_2_, ...), custom_call_target="tpu_custom_call" | custom-call | flops 3221225472 | bytes 12582912 | tf_op jit(solution)/shard_map/grads_one_sent/pallas_call | solution.py:425
  448.4 7.1 %collective-permute-done.83.refs_4_ = bf16[128,1024]{1,0:T(8,128)(2,1)S(1)} collective-permute-done((bf16[128,1024]{1,0:T(8,128)(2,1)S(1)}, bf16[128,1024]{1,0:T(8,128)(2,1)S(1)}, u32[]{:S(2)}, u32[]{:S(2)}) %collective-permute-start.83) | collective-permute-done | bytes 262176 | tf_op jit(solution)/shard_map/ppermute | solution.py:927
  468.9 4.7 collective-permute-done.94.p3
  473.7 6.4 grads_one_kept.1.refs_0_
  486.9 3.3 mix_back.7
  490.2 3.5 merge.1
  496.5 7.3 %attend_backward.3 = (bf16[1024,128]{1,0:T(8,128)(2,1)S(1)}, bf16[1024,128]{1,0:T(8,128)(2,1)S(1)}) custom-call(s32[1]{0:T(128)} %bitcast.1.rank.r, bf16[1024,128]{1,0:T(8,128)(2,1)} %copy-done.84, bf16[1024,128]{1,0:T(8,128)(2,1)} %copy-done.85, bf16[512,128]{1,0:T(8,128)(2,1)S(1)} %get-tuple-element.319.do0.refs_2_, ...), custom_call_target="tpu_custom_call" | custom-call | flops 4000000000 | bytes 1048576 | tf_op jit(solution)/shard_map/attend_backward/pallas_call | solution.py:115
  503.9 23.0 %ssm_backward.3 = (bf16[512,1024]{1,0:T(8,128)(2,1)}, bf16[512,1024]{1,0:T(8,128)(2,1)}, bf16[512,512]{1,0:T(8,128)(2,1)}, bf16[512,512]{1,0:T(8,128)(2,1)}, f32...) custom-call(s32[1]{0:T(128)} %bitcast.1.rank.r, s32[1]{0:T(128)} %bitcast.2.oh.refs_0_, ...), custom_call_target="tpu_custom_call" | custom-call | flops 8000000000 | bytes 31457280 | tf_op jit(solution)/shard_map/ssm_backward/pallas_call | solution.py:783
  526.9 3.4 shared_grads.3
  530.4 3.9 project_in_back.7
  536.5 7.6 %grads_two.3.base = bf16[1024,1664]{1,0:T(8,128)(2,1)} custom-call(s32[1]{0:T(128)} %constant.65.clone.1.sel_ref, bf16[512,1024]{1,0:T(8,128)(2,1)} %get-tuple-element.352.refs_0_.ha, bf16[512,1024]{1,0:T(8,128)(2,1)} %get-tuple-element.353.refs_1_.hb, bf16[512,1024]{1,0:T(8,128)(2,1)} %get-tuple-element.324.refs_4_.da.refs_2_, ...), custom_call_target="tpu_custom_call" | custom-call | flops 3489660928 | bytes 12582912 | tf_op jit(solution)/shard_map/grads_two/pallas_call | solution.py:425
  557.1 5.7 collective-permute-done.104.far
  595.3 29.6 %reduce-scatter.11.cloned.1.call-done.b0 = bf16[128,1664]{1,0:T(8,128)(2,1)} async-done(((bf16[1024,1664]{1,0:T(8,128)(2,1)}), bf16[128,1664]{1,0:T(8,128)(2,1)}) %reduce-scatter.11.cloned.1.call-update) | async-done | bytes 426000 | tf_op jit(solution)/shard_map/reduce_scatter | solution.py:976
  (753 shorter events, 265.1 us)
Async XLA Ops:
  7.2 77.6 %all-gather.5.cloned.1.call-start = ((), (), s32[]{:S(2)}) async-start(), calls=%async_computation.4 | async-start | bytes 4128768 | tf_op jit(solution)/shard_map/all_gather | solution.py:972
  15.0 140.4 %all-gather.7.cloned.1.call-start = ((), (), s32[]{:S(2)}) async-start(), calls=%async_computation.5 | async-start | bytes 3538944 | tf_op jit(solution)/shard_map/all_gather | solution.py:972
  17.1 190.5 %all-gather.9.cloned.1.call-start = ((), (), s32[]{:S(2)}) async-start(), calls=%async_computation.6 | async-start | bytes 3538944 | tf_op jit(solution)/shard_map/all_gather | solution.py:972
  17.9 75.4 %collective-permute-start = (bf16[128,1024]{1,0:T(8,128)(2,1)S(1)}, bf16[128,1024]{1,0:T(8,128)(2,1)}, u32[]{:S(2)}, u32[]{:S(2)}) collective-permute-start(bf16[128,1024]{1,0:T(8,128)(2,1)S(1)} %get-tuple-element.452.p2.x.v), channel_id=1, source_target_pairs={{0,1},{1,0},{2,3},{3,2},{4,5},{5,4},{6,7},{7,6},{8,9},{9,8},{10,11... | collective-permute-start | bytes 786440 | tf_op jit(solution)/shard_map/ppermute | solution.py:927
  18.4 69.3 %collective-permute-start.1 = (bf16[128,1024]{1,0:T(8,128)(2,1)S(1)}, bf16[128,1024]{1,0:T(8,128)(2,1)}, u32[]{:S(2)}, u32[]{:S(2)}) collective-permute-start(bf16[128,1024]{1,0:T(8,128)(2,1)S(1)} %get-tuple-element.452.p2.x.v), channel_id=1, source_target_pairs={{0,2},{1,3},{2,0},{3,1},{4,6},{5,7},{6,4},{7,5},{8,10},{9,11},{10,... | collective-permute-start | bytes 786440 | tf_op jit(solution)/shard_map/ppermute | solution.py:927
  22.7 71.2 %collective-permute-start.12 = (bf16[128,1024]{1,0:T(8,128)(2,1)}, bf16[128,1024]{1,0:T(8,128)(2,1)}, u32[]{:S(2)}, u32[]{:S(2)}) collective-permute-start(bf16[128,1024]{1,0:T(8,128)(2,1)} %get-tuple-element.453.p2.x.v), channel_id=1, source_target_pairs={{0,2},{1,3},{2,0},{3,1},{4,6},{5,7},{6,4},{7,5},{8,10},{9,11},{10,... | collective-permute-start | bytes 786440 | tf_op jit(solution)/shard_map/ppermute | solution.py:927
  24.4 249.8 %all-gather.11.cloned.1.call-start = ((), (), s32[]{:S(2)}) async-start(), calls=%async_computation.7 | async-start | bytes 3538944 | tf_op jit(solution)/shard_map/all_gather | solution.py:972
  38.0 49.4 %collective-permute-start.7 = (bf16[8,2,208]{2,1,0:T(2,128)(2,1)S(1)}, bf16[8,2,208]{2,1,0:T(2,128)(2,1)S(1)}, u32[]{:S(2)}, u32[]{:S(2)}) collective-permute-start(bf16[8,2,208]{2,1,0:T(2,128)(2,1)S(1)} %pad_maximum_fusion.7), channel_id=1, source_target_pairs={{0,2},{1,3},{2,0},{3,1},{4,6},{5,7},{6,4},{7,5},{8,10},{9,11},{10,... | collective-permute-start | bytes 19976 | tf_op jit(solution)/shard_map/ppermute | solution.py:927
  128.7 295.1 %reduce-scatter.5.cloned.1.call-start = ((), (), s32[]{:S(2)}) async-start(), calls=%async_computation.8 | async-start | bytes 3538944 | tf_op jit(solution)/shard_map/reduce_scatter | solution.py:976
  132.8 12.2 %collective-permute-start.31 = (bf16[128,1024]{1,0:T(8,128)(2,1)S(1)}, bf16[128,1024]{1,0:T(8,128)(2,1)S(1)}, u32[]{:S(2)}, u32[]{:S(2)}) collective-permute-start(bf16[128,1024]{1,0:T(8,128)(2,1)S(1)} %add_convert_fusion.15), channel_id=1, source_target_pairs={{0,2},{1,3},{2,0},{3,1},{4,6},{5,7},{6,4},{7,5},{8,10},{9,11},{10,... | collective-permute-start | bytes 786440 | tf_op jit(solution)/shard_map/ppermute | solution.py:927
  150.6 11.0 %collective-permute-start.32 = (bf16[128,1024]{1,0:T(8,128)(2,1)S(1)}, bf16[128,1024]{1,0:T(8,128)(2,1)S(1)}, u32[]{:S(2)}, u32[]{:S(2)}) collective-permute-start(bf16[128,1024]{1,0:T(8,128)(2,1)S(1)} %get-tuple-element.218.p2), channel_id=1, source_target_pairs={{0,1},{1,0},{2,3},{3,2},{4,5},{5,4},{6,7},{7,6},{8,9},{9,8},{10,11... | collective-permute-start | bytes 786440 | tf_op jit(solution)/shard_map/ppermute | solution.py:927
  168.8 13.0 %collective-permute-start.36 = (bf16[128,1024]{1,0:T(8,128)(2,1)S(1)}, bf16[128,1024]{1,0:T(8,128)(2,1)S(1)}, u32[]{:S(2)}, u32[]{:S(2)}) collective-permute-start(bf16[128,1024]{1,0:T(8,128)(2,1)S(1)} %add_convert_fusion.14), channel_id=1, source_target_pairs={{0,2},{1,3},{2,0},{3,1},{4,6},{5,7},{6,4},{7,5},{8,10},{9,11},{10,... | collective-permute-start | bytes 786440 | tf_op jit(solution)/shard_map/ppermute | solution.py:927
  170.4 17.0 %collective-permute-start.28 = (bf16[1024,128]{1,0:T(8,128)(2,1)S(1)}, bf16[1024,128]{1,0:T(8,128)(2,1)S(1)}, u32[]{:S(2)}, u32[]{:S(2)}) collective-permute-start(bf16[1024,128]{1,0:T(8,128)(2,1)S(1)} %get-tuple-element.446.refs_0_), channel_id=1, source_target_pairs={{0,2},{1,3},{2,0},{3,1},{4,6},{5,7},{6,4},{7,5},{8,10},{9,11},{10,... | collective-permute-start | bytes 786440 | tf_op jit(solution)/shard_map/ppermute | solution.py:927
  179.1 14.1 %collective-permute-start.25 = (bf16[128,1024]{1,0:T(8,128)(2,1)S(1)}, bf16[128,1024]{1,0:T(8,128)(2,1)}, u32[]{:S(2)}, u32[]{:S(2)}) collective-permute-start(bf16[128,1024]{1,0:T(8,128)(2,1)S(1)} %get-tuple-element.211.p2), channel_id=1, source_target_pairs={{0,2},{1,3},{2,0},{3,1},{4,6},{5,7},{6,4},{7,5},{8,10},{9,11},{10,... | collective-permute-start | bytes 786440 | tf_op jit(solution)/shard_map/ppermute | solution.py:927
  180.7 12.7 %collective-permute-start.27 = (bf16[1024,128]{1,0:T(8,128)(2,1)S(1)}, bf16[1024,128]{1,0:T(8,128)(2,1)S(1)}, u32[]{:S(2)}, u32[]{:S(2)}) collective-permute-start(bf16[1024,128]{1,0:T(8,128)(2,1)S(1)} %get-tuple-element.446.refs_0_), channel_id=1, source_target_pairs={{0,1},{1,0},{2,3},{3,2},{4,5},{5,4},{6,7},{7,6},{8,9},{9,8},{10,11... | collective-permute-start | bytes 786440 | tf_op jit(solution)/shard_map/ppermute | solution.py:927
  184.7 13.6 %collective-permute-start.38 = (bf16[128,1024]{1,0:T(8,128)(2,1)S(1)}, bf16[128,1024]{1,0:T(8,128)(2,1)}, u32[]{:S(2)}, u32[]{:S(2)}) collective-permute-start(bf16[128,1024]{1,0:T(8,128)(2,1)S(1)} %get-tuple-element.221.p2), channel_id=1, source_target_pairs={{0,2},{1,3},{2,0},{3,1},{4,6},{5,7},{6,4},{7,5},{8,10},{9,11},{10,... | collective-permute-start | bytes 786440 | tf_op jit(solution)/shard_map/ppermute | solution.py:927
  187.4 20.2 %collective-permute-start.29 = (bf16[1024,128]{1,0:T(8,128)(2,1)S(1)}, bf16[1024,128]{1,0:T(8,128)(2,1)S(1)}, u32[]{:S(2)}, u32[]{:S(2)}) collective-permute-start(bf16[1024,128]{1,0:T(8,128)(2,1)S(1)} %collective-permute-done.28.refs_2_), channel_id=1, source_target_pairs={{0,1},{1,0},{2,3},{3,2},{4,5},{5,4},{6,7},{7,6},{8,9},{9,8},{10,11... | collective-permute-start | bytes 786440 | tf_op jit(solution)/shard_map/ppermute | solution.py:927
  187.4 20.2 %collective-permute-start.24 = (bf16[128,1024]{1,0:T(8,128)(2,1)S(1)}, bf16[128,1024]{1,0:T(8,128)(2,1)}, u32[]{:S(2)}, u32[]{:S(2)}) collective-permute-start(bf16[128,1024]{1,0:T(8,128)(2,1)S(1)} %get-tuple-element.211.p2), channel_id=1, source_target_pairs={{0,1},{1,0},{2,3},{3,2},{4,5},{5,4},{6,7},{7,6},{8,9},{9,8},{10,11... | collective-permute-start | bytes 786440 | tf_op jit(solution)/shard_map/ppermute | solution.py:927
  193.1 14.5 %collective-permute-start.26 = (bf16[128,1024]{1,0:T(8,128)(2,1)}, bf16[128,1024]{1,0:T(8,128)(2,1)}, u32[]{:S(2)}, u32[]{:S(2)}) collective-permute-start(bf16[128,1024]{1,0:T(8,128)(2,1)} %collective-permute-done.25.p3), channel_id=1, source_target_pairs={{0,1},{1,0},{2,3},{3,2},{4,5},{5,4},{6,7},{7,6},{8,9},{9,8},{10,11... | collective-permute-start | bytes 786440 | tf_op jit(solution)/shard_map/ppermute | solution.py:927
  193.4 20.2 %collective-permute-start.37 = (bf16[128,1024]{1,0:T(8,128)(2,1)S(1)}, bf16[128,1024]{1,0:T(8,128)(2,1)}, u32[]{:S(2)}, u32[]{:S(2)}) collective-permute-start(bf16[128,1024]{1,0:T(8,128)(2,1)S(1)} %get-tuple-element.221.p2), channel_id=1, source_target_pairs={{0,1},{1,0},{2,3},{3,2},{4,5},{5,4},{6,7},{7,6},{8,9},{9,8},{10,11... | collective-permute-start | bytes 786440 | tf_op jit(solution)/shard_map/ppermute | solution.py:927
  198.3 15.4 %collective-permute-start.39 = (bf16[128,1024]{1,0:T(8,128)(2,1)}, bf16[128,1024]{1,0:T(8,128)(2,1)}, u32[]{:S(2)}, u32[]{:S(2)}) collective-permute-start(bf16[128,1024]{1,0:T(8,128)(2,1)} %collective-permute-done.38.p3), channel_id=1, source_target_pairs={{0,1},{1,0},{2,3},{3,2},{4,5},{5,4},{6,7},{7,6},{8,9},{9,8},{10,11... | collective-permute-start | bytes 786440 | tf_op jit(solution)/shard_map/ppermute | solution.py:927
  241.2 13.4 %collective-permute-start.56 = (bf16[128,1024]{1,0:T(8,128)(2,1)S(1)}, bf16[128,1024]{1,0:T(8,128)(2,1)S(1)}, u32[]{:S(2)}, u32[]{:S(2)}) collective-permute-start(bf16[128,1024]{1,0:T(8,128)(2,1)S(1)} %add_convert_fusion.10), channel_id=1, source_target_pairs={{0,2},{1,3},{2,0},{3,1},{4,6},{5,7},{6,4},{7,5},{8,10},{9,11},{10,... | collective-permute-start | bytes 786440 | tf_op jit(solution)/shard_map/ppermute | solution.py:927
  254.0 12.7 %collective-permute-start.51 = (bf16[128,1024]{1,0:T(8,128)(2,1)}, bf16[128,1024]{1,0:T(8,128)(2,1)}, u32[]{:S(2)}, u32[]{:S(2)}) collective-permute-start(bf16[128,1024]{1,0:T(8,128)(2,1)} %get-tuple-element.449.p2.refs_0_), channel_id=1, source_target_pairs={{0,2},{1,3},{2,0},{3,1},{4,6},{5,7},{6,4},{7,5},{8,10},{9,11},{10,... | collective-permute-start | bytes 786440 | tf_op jit(solution)/shard_map/ppermute | solution.py:927
  257.5 14.7 %collective-permute-start.58 = (bf16[128,1024]{1,0:T(8,128)(2,1)}, bf16[128,1024]{1,0:T(8,128)(2,1)}, u32[]{:S(2)}, u32[]{:S(2)}) collective-permute-start(bf16[128,1024]{1,0:T(8,128)(2,1)} %get-tuple-element.251.p2), channel_id=1, source_target_pairs={{0,2},{1,3},{2,0},{3,1},{4,6},{5,7},{6,4},{7,5},{8,10},{9,11},{10,... | collective-permute-start | bytes 786440 | tf_op jit(solution)/shard_map/ppermute | solution.py:927
  259.0 13.3 %collective-permute-start.45 = (bf16[128,1024]{1,0:T(8,128)(2,1)S(1)}, bf16[128,1024]{1,0:T(8,128)(2,1)S(1)}, u32[]{:S(2)}, u32[]{:S(2)}) collective-permute-start(bf16[128,1024]{1,0:T(8,128)(2,1)S(1)} %get-tuple-element.236.p2), channel_id=1, source_target_pairs={{0,1},{1,0},{2,3},{3,2},{4,5},{5,4},{6,7},{7,6},{8,9},{9,8},{10,11... | collective-permute-start | bytes 786440 | tf_op jit(solution)/shard_map/ppermute | solution.py:927
  260.9 11.9 %collective-permute-start.47 = (bf16[128,1024]{1,0:T(8,128)(2,1)S(1)}, bf16[128,1024]{1,0:T(8,128)(2,1)S(1)}, u32[]{:S(2)}, u32[]{:S(2)}) collective-permute-start(bf16[128,1024]{1,0:T(8,128)(2,1)S(1)} %collective-permute-done.46.p3), channel_id=1, source_target_pairs={{0,1},{1,0},{2,3},{3,2},{4,5},{5,4},{6,7},{7,6},{8,9},{9,8},{10,11... | collective-permute-start | bytes 786440 | tf_op jit(solution)/shard_map/ppermute | solution.py:927
  260.9 19.0 %collective-permute-start.50 = (bf16[128,1024]{1,0:T(8,128)(2,1)}, bf16[128,1024]{1,0:T(8,128)(2,1)}, u32[]{:S(2)}, u32[]{:S(2)}) collective-permute-start(bf16[128,1024]{1,0:T(8,128)(2,1)} %get-tuple-element.449.p2.refs_0_), channel_id=1, source_target_pairs={{0,1},{1,0},{2,3},{3,2},{4,5},{5,4},{6,7},{7,6},{8,9},{9,8},{10,11... | collective-permute-start | bytes 786440 | tf_op jit(solution)/shard_map/ppermute | solution.py:927
  266.6 13.3 %collective-permute-start.61 = (bf16[128,1024]{1,0:T(8,128)(2,1)}, bf16[128,1024]{1,0:T(8,128)(2,1)}, u32[]{:S(2)}, u32[]{:S(2)}) collective-permute-start(bf16[128,1024]{1,0:T(8,128)(2,1)} %get-tuple-element.448.p2.g), channel_id=1, source_target_pairs={{0,2},{1,3},{2,0},{3,1},{4,6},{5,7},{6,4},{7,5},{8,10},{9,11},{10,... | collective-permute-start | bytes 786440 | tf_op jit(solution)/shard_map/ppermute | solution.py:927
  272.3 12.0 %collective-permute-start.57 = (bf16[128,1024]{1,0:T(8,128)(2,1)}, bf16[128,1024]{1,0:T(8,128)(2,1)}, u32[]{:S(2)}, u32[]{:S(2)}) collective-permute-start(bf16[128,1024]{1,0:T(8,128)(2,1)} %get-tuple-element.251.p2), channel_id=1, source_target_pairs={{0,1},{1,0},{2,3},{3,2},{4,5},{5,4},{6,7},{7,6},{8,9},{9,8},{10,11... | collective-permute-start | bytes 786440 | tf_op jit(solution)/shard_map/ppermute | solution.py:927
  273.7 10.6 %collective-permute-start.59 = (bf16[128,1024]{1,0:T(8,128)(2,1)}, bf16[128,1024]{1,0:T(8,128)(2,1)}, u32[]{:S(2)}, u32[]{:S(2)}) collective-permute-start(bf16[128,1024]{1,0:T(8,128)(2,1)} %collective-permute-done.58.p3), channel_id=1, source_target_pairs={{0,1},{1,0},{2,3},{3,2},{4,5},{5,4},{6,7},{7,6},{8,9},{9,8},{10,11... | collective-permute-start | bytes 786440 | tf_op jit(solution)/shard_map/ppermute | solution.py:927
  284.1 10.3 %collective-permute-start.53 = (bf16[256,1024]{1,0:T(8,128)(2,1)S(1)}, bf16[256,1024]{1,0:T(8,128)(2,1)S(1)}, u32[]{:S(2)}, u32[]{:S(2)}) collective-permute-start(bf16[256,1024]{1,0:T(8,128)(2,1)S(1)} %get-tuple-element.244), channel_id=1, source_target_pairs={{0,1},{1,0},{2,3},{3,2},{4,5},{5,4},{6,7},{7,6},{8,9},{9,8},{10,11... | collective-permute-start | bytes 1572872 | tf_op jit(solution)/shard_map/ppermute | solution.py:927
  304.5 231.0 %reduce-scatter.9.cloned.1.call-start = ((), (), s32[]{:S(2)}) async-start(), calls=%async_computation.10 | async-start | bytes 3833856 | tf_op jit(solution)/shard_map/reduce_scatter | solution.py:976
  306.1 14.5 %collective-permute-start.67 = (bf16[128,1024]{1,0:T(8,128)(2,1)}, bf16[128,1024]{1,0:T(8,128)(2,1)S(1)}, u32[]{:S(2)}, u32[]{:S(2)}) collective-permute-start(bf16[128,1024]{1,0:T(8,128)(2,1)} %copy-done.68), channel_id=1, source_target_pairs={{0,2},{1,3},{2,0},{3,1},{4,6},{5,7},{6,4},{7,5},{8,10},{9,11},{10,... | collective-permute-start | bytes 786440 | tf_op jit(solution)/shard_map/ppermute | solution.py:927
  395.9 148.2 %reduce-scatter.7.cloned.1.call-start = ((), (), s32[]{:S(2)}) async-start(), calls=%async_computation.9 | async-start | bytes 1966080 | tf_op jit(solution)/shard_map/reduce_scatter | solution.py:997
  397.6 14.6 %collective-permute-start.84 = (bf16[128,1024]{1,0:T(8,128)(2,1)}, bf16[128,1024]{1,0:T(8,128)(2,1)S(1)}, u32[]{:S(2)}, u32[]{:S(2)}) collective-permute-start(bf16[128,1024]{1,0:T(8,128)(2,1)} %add_convert_fusion.7.refs_9_), channel_id=1, source_target_pairs={{0,2},{1,3},{2,0},{3,1},{4,6},{5,7},{6,4},{7,5},{8,10},{9,11},{10,... | collective-permute-start | bytes 786440 | tf_op jit(solution)/shard_map/ppermute | solution.py:927
  418.0 12.4 %collective-permute-start.85 = (bf16[128,1024]{1,0:T(8,128)(2,1)}, bf16[128,1024]{1,0:T(8,128)(2,1)}, u32[]{:S(2)}, u32[]{:S(2)}) collective-permute-start(bf16[128,1024]{1,0:T(8,128)(2,1)} %get-tuple-element.303.refs_2_), channel_id=1, source_target_pairs={{0,1},{1,0},{2,3},{3,2},{4,5},{5,4},{6,7},{7,6},{8,9},{9,8},{10,11... | collective-permute-start | bytes 786440 | tf_op jit(solution)/shard_map/ppermute | solution.py:927
  445.6 44.6 %collective-permute-start.110 = (bf16[512,1536]{1,0:T(8,128)(2,1)}, bf16[512,1536]{1,0:T(8,128)(2,1)}, u32[]{:S(2)}, u32[]{:S(2)}) collective-permute-start(bf16[512,1536]{1,0:T(8,128)(2,1)} %grads_one_sent.1.refs_6_.refs_8_), channel_id=1, source_target_pairs={{0,4},{4,0},{8,12},{12,8},{16,20},{20,16},{24,28},{28,24},{1,5},{5... | collective-permute-start | bytes 4718600 | tf_op jit(solution)/shard_map/ppermute | solution.py:927
  446.4 19.2 %collective-permute-start.99 = (bf16[256,1024]{1,0:T(8,128)(2,1)S(1)}, bf16[256,1024]{1,0:T(8,128)(2,1)S(1)}, u32[]{:S(2)}, u32[]{:S(2)}) collective-permute-start(bf16[256,1024]{1,0:T(8,128)(2,1)S(1)} %copy-done.71), channel_id=1, source_target_pairs={{0,1},{1,0},{2,3},{3,2},{4,5},{5,4},{6,7},{7,6},{8,9},{9,8},{10,11... | collective-permute-start | bytes 1572872 | tf_op jit(solution)/shard_map/ppermute | solution.py:927
  447.9 13.9 %collective-permute-start.92 = (bf16[128,1024]{1,0:T(8,128)(2,1)S(1)}, bf16[128,1024]{1,0:T(8,128)(2,1)S(1)}, u32[]{:S(2)}, u32[]{:S(2)}) collective-permute-start(bf16[128,1024]{1,0:T(8,128)(2,1)S(1)} %add_convert_fusion.4.refs_9_), channel_id=1, source_target_pairs={{0,2},{1,3},{2,0},{3,1},{4,6},{5,7},{6,4},{7,5},{8,10},{9,11},{10,... | collective-permute-start | bytes 786440 | tf_op jit(solution)/shard_map/ppermute | solution.py:927
  466.5 13.6 %collective-permute-start.89 = (bf16[128,1024]{1,0:T(8,128)(2,1)S(1)}, bf16[128,1024]{1,0:T(8,128)(2,1)S(1)}, u32[]{:S(2)}, u32[]{:S(2)}) collective-permute-start(bf16[128,1024]{1,0:T(8,128)(2,1)S(1)} %get-tuple-element.312.p2), channel_id=1, source_target_pairs={{0,1},{1,0},{2,3},{3,2},{4,5},{5,4},{6,7},{7,6},{8,9},{9,8},{10,11... | collective-permute-start | bytes 786440 | tf_op jit(solution)/shard_map/ppermute | solution.py:927
  466.6 18.9 %collective-permute-start.93 = (bf16[128,1024]{1,0:T(8,128)(2,1)S(1)}, bf16[128,1024]{1,0:T(8,128)(2,1)S(1)}, u32[]{:S(2)}, u32[]{:S(2)}) collective-permute-start(bf16[128,1024]{1,0:T(8,128)(2,1)S(1)} %get-tuple-element.315.p2), channel_id=1, source_target_pairs={{0,1},{1,0},{2,3},{3,2},{4,5},{5,4},{6,7},{7,6},{8,9},{9,8},{10,11... | collective-permute-start | bytes 786440 | tf_op jit(solution)/shard_map/ppermute | solution.py:927
  468.9 11.7 %collective-permute-start.91 = (bf16[128,1024]{1,0:T(8,128)(2,1)S(1)}, bf16[128,1024]{1,0:T(8,128)(2,1)S(1)}, u32[]{:S(2)}, u32[]{:S(2)}) collective-permute-start(bf16[128,1024]{1,0:T(8,128)(2,1)S(1)} %collective-permute-done.90.p3), channel_id=1, source_target_pairs={{0,1},{1,0},{2,3},{3,2},{4,5},{5,4},{6,7},{7,6},{8,9},{9,8},{10,11... | collective-permute-start | bytes 786440 | tf_op jit(solution)/shard_map/ppermute | solution.py:927
  473.6 11.8 %collective-permute-start.95 = (bf16[128,1024]{1,0:T(8,128)(2,1)}, bf16[128,1024]{1,0:T(8,128)(2,1)S(1)}, u32[]{:S(2)}, u32[]{:S(2)}) collective-permute-start(bf16[128,1024]{1,0:T(8,128)(2,1)} %collective-permute-done.94.p3), channel_id=1, source_target_pairs={{0,1},{1,0},{2,3},{3,2},{4,5},{5,4},{6,7},{7,6},{8,9},{9,8},{10,11... | collective-permute-start | bytes 786440 | tf_op jit(solution)/shard_map/ppermute | solution.py:927
  480.1 92.6 %collective-permute-start.48 = (bf16[256,1024]{1,0:T(8,128)(2,1)}, bf16[256,1024]{1,0:T(8,128)(2,1)}, u32[]{:S(2)}, u32[]{:S(2)}) collective-permute-start(bf16[256,1024]{1,0:T(8,128)(2,1)} %get-tuple-element.238), channel_id=1, source_target_pairs={{0,1},{1,0},{2,3},{3,2},{4,5},{5,4},{6,7},{7,6},{8,9},{9,8},{10,11... | collective-permute-start | bytes 1572872 | tf_op jit(solution)/shard_map/ppermute | solution.py:927
  480.6 96.4 %collective-permute-start.100 = (bf16[128,1024]{1,0:T(8,128)(2,1)}, bf16[128,1024]{1,0:T(8,128)(2,1)}, u32[]{:S(2)}, u32[]{:S(2)}) collective-permute-start(bf16[128,1024]{1,0:T(8,128)(2,1)} %add_convert_fusion.3), channel_id=1, source_target_pairs={{0,2},{1,3},{2,0},{3,1},{4,6},{5,7},{6,4},{7,5},{8,10},{9,11},{10,... | collective-permute-start | bytes 786440 | tf_op jit(solution)/shard_map/ppermute | solution.py:927
  493.7 131.1 %reduce-scatter.11.cloned.1.call-start = ((), (), s32[]{:S(2)}) async-start(), calls=%async_computation.11 | async-start | bytes 3833856 | tf_op jit(solution)/shard_map/reduce_scatter | solution.py:976
  534.3 18.2 %collective-permute-start.103 = (bf16[256,1024]{1,0:T(8,128)(2,1)}, bf16[256,1024]{1,0:T(8,128)(2,1)}, u32[]{:S(2)}, u32[]{:S(2)}) collective-permute-start(bf16[256,1024]{1,0:T(8,128)(2,1)} %get-tuple-element.336), channel_id=1, source_target_pairs={{0,1},{1,0},{2,3},{3,2},{4,5},{5,4},{6,7},{7,6},{8,9},{9,8},{10,11... | collective-permute-start | bytes 1572872 | tf_op jit(solution)/shard_map/ppermute | solution.py:927
  556.0 11.8 %collective-permute-start.102 = (bf16[128,1024]{1,0:T(8,128)(2,1)S(1)}, bf16[128,1024]{1,0:T(8,128)(2,1)S(1)}, u32[]{:S(2)}, u32[]{:S(2)}) collective-permute-start(bf16[128,1024]{1,0:T(8,128)(2,1)S(1)} %add_convert_fusion.2), channel_id=1, source_target_pairs={{0,2},{1,3},{2,0},{3,1},{4,6},{5,7},{6,4},{7,5},{8,10},{9,11},{10,... | collective-permute-start | bytes 786440 | tf_op jit(solution)/shard_map/ppermute | solution.py:927
  (228 other events, 2367.0 us)
Sparse Core Ops, SparseCore 0:
  15.1 69.6 all-gather.4
  87.5 58.7 all-gather.6
  148.5 59.0 all-gather.8
  209.7 59.0 all-gather.10
  304.6 73.2 reduce-scatter.4
  396.0 80.5 reduce-scatter.8
  493.8 34.0 reduce-scatter.6
  546.3 78.5 reduce-scatter.10
